TPU v7x, 256 devices: a whole 4x4x8 slice. The times are simulated.
256 devices in a mesh: row: 64 (over z_lo, x, y), col: 4 (over z_hi, core).
Axes of the slice: x: 4, y: 4, z: 8 (z_hi: 2, z_lo: 4; z = z_hi * 4 + z_lo), core: 2. Of those that a mesh axis runs over, the one named last changes fastest.
Arguments:
- features: float32 [65536, 256], P('row', 'col'), may hold values from -6 to 6
- weight: float32 [256, 256], replicated, may hold values from -0.375 to 0.375
- cotangent: float32 [65536, 256], P('row', 'col'), may hold values from -6 to 6
- degrees: int32 [65536], P('row'), may hold values from 1 to 16432, as said below
- tiles: int32 [8192, 128, 128], P('row'), may hold values from 0 to 1
- block_rows: int32 [8192], P('row'), may hold values from 0 to 7
- block_source: int32 [8192], P('row'), may hold values from 0 to 63
- block_slot: int32 [8192], P('row'), may hold values from 0 to 1
- block_count: int32 [64], P('row'), may hold values from 32 to 128, as said below
- pair_blocks: int32 [64, 64, 2], replicated, may hold values from 0 to 7, as said below
Outputs:
- output: float32 [65536, 256], P('row', 'col')
- h_grad: float32 [65536, 256], P('row', 'col')
- weight_grad: float32 [256, 256], P('col')
Inputs may be any that keep to these rules, and one draw needn't show every extreme that they name: Within one row index the 128 triples (block_rows, block_source, block_slot) are distinct. `block_count`: each row index has 32 to 128 live slots; some row index has exactly 128. `pair_blocks`: for every destination and source the 2 entries are distinct. `degrees`: each node's degree exceeds its number of nonzeros in its row of A.
All inputs are finite; a program needn't handle non-finite values.
Results may differ from a plain program's by a relative error of at most 0.00015.
Values sent between devices are 32-bit elements; how exact they have to be, the bound alone decides.
No kernel may reach another device: no remote copies, remote signals or barrier semaphores. Data moves between devices by JAX's collectives and lax.ppermute only.
A program may use at most 128 MiB of HBM per device.

v0:
```python
import jax
import jax.numpy as jnp
from jax import lax
from jax.sharding import PartitionSpec as P


def on_device(
    features,
    weight,
    cotangent,
    degrees,
    tiles,
    block_rows,
    block_source,
    block_slot,
    block_count,
    pair_blocks,
):
    highest = lax.Precision.HIGHEST
    rows_dev, panel_width = features.shape
    blocks, block_size = (tiles.shape[0], tiles.shape[1])
    groups = rows_dev // block_size
    n_row = lax.axis_size("row")
    own_row = lax.axis_index("row")
    own_col = lax.axis_index("col")
    degree_f = degrees.astype(jnp.float32)
    root_deg = lax.rsqrt(degree_f)
    inverse = 1.0 / degree_f
    live_mask = (jnp.arange(blocks, dtype=jnp.int32) < block_count[0]).astype(jnp.float32)
    adjacency = tiles.astype(jnp.float32) * live_mask[:, None, None]
    row_hot = (block_rows[:, None] == jnp.arange(groups, dtype=jnp.int32)[None, :]).astype(
        jnp.float32
    )
    own_pairs = pair_blocks[own_row]
    column = block_source * groups + own_pairs[block_source, block_slot]
    scaled = features * root_deg[:, None]
    whole = lax.all_gather(scaled, "row", axis=0, tiled=True)
    picked = jnp.take(whole.reshape(-1, block_size, panel_width), column, axis=0)
    contrib = jnp.einsum("bij,bjw->biw", adjacency, picked, precision=highest)
    summed = jnp.einsum("bg,biw->giw", row_hot, contrib, precision=highest).reshape(
        rows_dev, panel_width
    )
    aggregated = root_deg[:, None] * summed + features * inverse[:, None]
    full_width = lax.all_gather(aggregated, "col", axis=1, tiled=True)
    weight_cols = lax.dynamic_slice_in_dim(weight, own_col * panel_width, panel_width, 1)
    preact = jnp.dot(full_width, weight_cols, precision=highest)
    output = jax.nn.silu(preact)
    sigmoid_z = jax.nn.sigmoid(preact)
    delta_z = cotangent * sigmoid_z * (1.0 + preact * (1.0 - sigmoid_z))
    delta_full = lax.all_gather(delta_z, "col", axis=1, tiled=True)
    grad_part = lax.dot_general(aggregated, delta_full, (((0,), (0,)), ((), ())), precision=highest)
    weight_grad = lax.psum(grad_part, "row") * (n_row * rows_dev) ** (-0.5)
    weight_slab = lax.dynamic_slice_in_dim(weight, own_col * panel_width, panel_width, 0)
    back_in = lax.dot_general(delta_full, weight_slab, (((1,), (1,)), ((), ())), precision=highest)
    back_scaled = (back_in * root_deg[:, None]).reshape(groups, block_size, panel_width)
    picked_back = jnp.take(back_scaled, block_rows, axis=0)
    contrib_back = jnp.einsum("bji,bjw->biw", adjacency, picked_back, precision=highest)
    row_count = rows_dev * lax.axis_size("row")
    target_hot = (
        column[:, None] == jnp.arange(row_count // block_size, dtype=jnp.int32)[None, :]
    ).astype(jnp.float32)
    placed = jnp.einsum("bk,biw->kiw", target_hot, contrib_back, precision=highest)
    summed_back = lax.psum_scatter(
        placed.reshape(row_count, panel_width), "row", scatter_dimension=0, tiled=True
    )
    h_grad = root_deg[:, None] * summed_back + back_in * inverse[:, None]
    return (output, h_grad, weight_grad)


def solution(mesh):
    in_specs = (
        P("row", "col"),
        P(),
        P("row", "col"),
        P("row"),
        P("row", None, None),
        P("row"),
        P("row"),
        P("row"),
        P("row"),
        P(),
    )
    out_specs = (P("row", "col"), P("row", "col"), P("col", None))
    return jax.shard_map(
        on_device, mesh=mesh, in_specs=in_specs, out_specs=out_specs, check_vma=False
    )
```

profile of v0, /device:TPU:8, one launch (start us, length us, event | category | flops | bytes accessed | tf_op | source)
XLA Modules:
  0.0 1529.9 jit_solution(790774006529489017)
XLA Ops:
  7.2 0.0 all-gather.4.cloned.1.call-start
  7.2 0.7 convert_divide_fusion
  8.0 1.7 broadcast_multiply_fusion
  9.6 0.0 all-gather.4.cloned.1.call-update
  9.7 0.0 all-gather.6.cloned.1.call-start
  10.4 0.7 dynamic-slice_bitcast_fusion
  11.0 0.7 fusion.30
  11.7 1.5 gather_fusion
  13.2 0.7 compare_and_fusion.1
  13.9 378.9 %all-gather.4.cloned.1.call-done = f32[65536,64]{0,1:T(8,128)} async-done(((f32[1024,64]{0,1:T(8,128)}), f32[65536,64]{0,1:T(8,128)}) %all-gather.4.cloned.1.call-update) | async-done | bytes 16777232 | tf_op jit(solution)/shard_map/all_gather | solution.py:37
  392.8 11.8 copy_bitcast_fusion.1
  404.6 8.5 gather_fusion.1
  413.2 19.9 %fusion.1 = f32[128,128,64]{1,2,0:T(8,128)S(1)} fusion(s32[128,128,128]{2,1,0:T(8,128)} %param.14, f32[128,128,64]{1,2,0:T(8,128)} %gather_fusion.1, f32[128]{0:T(128)S(1)} %compare_convert_fusion, pred[128]{0:T(512)(128)(4,1)S(1)} %get-tuple-element.3), kind=kOutput, calls=%fused_computation.7 | convolution fusion | flops 1615855616 | bytes 16777856 | tf_op jit(solution)/shard_map/bij,bjw->biw/dot_general | solution.py:39
  433.0 3.8 fusion.4
  436.9 0.8 fusion.14
  437.7 0.2 all-gather.8.cloned.1.call-start
  437.9 30.8 %all-gather.6.cloned.1.call-done = f32[1024,256]{0,1:T(8,128)} async-done(((f32[1024,64]{0,1:T(8,128)}), f32[1024,256]{0,1:T(8,128)}) %all-gather.6.cloned.1.call-update) | async-done | bytes 1048592 | tf_op jit(solution)/shard_map/all_gather | solution.py:44
  468.7 2.9 add_multiply_fusion
  471.6 0.0 all-gather.8.cloned.1.call-update
  471.6 0.0 all-reduce.2.cloned.1.call-start
  471.7 28.0 %all-gather.8.cloned.1.call-done = f32[1024,256]{0,1:T(8,128)} async-done(((f32[1024,64]{0,1:T(8,128)}), f32[1024,256]{0,1:T(8,128)}) %all-gather.8.cloned.1.call-update) | async-done | bytes 1048592 | tf_op jit(solution)/shard_map/all_gather | solution.py:50
  499.7 3.0 fusion.35
  502.7 0.0 reduce-scatter.2.cloned.1.call-start
  502.8 2.0 fusion.21
  504.8 2.8 gather_fusion.2
  507.6 11.6 fusion
  519.2 8.7 fusion.2
  527.9 11.7 copy.29
  539.7 576.3 %all-reduce.2.cloned.1.call-done = f32[64,256]{1,0:T(8,128)} async-done(((f32[64,256]{1,0:T(8,128)}), f32[64,256]{1,0:T(8,128)}) %all-reduce.2.cloned.1.call-update) | async-done | bytes 65552 | tf_op jit(solution)/shard_map/psum | solution.py:52
  1116.0 1.5 broadcast_multiply_fusion.1
  1117.4 404.3 %reduce-scatter.2.cloned.1.call-done = f32[1024,64]{0,1:T(8,128)} async-done(((f32[65536,64]{0,1:T(8,128)}), f32[1024,64]{0,1:T(8,128)}) %reduce-scatter.2.cloned.1.call-update) | async-done | bytes 262160 | tf_op jit(solution)/shard_map/reduce_scatter | solution.py:63
  1521.7 1.7 multiply_add_fusion
  (20 shorter events, 0.1 us)
Async XLA Ops:
  7.2 461.5 %copy-start = (f32[256,256]{1,0:T(8,128)S(1)}, f32[256,256]{1,0:T(8,128)}, u32[]{:S(2)}) copy-start(f32[256,256]{1,0:T(8,128)} %param.11) | copy-start | bytes 786436
  7.2 385.6 %all-gather.4.cloned.1.call-start = ((), (), s32[]{:S(2)}) async-start(), calls=%async_computation.1 | async-start | bytes 17039360 | tf_op jit(solution)/shard_map/all_gather | solution.py:37
  9.7 459.0 %all-gather.6.cloned.1.call-start = ((), (), s32[]{:S(2)}) async-start(), calls=%async_computation.2 | async-start | bytes 1310720 | tf_op jit(solution)/shard_map/all_gather | solution.py:44
  413.2 19.9 %copy-start.4 = (s32[128]{0:T(128)S(1)}, s32[128]{0:T(128)}, u32[]{:S(2)}) copy-start(s32[128]{0:T(128)} %param.15) | copy-start | bytes 1540
  413.2 23.7 %copy-start.2 = (f32[1024,64]{0,1:T(8,128)S(1)}, f32[1024,64]{0,1:T(8,128)}, u32[]{:S(2)}) copy-start(f32[1024,64]{0,1:T(8,128)} %param.10) | copy-start | bytes 786436
  413.2 55.5 %copy-start.3 = (f32[1024,64]{0,1:T(8,128)S(1)}, f32[1024,64]{0,1:T(8,128)}, u32[]{:S(2)}) copy-start(f32[1024,64]{0,1:T(8,128)} %param.12) | copy-start | bytes 786436
  437.7 62.0 %all-gather.8.cloned.1.call-start = ((), (), s32[]{:S(2)}) async-start(), calls=%async_computation.3 | async-start | bytes 1310720 | tf_op jit(solution)/shard_map/all_gather | solution.py:50
  471.6 644.3 %all-reduce.2.cloned.1.call-start = ((), (), s32[]{:S(2)}) async-start(), calls=%async_computation.5 | async-start | bytes 131072 | tf_op jit(solution)/shard_map/psum | solution.py:52
  502.7 1019.0 %reduce-scatter.2.cloned.1.call-start = ((), (), s32[]{:S(2)}) async-start(), calls=%async_computation.4 | async-start | bytes 17039360 | tf_op jit(solution)/shard_map/reduce_scatter | solution.py:63
  539.7 983.7 %copy-start.1 = (f32[256,256]{1,0:T(8,128)S(1)}, f32[256,256]{1,0:T(8,128)}, u32[]{:S(2)}) copy-start(f32[256,256]{1,0:T(8,128)} %param.11) | copy-start | bytes 786436
Sparse Core Ops, SparseCore 0:
  10.4 382.3 all-gather.3
  437.8 30.8 all-gather.5
  471.8 27.8 all-gather.7
  502.9 613.0 all-reduce.1
  1118.5 403.1 reduce-scatter.1
where the time goes:
time: 1530 us
  waiting for transfers between devices  1420 us (93%)
  matrix products  52 us (3%)
  local copies, waits for them, and re-layouts  37.1 us (2%)
    psum x1, waiting for transfers between devices, on_device(): weight_grad = lax.psum(grad_part, 'row') * (n_row * rows_dev) ** (-0.5)  576 us
    reduce_scatter x1, waiting for transfers between devices, on_device(): lax.psum_scatter(placed.reshape(row_count, panel_width), 'row', scatter_d...  404 us
    all_gather x1, waiting for transfers between devices, on_device(): whole = lax.all_gather(scaled, 'row', axis=0, tiled=True)  379 us
    all_gather x1, waiting for transfers between devices, on_device(): full_width = lax.all_gather(aggregated, 'col', axis=1, tiled=True)  30.8 us
  transfers between devices with their start and end apart: 5, of which 5 were waited for; matrix products, arithmetic and copies ran while one was open for 3% of the time, Pallas kernels for 0%

commit v1 on v0

v1 whole, which is shorter than its diff:
```python
import functools

import jax
import jax.numpy as jnp
from jax import lax
from jax.experimental import pallas as pl
from jax.experimental.pallas import tpu as pltpu
from jax.sharding import PartitionSpec as P

SIDE = 4
RB = 8
GROUP = 8
CUTS = 4
PER = SIDE * SIDE * 2
F32 = jnp.float32
BF16 = jnp.bfloat16
NT = (((1,), (1,)), ((), ()))
NN = (((1,), (0,)), ((), ()))
TN = (((0,), (0,)), ((), ()))


def row_id(z, x, y):
    return z * SIDE * SIDE + x * SIDE + y


def shift(value, du, dv):
    pairs = []
    for row in range(SIDE**3):
        z, x, y = row // (SIDE * SIDE), row // SIDE % SIDE, row % SIDE
        for col in range(4):
            dx, dy = (dv, du) if col % 2 else (du, dv)
            pairs.append((row * 4 + col, row_id(z, (x + dx) % SIDE, (y + dy) % SIDE) * 4 + col))
    return lax.ppermute(value, ("row", "col"), pairs)


def swap_z(value, k):
    return lax.ppermute(value, "row", [(r, r ^ (k * SIDE * SIDE)) for r in range(SIDE**3)])


def swap_col(value, k):
    return lax.ppermute(value, "col", [(c, c ^ k) for c in range(4)])


def halves(value):
    high = value.astype(BF16)
    return high, (value - high.astype(F32)).astype(BF16)


def dot(a, b, dims):
    return lax.dot_general(a, b, dims, preferred_element_type=F32)


def dot3(a, b, dims):
    a_high, a_low = a
    b_high, b_low = b
    return dot(a_high, b_high, dims) + (dot(a_high, b_low, dims) + dot(a_low, b_high, dims))


def lanes(index, size):
    return pl.ds(pl.multiple_of(index * size, size), size)


def fetch(sources, targets, sems):
    copies = [
        pltpu.make_async_copy(source, target, sems.at[i])
        for i, (source, target) in enumerate(zip(sources, targets))
    ]
    for copy in copies:
        copy.start()
    return copies


def wait(copies):
    for copy in copies:
        copy.wait()


def convert_kernel(tiles, out, held, built, in_sems, out_sems):
    n = in_sems.shape[0]
    span = tiles.shape[0] // n
    cuts = [pl.ds(i * span, span) for i in range(n)]
    loads = fetch([tiles.at[c] for c in cuts], [held.at[c] for c in cuts], in_sems)
    copies = []
    for i, cut in enumerate(cuts):
        loads[i].wait()

        def one(t, carry):
            built[t] = held[t].astype(F32).astype(BF16)
            return carry

        lax.fori_loop(i * span, (i + 1) * span, one, 0, unroll=2)
        copy = pltpu.make_async_copy(built.at[cut], out.at[cut], out_sems.at[i])
        copy.start()
        copies.append(copy)
    wait(copies)


def pack_kernel(pick, *refs):
    n = SIDE
    ins, outs, (held, built, in_sems, out_sems) = refs[:n], refs[n : 2 * n], refs[2 * n :]
    wait(fetch(ins, [held.at[i] for i in range(n)], in_sems))
    copies = []
    for far in (2, 1, 3, 0):
        for near in range(SIDE):
            for k in range(SIDE):
                for p in range(2):
                    block = pick[((far * SIDE + near) * SIDE + k) * 2 + p]
                    built[far, (near * SIDE + k) * 2 + p] = held[near, k * RB + block]
        copy = pltpu.make_async_copy(built.at[far], outs[far], out_sems.at[far])
        copy.start()
        copies.append(copy)
    wait(copies)


def unpack_kernel(pick, *refs):
    n = SIDE
    ins, outs, (held, built, in_sems, out_sems) = refs[:n], refs[n : 2 * n], refs[2 * n :]
    loads = fetch(ins, [held.at[i] for i in range(n)], in_sems)
    built[...] = jnp.zeros_like(built)
    wait(loads)
    tail = (held[0, PER:] + held[1, PER:]) + (held[2, PER:] + held[3, PER:])
    copies = []
    for near in (2, 1, 3, 0):
        for far in range(SIDE):
            for k in range(SIDE):
                for p in range(2):
                    block = pick[((far * SIDE + near) * SIDE + k) * 2 + p]
                    built[near, k * RB + block] += held[far, (near * SIDE + k) * 2 + p]
        built[near, PER:] = tail
        copy = pltpu.make_async_copy(built.at[near], outs[near], out_sems.at[near])
        copy.start()
        copies.append(copy)
    wait(copies)


def join_kernel(*refs):
    n = SIDE
    ins, outs, (held, built, in_sems, out_sems) = refs[:n], refs[n : 2 * n], refs[2 * n :]
    wait(fetch(ins, [held.at[i] for i in range(n)], in_sems))
    copies = []
    for k in (2, 3, 1, 0):
        for target, source in ((pl.ds(0, RB), pl.ds(k * RB, RB)), (pl.ds(RB, 2), pl.ds(PER, 2))):
            built[k, target] = (held[0, source] + held[1, source]) + (
                held[2, source] + held[3, source]
            )
        copy = pltpu.make_async_copy(built.at[k], outs[k], out_sems.at[k])
        copy.start()
        copies.append(copy)
    wait(copies)


def run_groups(group, count, span, tile_loads):
    groups = (count + GROUP - 1) // GROUP
    step = span // GROUP
    for i, load in enumerate(tile_loads):
        load.wait()
        lax.fori_loop(jnp.minimum(i * step, groups), jnp.minimum((i + 1) * step, groups), group, 0)


def forward_kernel(
    rows, at, info, scaled, root, tiles, q0, q1, q2, q3,
    o0, o1, o2, o3, held, blocks, total, tile_sems, sems,
):
    span = tiles.shape[0] // CUTS
    cuts = [pl.ds(i * span, span) for i in range(CUTS)]
    loads = fetch((q0, q1, q2, q3), [blocks.at[pl.ds(i * PER, PER)] for i in range(SIDE)], sems)
    tile_loads = fetch([tiles.at[c] for c in cuts], [held.at[c] for c in cuts], tile_sems)
    total[...] = jnp.zeros_like(total)
    wait(loads)
    width = total.shape[1]

    def group(g, carry):
        first = g * GROUP
        sums = []
        for u in range(GROUP):
            pair = jnp.concatenate(halves(blocks[at[first + u]]), 0)
            both = dot(pair, held[first + u], NT)
            sums.append(both[:width] + both[width:])
        for u in range(GROUP):
            total[rows[first + u]] += sums[u]
        return carry

    run_groups(group, info[0], span, tile_loads)
    size = total.shape[2]
    own = info[1]
    for k, out in enumerate((o0, o1, o2, o3)):
        for h in range(2):
            b = (own ^ k) * 2 + h
            span = lanes(b, size)
            out[:, h * size : (h + 1) * size] = (total[b] + scaled[:, span]) * root[:, span]


def dense_kernel(
    scale, info, a0, a1, a2, a3, c0, c1, c2, c3, weight,
    b0, b1, b2, b3, y0, y1, y2, y3, work, work2,
):
    own = info[1]
    part = a0.shape[0]
    rows = [pl.ds(pl.multiple_of((own ^ k) * part, part), part) for k in range(4)]
    for k, (a, c) in enumerate(zip((a0, a1, a2, a3), (c0, c1, c2, c3))):
        work[rows[k], :] = a[...]
        work2[rows[k], :] = c[...]
    agg = halves(work[...])
    w = halves(weight[...])
    preact = dot3(w, agg, TN)
    gate = jax.nn.sigmoid(preact)
    delta = halves(work2[...] * gate * (1.0 + preact * (1.0 - gate)))
    work[...] = preact * gate
    for k, out in enumerate((y0, y1, y2, y3)):
        out[...] = work[rows[k], :]
    work2[...] = dot3(w, delta, NN)
    work[...] = dot3(agg, delta, NT) * scale
    for k, out in enumerate((b0, b1, b2, b3)):
        out[:part, :] = work2[rows[k], :]
        out[part:, :] = work[rows[k], :]


def backward_kernel(
    rows, at, info, root, inverse, i0, i1, i2, i3, tiles,
    direct, e0, e1, e2, e3, held, blocks, source, tail, tile_sems, sems, tail_sems,
):
    parts = (e0, e1, e2, e3)
    size = tiles.shape[2]
    width = i0.shape[0] // 2
    span = tiles.shape[0] // CUTS
    cuts = [pl.ds(i * span, span) for i in range(CUTS)]
    tile_loads = fetch([tiles.at[c] for c in cuts], [held.at[c] for c in cuts], tile_sems)
    for h in range(2):
        cols = slice(h * size, (h + 1) * size)
        tail[h] = (i0[width:, cols] + i1[width:, cols]) + (i2[width:, cols] + i3[width:, cols])
    tails = fetch([tail] * SIDE, [part.at[pl.ds(PER, 2)] for part in parts], tail_sems)
    blocks[...] = jnp.zeros_like(blocks)
    own = info[1]
    for k, piece in enumerate((i0, i1, i2, i3)):
        for h in range(2):
            b = (own ^ k) * 2 + h
            where = lanes(b, size)
            value = piece[:width, h * size : (h + 1) * size]
            direct[:, where] = value * inverse[:, where]
            source[b] = jnp.concatenate(halves(value * root[:, where]), 0)

    def group(g, carry):
        first = g * GROUP
        sums = []
        for u in range(GROUP):
            both = dot(source[rows[first + u]], held[first + u], NN)
            sums.append(both[:width] + both[width:])
        for u in range(GROUP):
            blocks[at[first + u]] += sums[u]
        return carry

    run_groups(group, info[0], span, tile_loads)
    sent = fetch(
        [blocks.at[pl.ds(i * PER, PER)] for i in range(SIDE)],
        [part.at[pl.ds(0, PER)] for part in parts],
        sems,
    )
    wait(sent)
    wait(tails)


VMEM = pl.BlockSpec(memory_space=pltpu.VMEM)
SMEM = pl.BlockSpec(memory_space=pltpu.SMEM)
HBM = pl.BlockSpec(memory_space=pltpu.HBM)
LIMIT = 40 * 1024 * 1024
DMA = pltpu.SemaphoreType.DMA


def struct(*shape):
    return jax.ShapeDtypeStruct(shape, F32)


def call(kernel, name, out_shape, in_specs, out_specs, scratch, nbytes=1 << 22):
    return pl.pallas_call(
        kernel,
        out_shape=out_shape,
        in_specs=in_specs,
        out_specs=out_specs,
        scratch_shapes=scratch,
        compiler_params=pltpu.CompilerParams(vmem_limit_bytes=LIMIT),
        cost_estimate=pl.CostEstimate(flops=0, bytes_accessed=nbytes, transcendentals=0),
        name=name,
    )


def on_device(
    features,
    weight,
    cotangent,
    degrees,
    tiles,
    block_rows,
    block_source,
    block_slot,
    block_count,
    pair_blocks,
):
    nodes, width = features.shape
    slots, size = tiles.shape[0], tiles.shape[1]
    quarter = nodes // 4
    n_row = lax.axis_size("row")
    own = lax.axis_index("row")
    own_col = lax.axis_index("col")
    turned = own_col % 2 == 1

    def place(row):
        x, y = row // SIDE % SIDE, row % SIDE
        return row // (SIDE * SIDE), jnp.where(turned, y, x), jnp.where(turned, x, y)

    def row_at(z, u, v):
        return jnp.where(turned, row_id(z, v % SIDE, u % SIDE), row_id(z, u % SIDE, v % SIDE))

    z, u, v = place(own)
    box = jnp.arange(SIDE, dtype=jnp.int32)

    degree_f = degrees.astype(F32)[None, :]
    root = lax.rsqrt(degree_f)
    inverse = 1.0 / degree_f
    features_t = features.T
    cotangent_t = cotangent.T

    far, near, deep = box[:, None, None], box[None, :, None], box[None, None, :]
    pick = pair_blocks[row_at(z, u, v + far), row_at(z ^ deep, u - near, v)].reshape(-1)

    live = jnp.arange(slots, dtype=jnp.int32) < block_count[0]
    from_z, from_u, from_v = place(block_source)
    at = (v - from_v) % SIDE * SIDE + (u - from_u) % SIDE
    at = (at * SIDE + (from_z ^ z)) * 2 + block_slot
    n_blocks = PER * SIDE
    rows_forward = jnp.where(live, block_rows, RB)
    at_back = jnp.where(live, at, n_blocks)
    info = jnp.stack([block_count[0], own_col.astype(jnp.int32)])

    scaled = features_t * root
    blocked = scaled.reshape(width, RB, size).transpose(1, 0, 2)
    stack = [blocked] + [swap_z(blocked, d) for d in range(1, SIDE)]
    adjacency = call(
        convert_kernel,
        "convert",
        jax.ShapeDtypeStruct(tiles.shape, BF16),
        [HBM],
        HBM,
        [pltpu.VMEM(tiles.shape, jnp.int32), pltpu.VMEM(tiles.shape, BF16), DMA((8,)), DMA((8,))],
        nbytes=12 << 20,
    )(tiles)
    stack, adjacency, pick = lax.optimization_barrier((stack, adjacency, pick))
    stack = jnp.concatenate(stack)
    arrived = [stack] + [shift(stack, d, 0) for d in (1, 2, 3)]
    shape = (PER, width, size)
    packed = call(
        pack_kernel,
        "pack",
        [struct(*shape)] * SIDE,
        [SMEM] + [HBM] * SIDE,
        [HBM] * SIDE,
        [pltpu.VMEM((SIDE,) + shape, F32)] * 2 + [DMA((SIDE,))] * 2,
        nbytes=8 << 20,
    )(pick, *arrived)

    def piece(value, d):
        return lax.dynamic_slice_in_dim(value, (own_col ^ d) * quarter, quarter, 1)

    def exchange(pieces):
        return [pieces[0]] + [swap_col(pieces[d], d) for d in (1, 2, 3)]

    cot = [piece(cotangent_t, d) for d in range(4)]
    cot, packed = lax.optimization_barrier((cot, packed))
    got = [packed[0]] + [shift(packed[d], 0, d) for d in (1, 2, 3)]
    cot = exchange(cot)
    got, cot = lax.optimization_barrier((got, cot))
    agg = call(
        forward_kernel,
        "forward",
        [struct(width, quarter)] * 4,
        [SMEM] * 3 + [VMEM] * 2 + [HBM] * (SIDE + 1),
        [VMEM] * 4,
        [
            pltpu.VMEM(tiles.shape, BF16),
            pltpu.VMEM((n_blocks, width, size), F32),
            pltpu.VMEM((RB + 1, width, size), F32),
            DMA((CUTS,)),
            DMA((SIDE,)),
        ],
        nbytes=16 << 20,
    )(rows_forward, at, info, scaled, root, adjacency, *got)
    agg = exchange(agg)
    dense = call(
        functools.partial(dense_kernel, (n_row * nodes) ** (-0.5)),
        "dense",
        [struct(2 * width, quarter)] * 4 + [struct(width, quarter)] * 4,
        [SMEM] + [VMEM] * 9,
        [VMEM] * 8,
        [pltpu.VMEM((4 * width, quarter), F32), pltpu.VMEM((4 * width, quarter), F32)],
    )(info, *agg, *cot, weight)
    back = exchange(dense[:4])

    shape = (PER + 2, width, size)
    direct, *sent = call(
        backward_kernel,
        "backward",
        [struct(width, nodes)] + [struct(*shape)] * SIDE,
        [SMEM] * 3 + [VMEM] * 6 + [HBM],
        [VMEM] + [HBM] * SIDE,
        [
            pltpu.VMEM(tiles.shape, BF16),
            pltpu.VMEM((n_blocks + 1, width, size), F32),
            pltpu.VMEM((RB, 2 * width, size), BF16),
            pltpu.VMEM((2, width, size), F32),
            DMA((CUTS,)),
            DMA((SIDE,)),
            DMA((SIDE,)),
        ],
        nbytes=16 << 20,
    )(block_rows, at_back, info, root, inverse, *back, adjacency)

    sent, out = lax.optimization_barrier((sent, dense[4:]))
    home = [sent[0]] + [shift(sent[d], 0, -d) for d in (1, 2, 3)]
    out = exchange(out)
    home, out = lax.optimization_barrier((home, out))
    summed = call(
        unpack_kernel,
        "unpack",
        [struct(*shape)] * SIDE,
        [SMEM] + [HBM] * SIDE,
        [HBM] * SIDE,
        [pltpu.VMEM((SIDE,) + shape, F32)] * 2 + [DMA((SIDE,))] * 2,
        nbytes=8 << 20,
    )(pick, *home)
    arrived = [summed[0]] + [shift(summed[d], -d, 0) for d in (1, 2, 3)]
    ends = call(
        join_kernel,
        "join",
        [struct(RB + 2, width, size)] * SIDE,
        [HBM] * SIDE,
        [HBM] * SIDE,
        [pltpu.VMEM((SIDE,) + shape, F32), pltpu.VMEM((SIDE, RB + 2, width, size), F32)]
        + [DMA((SIDE,))] * 2,
        nbytes=8 << 20,
    )(*arrived)
    total = ends[0] + swap_z(ends[1], 1) + swap_z(ends[2], 2) + swap_z(ends[3], 3)
    summed_back = total[:RB].transpose(1, 0, 2).reshape(width, nodes)
    h_grad = (root * summed_back + direct).T
    grad = total[RB:].transpose(1, 0, 2).reshape(width, 4 * width)

    output = jnp.zeros((width, nodes), F32)
    for d in range(4):
        output = lax.dynamic_update_slice_in_dim(output, out[d], (own_col ^ d) * quarter, 1)
    return (output.T, h_grad, grad)


def solution(mesh):
    in_specs = (
        P("row", "col"),
        P(),
        P("row", "col"),
        P("row"),
        P("row", None, None),
        P("row"),
        P("row"),
        P("row"),
        P("row"),
        P(),
    )
    out_specs = (P("row", "col"), P("row", "col"), P("col", None))
    return jax.shard_map(
        on_device, mesh=mesh, in_specs=in_specs, out_specs=out_specs, check_vma=False
    )
```

time: 1530 us -> 228 us (0.15)
  waiting for transfers between devices: 1420 us -> 131 us
  starting transfers between devices: 0.39 us -> 59.4 us
  matrix products: 52 us -> 0 us
  local copies, waits for them, and re-layouts: 37.1 us -> 9.86 us
  Pallas kernels: 0 us -> 18.9 us
    psum x1 -> x0, waiting for transfers between devices: 576 us -> none  [on_device(): weight_grad = lax.psum(grad_part, 'row') * (n_row * rows_dev) ** (-0.5)]
    all_gather x3 -> x0, waiting for transfers between devices: 438 us -> none  [the longest x1 379 us: on_device(): whole = lax.all_gather(scaled, 'row', axis=0, tiled=True)]
    reduce_scatter x1 -> x0, waiting for transfers between devices: 404 us -> none  [on_device(): lax.psum_scatter(placed.reshape(row_count, panel_width), 'row', scatter_d...]
    ppermute x0 -> x30, waiting for transfers between devices: none -> 131 us  [the longest x12 71.6 us: shift(): return lax.ppermute(value, ('row', 'col'), pairs)]
    ppermute x0 -> x30, starting transfers between devices: none -> 59.4 us  [the longest x12 25.2 us: swap_col(): return lax.ppermute(value, 'col', [(c, c ^ k) for c in range(4)])]
    dot_general x7 -> x0, matrix products: 52 us -> none  [the longest x1 19.9 us: on_device(): contrib = jnp.einsum('bij,bjw->biw', adjacency, picked, precision=highest)]
    pallas_call x0 -> x7, Pallas kernels: none -> 18.9 us  [the longest x1 4.61 us: on_device(): call(forward_kernel, 'forward', [struct(width, quarter)] * 4, [SMEM] * 3...]
  transfers between devices with their start and end apart: 5 -> 30, of which waited for: 5 -> 20; matrix products, arithmetic and copies ran while one was open for 3% -> 1% of each run, Pallas kernels for 0% -> 1%
where the time goes in v1:
time: 228 us; the launch traced here: 224 us
  waiting for transfers between devices  131 us (57%)
  starting transfers between devices  59.4 us (26%)
  Pallas kernels  18.9 us (8%)
  local copies, waits for them, and re-layouts  9.86 us (4%)
  other arithmetic  2.82 us (1%)
    ppermute x12, waiting for transfers between devices, shift(): return lax.ppermute(value, ('row', 'col'), pairs)  71.6 us
    ppermute x6, waiting for transfers between devices, swap_z(): lax.ppermute(value, 'row', [(r, r ^ k * SIDE * SIDE) for r in range(SIDE...  31.3 us
    ppermute x12, waiting for transfers between devices, swap_col(): return lax.ppermute(value, 'col', [(c, c ^ k) for c in range(4)])  28.5 us
    ppermute x12, starting transfers between devices, swap_col(): return lax.ppermute(value, 'col', [(c, c ^ k) for c in range(4)])  25.2 us
    ppermute x12, starting transfers between devices, shift(): return lax.ppermute(value, ('row', 'col'), pairs)  18.7 us
    ppermute x6, starting transfers between devices, swap_z(): lax.ppermute(value, 'row', [(r, r ^ k * SIDE * SIDE) for r in range(SIDE...  15.5 us
    unnamed x22, local copies, waits for them, and re-layouts  6.1 us
    pallas_call x1, Pallas kernels, on_device(): call(forward_kernel, 'forward', [struct(width, quarter)] * 4, [SMEM] * 3...  4.61 us
  transfers between devices with their start and end apart: 30, of which 20 were waited for; matrix products, arithmetic and copies ran while one was open for 1% of the time, Pallas kernels for 1%

profile of v1, /device:TPU:8, one launch (start us, length us, event | category | flops | bytes accessed | tf_op | source)
XLA Modules:
  0.0 224.0 jit_solution(11519885592094866639)
XLA Ops:
  4.4 3.3 %collective-permute-start.1 = (f32[8,64,128]{2,1,0:T(8,128)S(1)}, f32[8,64,128]{2,1,0:T(8,128)S(1)}, u32[]{:S(2)}, u32[]{:S(2)}) collective-permute-start(f32[8,64,128]{2,1,0:T(8,128)S(1)} %bitcast.49), channel_id=1, source_target_pairs={{0,128},{4,132},{8,136},{12,140},{16,144},{20,148},{24,152},{28,15... | collective-permute-start | bytes 786440 | tf_op jit(solution)/shard_map/ppermute | solution.py:37
  9.7 3.4 %copy-done.2 = s32[128,128,128]{2,1,0:T(8,128)S(1)} copy-done((s32[128,128,128]{2,1,0:T(8,128)S(1)}, s32[128,128,128]{2,1,0:T(8,128)}, u32[]{:S(2)}) %copy-start.2) | copy-done | bytes 8388632
  16.8 9.3 %collective-permute-done.1 = f32[8,64,128]{2,1,0:T(8,128)S(1)} collective-permute-done((f32[8,64,128]{2,1,0:T(8,128)S(1)}, f32[8,64,128]{2,1,0:T(8,128)S(1)}, u32[]{:S(2)}, u32[]{:S(2)}) %collective-permute-start.1) | collective-permute-done | bytes 262176 | tf_op jit(solution)/shard_map/ppermute | solution.py:37
  28.7 2.7 %collective-permute-start.4 = (f32[32,64,128]{2,1,0:T(8,128)S(1)}, f32[32,64,128]{2,1,0:T(8,128)S(1)}, u32[]{:S(2)}, u32[]{:S(2)}) collective-permute-start(f32[32,64,128]{2,1,0:T(8,128)S(1)} %constant_dynamic-update-slice_fusion.refs_0_), channel_id=1, source_target_pairs={{0,32},{1,9},{2,34},{3,11},{4,36},{5,13},{6,38},{7,15},{8,40},{9,1... | collective-permute-start | bytes 3145736 | tf_op jit(solution)/shard_map/ppermute | solution.py:33
  33.9 9.3 %collective-permute-done.3.refs_1_ = f32[32,64,128]{2,1,0:T(8,128)S(1)} collective-permute-done((f32[32,64,128]{2,1,0:T(8,128)S(1)}, f32[32,64,128]{2,1,0:T(8,128)S(1)}, u32[]{:S(2)}, u32[]{:S(2)}) %collective-permute-start.3) | collective-permute-done | bytes 1048608 | tf_op jit(solution)/shard_map/ppermute | solution.py:33
  43.2 12.2 %collective-permute-done.4.refs_2_ = f32[32,64,128]{2,1,0:T(8,128)S(1)} collective-permute-done((f32[32,64,128]{2,1,0:T(8,128)S(1)}, f32[32,64,128]{2,1,0:T(8,128)S(1)}, u32[]{:S(2)}, u32[]{:S(2)}) %collective-permute-start.4) | collective-permute-done | bytes 1048608 | tf_op jit(solution)/shard_map/ppermute | solution.py:33
  55.5 2.7 %pack.1 = (f32[32,64,128]{2,1,0:T(8,128)S(1)}, f32[32,64,128]{2,1,0:T(8,128)S(1)}, f32[32,64,128]{2,1,0:T(8,128)S(1)}, f32[32,64,128]{2,1,0:T(8,128)S(1)}) custom-call(s32[128]{0:T(128)S(1)} %reshape.122.pick, f32[32,64,128]{2,1,0:T(8,128)S(1)} %constant_dynamic-update-slice_fusion.refs_0_, f32[32,64,128]{2,1,0:T(8,128)S(1)} %collective-permute-done.3.refs_1_, ...), custom_call_target="tpu_custom_call" | custom-call | bytes 8388608 | tf_op jit(solution)/shard_map/pack/pallas_call | solution.py:350
  60.7 2.4 %collective-permute-start.8 = (f32[32,64,128]{2,1,0:T(8,128)S(1)}, f32[32,64,128]{2,1,0:T(8,128)S(1)}, u32[]{:S(2)}, u32[]{:S(2)}) collective-permute-start(f32[32,64,128]{2,1,0:T(8,128)S(1)} %get-tuple-element.83), channel_id=1, source_target_pairs={{0,12},{1,49},{2,14},{3,51},{4,0},{5,53},{6,2},{7,55},{8,4},{9,57}... | collective-permute-start | bytes 3145736 | tf_op jit(solution)/shard_map/ppermute | solution.py:33
  63.8 6.1 %collective-permute-start.10 = (f32[64,256]{1,0:T(8,128)S(1)}, f32[64,256]{1,0:T(8,128)S(1)}, u32[]{:S(2)}, u32[]{:S(2)}) collective-permute-start(f32[64,256]{1,0:T(8,128)S(1)} %get-tuple-element.86), channel_id=1, source_target_pairs={{0,2},{1,3},{2,0},{3,1},{4,6},{5,7},{6,4},{7,5},{8,10},{9,11},{10,... | collective-permute-start | bytes 196616 | tf_op jit(solution)/shard_map/ppermute | solution.py:41
  69.9 2.5 %collective-permute-done.10.c2 = f32[64,256]{1,0:T(8,128)S(1)} collective-permute-done((f32[64,256]{1,0:T(8,128)S(1)}, f32[64,256]{1,0:T(8,128)S(1)}, u32[]{:S(2)}, u32[]{:S(2)}) %collective-permute-start.10) | collective-permute-done | bytes 65568 | tf_op jit(solution)/shard_map/ppermute | solution.py:41
  72.5 5.5 %collective-permute-done.11.c3 = f32[64,256]{1,0:T(8,128)S(1)} collective-permute-done((f32[64,256]{1,0:T(8,128)S(1)}, f32[64,256]{1,0:T(8,128)S(1)}, u32[]{:S(2)}, u32[]{:S(2)}) %collective-permute-start.11) | collective-permute-done | bytes 65568 | tf_op jit(solution)/shard_map/ppermute | solution.py:41
  78.1 8.7 %collective-permute-done.8.q3 = f32[32,64,128]{2,1,0:T(8,128)S(1)} collective-permute-done((f32[32,64,128]{2,1,0:T(8,128)S(1)}, f32[32,64,128]{2,1,0:T(8,128)S(1)}, u32[]{:S(2)}, u32[]{:S(2)}) %collective-permute-start.8) | collective-permute-done | bytes 1048608 | tf_op jit(solution)/shard_map/ppermute | solution.py:33
  86.8 4.6 %forward.1 = (f32[64,256]{1,0:T(8,128)S(1)}, f32[64,256]{1,0:T(8,128)S(1)}, f32[64,256]{1,0:T(8,128)S(1)}, f32[64,256]{1,0:T(8,128)S(1)}) custom-call(s32[128]{0:T(128)S(1)} %compare_select_fusion.12.rows, s32[128]{0:T(128)S(1)} %get-tuple-element.138.at, s32[2]{0:T(128)S(1)} %pad_add_fusion.info, f32[64,1024]{1,0:T(8,128)S(1)} %get-tuple-element.140.scaled, ...), custom_call_target="tpu_custom_call" | custom-call | bytes 16777216 | tf_op jit(solution)/shard_map/forward/pallas_call | solution.py:371
  91.5 6.1 %collective-permute-start.13 = (f32[64,256]{1,0:T(8,128)S(1)}, f32[64,256]{1,0:T(8,128)S(1)}, u32[]{:S(2)}, u32[]{:S(2)}) collective-permute-start(f32[64,256]{1,0:T(8,128)S(1)} %get-tuple-element.94), channel_id=1, source_target_pairs={{0,2},{1,3},{2,0},{3,1},{4,6},{5,7},{6,4},{7,5},{8,10},{9,11},{10,... | collective-permute-start | bytes 196616 | tf_op jit(solution)/shard_map/ppermute | solution.py:41
  97.6 3.6 %collective-permute-done.13.a2 = f32[64,256]{1,0:T(8,128)S(1)} collective-permute-done((f32[64,256]{1,0:T(8,128)S(1)}, f32[64,256]{1,0:T(8,128)S(1)}, u32[]{:S(2)}, u32[]{:S(2)}) %collective-permute-start.13) | collective-permute-done | bytes 65568 | tf_op jit(solution)/shard_map/ppermute | solution.py:41
  101.2 4.3 %collective-permute-done.14.a3 = f32[64,256]{1,0:T(8,128)S(1)} collective-permute-done((f32[64,256]{1,0:T(8,128)S(1)}, f32[64,256]{1,0:T(8,128)S(1)}, u32[]{:S(2)}, u32[]{:S(2)}) %collective-permute-start.14) | collective-permute-done | bytes 65568 | tf_op jit(solution)/shard_map/ppermute | solution.py:41
  110.0 3.9 %collective-permute-start.17 = (f32[128,256]{1,0:T(8,128)S(1)}, f32[128,256]{1,0:T(8,128)S(1)}, u32[]{:S(2)}, u32[]{:S(2)}) collective-permute-start(f32[128,256]{1,0:T(8,128)S(1)} %get-tuple-element.103), channel_id=1, source_target_pairs={{0,3},{1,2},{2,1},{3,0},{4,7},{5,6},{6,5},{7,4},{8,11},{9,10},{10,... | collective-permute-start | bytes 393224 | tf_op jit(solution)/shard_map/ppermute | solution.py:41
  113.9 5.0 %collective-permute-done.16.i2 = f32[128,256]{1,0:T(8,128)S(1)} collective-permute-done((f32[128,256]{1,0:T(8,128)S(1)}, f32[128,256]{1,0:T(8,128)S(1)}, u32[]{:S(2)}, u32[]{:S(2)}) %collective-permute-start.16) | collective-permute-done | bytes 131104 | tf_op jit(solution)/shard_map/ppermute | solution.py:41
  118.9 3.1 %collective-permute-done.17.i3 = f32[128,256]{1,0:T(8,128)S(1)} collective-permute-done((f32[128,256]{1,0:T(8,128)S(1)}, f32[128,256]{1,0:T(8,128)S(1)}, u32[]{:S(2)}, u32[]{:S(2)}) %collective-permute-start.17) | collective-permute-done | bytes 131104 | tf_op jit(solution)/shard_map/ppermute | solution.py:41
  122.0 4.4 %backward.1 = (f32[64,1024]{1,0:T(8,128)S(1)}, f32[34,64,128]{2,1,0:T(8,128)S(1)}, f32[34,64,128]{2,1,0:T(8,128)S(1)}, f32[34,64,128]{2,1,0:T(8,128)S(1)}, f32[34,64,128]{2,1,0:T(8,128)S(1)}) custom-call(s32[128]{0:T(128)S(1)} %copy-done.4, s32[128]{0:T(128)S(1)} %get-tuple-element.137.at, s32[2]{0:T(128)S(1)} %pad_add_fusion.info, f32[1,1024]{1,0:T(1,128)S(1)} %bitcast.46, ...), custom_call_target="tpu_custom_call" | custom-call | bytes 16777216 | tf_op jit(solution)/shard_map/backward/pallas_call | solution.py:398
  126.5 3.7 %collective-permute-start.19 = (f32[34,64,128]{2,1,0:T(8,128)S(1)}, f32[34,64,128]{2,1,0:T(8,128)S(1)}, u32[]{:S(2)}, u32[]{:S(2)}) collective-permute-start(f32[34,64,128]{2,1,0:T(8,128)S(1)} %get-tuple-element.114), channel_id=1, source_target_pairs={{0,8},{1,33},{2,10},{3,35},{4,12},{5,37},{6,14},{7,39},{8,0},{9,41... | collective-permute-start | bytes 3342344 | tf_op jit(solution)/shard_map/ppermute | solution.py:33
  132.2 3.9 %collective-permute-start.23 = (f32[64,256]{1,0:T(8,128)S(1)}, f32[64,256]{1,0:T(8,128)S(1)}, u32[]{:S(2)}, u32[]{:S(2)}) collective-permute-start(f32[64,256]{1,0:T(8,128)S(1)} %get-tuple-element.119), channel_id=1, source_target_pairs={{0,3},{1,2},{2,1},{3,0},{4,7},{5,6},{6,5},{7,4},{8,11},{9,10},{10,... | collective-permute-start | bytes 196616 | tf_op jit(solution)/shard_map/ppermute | solution.py:41
  136.1 2.9 %collective-permute-done.22 = f32[64,256]{1,0:T(8,128)S(1)} collective-permute-done((f32[64,256]{1,0:T(8,128)S(1)}, f32[64,256]{1,0:T(8,128)S(1)}, u32[]{:S(2)}, u32[]{:S(2)}) %collective-permute-start.22) | collective-permute-done | bytes 65568 | tf_op jit(solution)/shard_map/ppermute | solution.py:41
  142.3 13.4 %collective-permute-done.19.refs_2_ = f32[34,64,128]{2,1,0:T(8,128)S(1)} collective-permute-done((f32[34,64,128]{2,1,0:T(8,128)S(1)}, f32[34,64,128]{2,1,0:T(8,128)S(1)}, u32[]{:S(2)}, u32[]{:S(2)}) %collective-permute-start.19) | collective-permute-done | bytes 1114144 | tf_op jit(solution)/shard_map/ppermute | solution.py:33
  156.4 2.8 %unpack.1 = (f32[34,64,128]{2,1,0:T(8,128)S(1)}, f32[34,64,128]{2,1,0:T(8,128)S(1)}, f32[34,64,128]{2,1,0:T(8,128)S(1)}, f32[34,64,128]{2,1,0:T(8,128)S(1)}) custom-call(s32[128]{0:T(128)S(1)} %reshape.122.pick, f32[34,64,128]{2,1,0:T(8,128)S(1)} %get-tuple-element.124.refs_0_, f32[34,64,128]{2,1,0:T(8,128)S(1)} %collective-permute-done.18.refs_1_, ...), custom_call_target="tpu_custom_call" | custom-call | bytes 8388608 | tf_op jit(solution)/shard_map/unpack/pallas_call | solution.py:420
  159.3 4.1 %collective-permute-start.25 = (f32[34,64,128]{2,1,0:T(8,128)S(1)}, f32[34,64,128]{2,1,0:T(8,128)S(1)}, u32[]{:S(2)}, u32[]{:S(2)}) collective-permute-start(f32[34,64,128]{2,1,0:T(8,128)S(1)} %get-tuple-element.130), channel_id=1, source_target_pairs={{0,32},{1,9},{2,34},{3,11},{4,36},{5,13},{6,38},{7,15},{8,40},{9,1... | collective-permute-start | bytes 3342344 | tf_op jit(solution)/shard_map/ppermute | solution.py:33
  163.5 11.4 %collective-permute-done.24.refs_1_ = f32[34,64,128]{2,1,0:T(8,128)S(1)} collective-permute-done((f32[34,64,128]{2,1,0:T(8,128)S(1)}, f32[34,64,128]{2,1,0:T(8,128)S(1)}, u32[]{:S(2)}, u32[]{:S(2)}) %collective-permute-start.24) | collective-permute-done | bytes 1114144 | tf_op jit(solution)/shard_map/ppermute | solution.py:33
  177.0 11.8 %collective-permute-done.26.refs_3_ = f32[34,64,128]{2,1,0:T(8,128)S(1)} collective-permute-done((f32[34,64,128]{2,1,0:T(8,128)S(1)}, f32[34,64,128]{2,1,0:T(8,128)S(1)}, u32[]{:S(2)}, u32[]{:S(2)}) %collective-permute-start.26) | collective-permute-done | bytes 1114144 | tf_op jit(solution)/shard_map/ppermute | solution.py:33
  190.2 7.8 %collective-permute-start.27 = (f32[10,64,128]{2,1,0:T(8,128)S(1)}, f32[10,64,128]{2,1,0:T(8,128)S(1)}, u32[]{:S(2)}, u32[]{:S(2)}) collective-permute-start(f32[10,64,128]{2,1,0:T(8,128)S(1)} %get-tuple-element.133), channel_id=1, source_target_pairs={{0,64},{4,68},{8,72},{12,76},{16,80},{20,84},{24,88},{28,92},{32,9... | collective-permute-start | bytes 983048 | tf_op jit(solution)/shard_map/ppermute | solution.py:37
  198.0 2.5 %collective-permute-start.29 = (f32[10,64,128]{2,1,0:T(8,128)S(1)}, f32[10,64,128]{2,1,0:T(8,128)S(1)}, u32[]{:S(2)}, u32[]{:S(2)}) collective-permute-start(f32[10,64,128]{2,1,0:T(8,128)S(1)} %get-tuple-element.135), channel_id=1, source_target_pairs={{0,192},{4,196},{8,200},{12,204},{16,208},{20,212},{24,216},{28,22... | collective-permute-start | bytes 983048 | tf_op jit(solution)/shard_map/ppermute | solution.py:37
  200.5 8.1 %collective-permute-done.27 = f32[10,64,128]{2,1,0:T(8,128)S(1)} collective-permute-done((f32[10,64,128]{2,1,0:T(8,128)S(1)}, f32[10,64,128]{2,1,0:T(8,128)S(1)}, u32[]{:S(2)}, u32[]{:S(2)}) %collective-permute-start.27) | collective-permute-done | bytes 327712 | tf_op jit(solution)/shard_map/ppermute | solution.py:37
  208.6 14.0 %collective-permute-done.28 = f32[10,64,128]{2,1,0:T(8,128)S(1)} collective-permute-done((f32[10,64,128]{2,1,0:T(8,128)S(1)}, f32[10,64,128]{2,1,0:T(8,128)S(1)}, u32[]{:S(2)}, u32[]{:S(2)}) %collective-permute-start.28) | collective-permute-done | bytes 327712 | tf_op jit(solution)/shard_map/ppermute | solution.py:37
  (81 shorter events, 32.9 us)
Async XLA Ops:
  2.4 14.4 %collective-permute-start = (f32[8,64,128]{2,1,0:T(8,128)S(1)}, f32[8,64,128]{2,1,0:T(8,128)S(1)}, u32[]{:S(2)}, u32[]{:S(2)}) collective-permute-start(f32[8,64,128]{2,1,0:T(8,128)S(1)} %bitcast.48), channel_id=1, source_target_pairs={{0,64},{4,68},{8,72},{12,76},{16,80},{20,84},{24,88},{28,92},{32,9... | collective-permute-start | bytes 786440 | tf_op jit(solution)/shard_map/ppermute | solution.py:37
  4.4 21.7 %collective-permute-start.1 = (f32[8,64,128]{2,1,0:T(8,128)S(1)}, f32[8,64,128]{2,1,0:T(8,128)S(1)}, u32[]{:S(2)}, u32[]{:S(2)}) collective-permute-start(f32[8,64,128]{2,1,0:T(8,128)S(1)} %bitcast.49), channel_id=1, source_target_pairs={{0,128},{4,132},{8,136},{12,140},{16,144},{20,148},{24,152},{28,15... | collective-permute-start | bytes 786440 | tf_op jit(solution)/shard_map/ppermute | solution.py:37
  7.7 18.4 %collective-permute-start.2 = (f32[8,64,128]{2,1,0:T(8,128)S(1)}, f32[8,64,128]{2,1,0:T(8,128)}, u32[]{:S(2)}, u32[]{:S(2)}) collective-permute-start(f32[8,64,128]{2,1,0:T(8,128)S(1)} %bitcast.50), channel_id=1, source_target_pairs={{0,192},{4,196},{8,200},{12,204},{16,208},{20,212},{24,216},{28,22... | collective-permute-start | bytes 786440 | tf_op jit(solution)/shard_map/ppermute | solution.py:37
  27.1 16.1 %collective-permute-start.3 = (f32[32,64,128]{2,1,0:T(8,128)S(1)}, f32[32,64,128]{2,1,0:T(8,128)S(1)}, u32[]{:S(2)}, u32[]{:S(2)}) collective-permute-start(f32[32,64,128]{2,1,0:T(8,128)S(1)} %constant_dynamic-update-slice_fusion.refs_0_), channel_id=1, source_target_pairs={{0,16},{1,5},{2,18},{3,7},{4,20},{5,9},{6,22},{7,11},{8,24},{9,13}... | collective-permute-start | bytes 3145736 | tf_op jit(solution)/shard_map/ppermute | solution.py:33
  28.7 26.7 %collective-permute-start.4 = (f32[32,64,128]{2,1,0:T(8,128)S(1)}, f32[32,64,128]{2,1,0:T(8,128)S(1)}, u32[]{:S(2)}, u32[]{:S(2)}) collective-permute-start(f32[32,64,128]{2,1,0:T(8,128)S(1)} %constant_dynamic-update-slice_fusion.refs_0_), channel_id=1, source_target_pairs={{0,32},{1,9},{2,34},{3,11},{4,36},{5,13},{6,38},{7,15},{8,40},{9,1... | collective-permute-start | bytes 3145736 | tf_op jit(solution)/shard_map/ppermute | solution.py:33
  31.4 24.0 %collective-permute-start.5 = (f32[32,64,128]{2,1,0:T(8,128)S(1)}, f32[32,64,128]{2,1,0:T(8,128)}, u32[]{:S(2)}, u32[]{:S(2)}) collective-permute-start(f32[32,64,128]{2,1,0:T(8,128)S(1)} %constant_dynamic-update-slice_fusion.refs_0_), channel_id=1, source_target_pairs={{0,48},{1,13},{2,50},{3,15},{4,52},{5,1},{6,54},{7,3},{8,56},{9,5}... | collective-permute-start | bytes 3145736 | tf_op jit(solution)/shard_map/ppermute | solution.py:33
  33.8 36.1 %copy-start.4 = (s32[128]{0:T(128)S(1)}, s32[128]{0:T(128)}, u32[]{:S(2)}) copy-start(s32[128]{0:T(128)} %rows.1) | copy-start | bytes 1540
  33.8 52.9 %copy-start.1 = (bf16[128,128,128]{2,1,0:T(8,128)(2,1)S(1)}, bf16[128,128,128]{2,1,0:T(8,128)(2,1)}, u32[]{:S(2)}) copy-start(bf16[128,128,128]{2,1,0:T(8,128)(2,1)} %copy-done) | copy-start | bytes 12582916
  58.1 19.9 %collective-permute-start.6 = (f32[32,64,128]{2,1,0:T(8,128)S(1)}, f32[32,64,128]{2,1,0:T(8,128)S(1)}, u32[]{:S(2)}, u32[]{:S(2)}) collective-permute-start(f32[32,64,128]{2,1,0:T(8,128)S(1)} %get-tuple-element.81), channel_id=1, source_target_pairs={{0,4},{1,17},{2,6},{3,19},{4,8},{5,21},{6,10},{7,23},{8,12},{9,25}... | collective-permute-start | bytes 3145736 | tf_op jit(solution)/shard_map/ppermute | solution.py:33
  59.8 18.3 %collective-permute-start.7 = (f32[32,64,128]{2,1,0:T(8,128)S(1)}, f32[32,64,128]{2,1,0:T(8,128)S(1)}, u32[]{:S(2)}, u32[]{:S(2)}) collective-permute-start(f32[32,64,128]{2,1,0:T(8,128)S(1)} %get-tuple-element.82), channel_id=1, source_target_pairs={{0,8},{1,33},{2,10},{3,35},{4,12},{5,37},{6,14},{7,39},{8,0},{9,41... | collective-permute-start | bytes 3145736 | tf_op jit(solution)/shard_map/ppermute | solution.py:33
  60.7 26.0 %collective-permute-start.8 = (f32[32,64,128]{2,1,0:T(8,128)S(1)}, f32[32,64,128]{2,1,0:T(8,128)S(1)}, u32[]{:S(2)}, u32[]{:S(2)}) collective-permute-start(f32[32,64,128]{2,1,0:T(8,128)S(1)} %get-tuple-element.83), channel_id=1, source_target_pairs={{0,12},{1,49},{2,14},{3,51},{4,0},{5,53},{6,2},{7,55},{8,4},{9,57}... | collective-permute-start | bytes 3145736 | tf_op jit(solution)/shard_map/ppermute | solution.py:33
  63.8 8.6 %collective-permute-start.10 = (f32[64,256]{1,0:T(8,128)S(1)}, f32[64,256]{1,0:T(8,128)S(1)}, u32[]{:S(2)}, u32[]{:S(2)}) collective-permute-start(f32[64,256]{1,0:T(8,128)S(1)} %get-tuple-element.86), channel_id=1, source_target_pairs={{0,2},{1,3},{2,0},{3,1},{4,6},{5,7},{6,4},{7,5},{8,10},{9,11},{10,... | collective-permute-start | bytes 196616 | tf_op jit(solution)/shard_map/ppermute | solution.py:41
  69.9 8.2 %collective-permute-start.11 = (f32[64,256]{1,0:T(8,128)S(1)}, f32[64,256]{1,0:T(8,128)S(1)}, u32[]{:S(2)}, u32[]{:S(2)}) collective-permute-start(f32[64,256]{1,0:T(8,128)S(1)} %get-tuple-element.87), channel_id=1, source_target_pairs={{0,3},{1,2},{2,1},{3,0},{4,7},{5,6},{6,5},{7,4},{8,11},{9,10},{10,... | collective-permute-start | bytes 196616 | tf_op jit(solution)/shard_map/ppermute | solution.py:41
  72.5 5.6 %collective-permute-start.9 = (f32[64,256]{1,0:T(8,128)S(1)}, f32[64,256]{1,0:T(8,128)S(1)}, u32[]{:S(2)}, u32[]{:S(2)}) collective-permute-start(f32[64,256]{1,0:T(8,128)S(1)} %get-tuple-element.85), channel_id=1, source_target_pairs={{0,1},{1,0},{2,3},{3,2},{4,5},{5,4},{6,7},{7,6},{8,9},{9,8},{10,11... | collective-permute-start | bytes 196616 | tf_op jit(solution)/shard_map/ppermute | solution.py:41
  91.4 6.2 %collective-permute-start.12 = (f32[64,256]{1,0:T(8,128)S(1)}, f32[64,256]{1,0:T(8,128)S(1)}, u32[]{:S(2)}, u32[]{:S(2)}) collective-permute-start(f32[64,256]{1,0:T(8,128)S(1)} %get-tuple-element.93), channel_id=1, source_target_pairs={{0,1},{1,0},{2,3},{3,2},{4,5},{5,4},{6,7},{7,6},{8,9},{9,8},{10,11... | collective-permute-start | bytes 196616 | tf_op jit(solution)/shard_map/ppermute | solution.py:41
  91.5 9.7 %collective-permute-start.13 = (f32[64,256]{1,0:T(8,128)S(1)}, f32[64,256]{1,0:T(8,128)S(1)}, u32[]{:S(2)}, u32[]{:S(2)}) collective-permute-start(f32[64,256]{1,0:T(8,128)S(1)} %get-tuple-element.94), channel_id=1, source_target_pairs={{0,2},{1,3},{2,0},{3,1},{4,6},{5,7},{6,4},{7,5},{8,10},{9,11},{10,... | collective-permute-start | bytes 196616 | tf_op jit(solution)/shard_map/ppermute | solution.py:41
  97.5 8.0 %collective-permute-start.14 = (f32[64,256]{1,0:T(8,128)S(1)}, f32[64,256]{1,0:T(8,128)S(1)}, u32[]{:S(2)}, u32[]{:S(2)}) collective-permute-start(f32[64,256]{1,0:T(8,128)S(1)} %get-tuple-element.95), channel_id=1, source_target_pairs={{0,3},{1,2},{2,1},{3,0},{4,7},{5,6},{6,5},{7,4},{8,11},{9,10},{10,... | collective-permute-start | bytes 196616 | tf_op jit(solution)/shard_map/ppermute | solution.py:41
  106.8 7.1 %collective-permute-start.15 = (f32[128,256]{1,0:T(8,128)S(1)}, f32[128,256]{1,0:T(8,128)S(1)}, u32[]{:S(2)}, u32[]{:S(2)}) collective-permute-start(f32[128,256]{1,0:T(8,128)S(1)} %get-tuple-element.101), channel_id=1, source_target_pairs={{0,1},{1,0},{2,3},{3,2},{4,5},{5,4},{6,7},{7,6},{8,9},{9,8},{10,11... | collective-permute-start | bytes 393224 | tf_op jit(solution)/shard_map/ppermute | solution.py:41
  108.5 10.4 %collective-permute-start.16 = (f32[128,256]{1,0:T(8,128)S(1)}, f32[128,256]{1,0:T(8,128)S(1)}, u32[]{:S(2)}, u32[]{:S(2)}) collective-permute-start(f32[128,256]{1,0:T(8,128)S(1)} %get-tuple-element.102), channel_id=1, source_target_pairs={{0,2},{1,3},{2,0},{3,1},{4,6},{5,7},{6,4},{7,5},{8,10},{9,11},{10,... | collective-permute-start | bytes 393224 | tf_op jit(solution)/shard_map/ppermute | solution.py:41
  110.0 12.0 %collective-permute-start.17 = (f32[128,256]{1,0:T(8,128)S(1)}, f32[128,256]{1,0:T(8,128)S(1)}, u32[]{:S(2)}, u32[]{:S(2)}) collective-permute-start(f32[128,256]{1,0:T(8,128)S(1)} %get-tuple-element.103), channel_id=1, source_target_pairs={{0,3},{1,2},{2,1},{3,0},{4,7},{5,6},{6,5},{7,4},{8,11},{9,10},{10,... | collective-permute-start | bytes 393224 | tf_op jit(solution)/shard_map/ppermute | solution.py:41
  126.4 15.8 %collective-permute-start.18 = (f32[34,64,128]{2,1,0:T(8,128)S(1)}, f32[34,64,128]{2,1,0:T(8,128)S(1)}, u32[]{:S(2)}, u32[]{:S(2)}) collective-permute-start(f32[34,64,128]{2,1,0:T(8,128)S(1)} %get-tuple-element.113), channel_id=1, source_target_pairs={{0,12},{1,49},{2,14},{3,51},{4,0},{5,53},{6,2},{7,55},{8,4},{9,57}... | collective-permute-start | bytes 3342344 | tf_op jit(solution)/shard_map/ppermute | solution.py:33
  126.5 29.1 %collective-permute-start.19 = (f32[34,64,128]{2,1,0:T(8,128)S(1)}, f32[34,64,128]{2,1,0:T(8,128)S(1)}, u32[]{:S(2)}, u32[]{:S(2)}) collective-permute-start(f32[34,64,128]{2,1,0:T(8,128)S(1)} %get-tuple-element.114), channel_id=1, source_target_pairs={{0,8},{1,33},{2,10},{3,35},{4,12},{5,37},{6,14},{7,39},{8,0},{9,41... | collective-permute-start | bytes 3342344 | tf_op jit(solution)/shard_map/ppermute | solution.py:33
  130.2 26.2 %collective-permute-start.20 = (f32[34,64,128]{2,1,0:T(8,128)S(1)}, f32[34,64,128]{2,1,0:T(8,128)S(1)}, u32[]{:S(2)}, u32[]{:S(2)}) collective-permute-start(f32[34,64,128]{2,1,0:T(8,128)S(1)} %get-tuple-element.115), channel_id=1, source_target_pairs={{0,4},{1,17},{2,6},{3,19},{4,8},{5,21},{6,10},{7,23},{8,12},{9,25}... | collective-permute-start | bytes 3342344 | tf_op jit(solution)/shard_map/ppermute | solution.py:33
  130.2 1.9 collective-permute-start.21
  130.8 8.2 %collective-permute-start.22 = (f32[64,256]{1,0:T(8,128)S(1)}, f32[64,256]{1,0:T(8,128)S(1)}, u32[]{:S(2)}, u32[]{:S(2)}) collective-permute-start(f32[64,256]{1,0:T(8,128)S(1)} %get-tuple-element.118), channel_id=1, source_target_pairs={{0,2},{1,3},{2,0},{3,1},{4,6},{5,7},{6,4},{7,5},{8,10},{9,11},{10,... | collective-permute-start | bytes 196616 | tf_op jit(solution)/shard_map/ppermute | solution.py:41
  132.2 8.2 %collective-permute-start.23 = (f32[64,256]{1,0:T(8,128)S(1)}, f32[64,256]{1,0:T(8,128)S(1)}, u32[]{:S(2)}, u32[]{:S(2)}) collective-permute-start(f32[64,256]{1,0:T(8,128)S(1)} %get-tuple-element.119), channel_id=1, source_target_pairs={{0,3},{1,2},{2,1},{3,0},{4,7},{5,6},{6,5},{7,4},{8,11},{9,10},{10,... | collective-permute-start | bytes 196616 | tf_op jit(solution)/shard_map/ppermute | solution.py:41
  159.2 15.6 %collective-permute-start.24 = (f32[34,64,128]{2,1,0:T(8,128)S(1)}, f32[34,64,128]{2,1,0:T(8,128)S(1)}, u32[]{:S(2)}, u32[]{:S(2)}) collective-permute-start(f32[34,64,128]{2,1,0:T(8,128)S(1)} %get-tuple-element.129), channel_id=1, source_target_pairs={{0,48},{1,13},{2,50},{3,15},{4,52},{5,1},{6,54},{7,3},{8,56},{9,5}... | collective-permute-start | bytes 3342344 | tf_op jit(solution)/shard_map/ppermute | solution.py:33
  159.3 17.7 %collective-permute-start.25 = (f32[34,64,128]{2,1,0:T(8,128)S(1)}, f32[34,64,128]{2,1,0:T(8,128)S(1)}, u32[]{:S(2)}, u32[]{:S(2)}) collective-permute-start(f32[34,64,128]{2,1,0:T(8,128)S(1)} %get-tuple-element.130), channel_id=1, source_target_pairs={{0,32},{1,9},{2,34},{3,11},{4,36},{5,13},{6,38},{7,15},{8,40},{9,1... | collective-permute-start | bytes 3342344 | tf_op jit(solution)/shard_map/ppermute | solution.py:33
  163.4 25.4 %collective-permute-start.26 = (f32[34,64,128]{2,1,0:T(8,128)S(1)}, f32[34,64,128]{2,1,0:T(8,128)S(1)}, u32[]{:S(2)}, u32[]{:S(2)}) collective-permute-start(f32[34,64,128]{2,1,0:T(8,128)S(1)} %get-tuple-element.131), channel_id=1, source_target_pairs={{0,16},{1,5},{2,18},{3,7},{4,20},{5,9},{6,22},{7,11},{8,24},{9,13}... | collective-permute-start | bytes 3342344 | tf_op jit(solution)/shard_map/ppermute | solution.py:33
  190.2 18.3 %collective-permute-start.27 = (f32[10,64,128]{2,1,0:T(8,128)S(1)}, f32[10,64,128]{2,1,0:T(8,128)S(1)}, u32[]{:S(2)}, u32[]{:S(2)}) collective-permute-start(f32[10,64,128]{2,1,0:T(8,128)S(1)} %get-tuple-element.133), channel_id=1, source_target_pairs={{0,64},{4,68},{8,72},{12,76},{16,80},{20,84},{24,88},{28,92},{32,9... | collective-permute-start | bytes 983048 | tf_op jit(solution)/shard_map/ppermute | solution.py:37
  198.0 24.5 %collective-permute-start.28 = (f32[10,64,128]{2,1,0:T(8,128)S(1)}, f32[10,64,128]{2,1,0:T(8,128)S(1)}, u32[]{:S(2)}, u32[]{:S(2)}) collective-permute-start(f32[10,64,128]{2,1,0:T(8,128)S(1)} %get-tuple-element.134), channel_id=1, source_target_pairs={{0,128},{4,132},{8,136},{12,140},{16,144},{20,148},{24,152},{28,15... | collective-permute-start | bytes 983048 | tf_op jit(solution)/shard_map/ppermute | solution.py:37
  198.0 24.5 %collective-permute-start.29 = (f32[10,64,128]{2,1,0:T(8,128)S(1)}, f32[10,64,128]{2,1,0:T(8,128)S(1)}, u32[]{:S(2)}, u32[]{:S(2)}) collective-permute-start(f32[10,64,128]{2,1,0:T(8,128)S(1)} %get-tuple-element.135), channel_id=1, source_target_pairs={{0,192},{4,196},{8,200},{12,204},{16,208},{20,212},{24,216},{28,22... | collective-permute-start | bytes 983048 | tf_op jit(solution)/shard_map/ppermute | solution.py:37
  (7 other events, 114.9 us)

commit v2 on v1

--- a/solution.py
+++ b/solution.py
@@ -95,17 +95,22 @@
     wait(copies)
 
 
+SPANS = ((0, RB), (RB, RB), (2 * RB, 2 * RB))
+
+
 def pack_kernel(pick, *refs):
-    n = SIDE
-    ins, outs, (held, built, in_sems, out_sems) = refs[:n], refs[n : 2 * n], refs[2 * n :]
-    wait(fetch(ins, [held.at[i] for i in range(n)], in_sems))
+    n = SIDE * len(SPANS)
+    ins, outs = refs[:n], refs[n : n + SIDE]
+    held, built, in_sems, out_sems = refs[n + SIDE :]
+    spots = [held.at[near, pl.ds(*span)] for span in SPANS for near in range(SIDE)]
+    wait(fetch(ins, spots, in_sems))
     copies = []
-    for far in (2, 1, 3, 0):
+    for far in (2, 3, 1, 0):
         for near in range(SIDE):
             for k in range(SIDE):
                 for p in range(2):
-                    block = pick[((far * SIDE + near) * SIDE + k) * 2 + p]
-                    built[far, (near * SIDE + k) * 2 + p] = held[near, k * RB + block]
+                    at = (near * SIDE + k) * 2 + p
+                    built[far, at] = held[near, k * RB + pick[far * PER + at]]
         copy = pltpu.make_async_copy(built.at[far], outs[far], out_sems.at[far])
         copy.start()
         copies.append(copy)
@@ -113,33 +118,50 @@
 
 
 def unpack_kernel(pick, *refs):
-    n = SIDE
-    ins, outs, (held, built, in_sems, out_sems) = refs[:n], refs[n : 2 * n], refs[2 * n :]
-    loads = fetch(ins, [held.at[i] for i in range(n)], in_sems)
+    n = SIDE * len(SPANS)
+    ins, outs = refs[:SIDE], refs[SIDE : SIDE + n]
+    held, built, in_sems, out_sems = refs[SIDE + n :]
+    loads = fetch(ins, [held.at[i] for i in range(SIDE)], in_sems)
     built[...] = jnp.zeros_like(built)
     wait(loads)
     tail = (held[0, PER:] + held[1, PER:]) + (held[2, PER:] + held[3, PER:])
     copies = []
-    for near in (2, 1, 3, 0):
-        for far in range(SIDE):
-            for k in range(SIDE):
-                for p in range(2):
-                    block = pick[((far * SIDE + near) * SIDE + k) * 2 + p]
-                    built[near, k * RB + block] += held[far, (near * SIDE + k) * 2 + p]
-        built[near, PER:] = tail
-        copy = pltpu.make_async_copy(built.at[near], outs[near], out_sems.at[near])
-        copy.start()
-        copies.append(copy)
+    for part in (2, 1, 0):
+        start, size = SPANS[part]
+        for near in (1, 2, 3, 0):
+            for k in range(start // RB, (start + size) // RB):
+                for far in range(SIDE):
+                    for p in range(2):
+                        at = (near * SIDE + k) * 2 + p
+                        built[near, k * RB + pick[far * PER + at]] += held[far, at]
+            if part == 2:
+                built[near, PER:] = tail
+            message = part * SIDE + near
+            copy = pltpu.make_async_copy(
+                built.at[near, pl.ds(start, size + 2 * (part == 2))],
+                outs[message],
+                out_sems.at[message],
+            )
+            copy.start()
+            copies.append(copy)
     wait(copies)
 
 
-def join_kernel(*refs):
-    n = SIDE
-    ins, outs, (held, built, in_sems, out_sems) = refs[:n], refs[n : 2 * n], refs[2 * n :]
-    wait(fetch(ins, [held.at[i] for i in range(n)], in_sems))
+def join_kernel(count, *refs):
+    n = SIDE if count == 2 else SIDE + 1
+    ins, outs = refs[:n], refs[n : n + count]
+    held, built, in_sems, out_sems = refs[n + count :]
+    targets = [held.at[i] for i in range(SIDE)]
+    if count == 1:
+        ins = ins[:SIDE] + (ins[SIDE].at[pl.ds(RB, 2)],)
+        targets.append(built.at[0, pl.ds(RB, 2)])
+    wait(fetch(ins, targets, in_sems))
     copies = []
-    for k in (2, 3, 1, 0):
-        for target, source in ((pl.ds(0, RB), pl.ds(k * RB, RB)), (pl.ds(RB, 2), pl.ds(PER, 2))):
+    for k in range(count):
+        spans = [(pl.ds(0, RB), pl.ds(k * RB, RB))]
+        if count == 2:
+            spans.append((pl.ds(RB, 2), pl.ds(2 * RB, 2)))
+        for target, source in spans:
             built[k, target] = (held[0, source] + held[1, source]) + (
                 held[2, source] + held[3, source]
             )
@@ -163,7 +185,8 @@
 ):
     span = tiles.shape[0] // CUTS
     cuts = [pl.ds(i * span, span) for i in range(CUTS)]
-    loads = fetch((q0, q1, q2, q3), [blocks.at[pl.ds(i * PER, PER)] for i in range(SIDE)], sems)
+    parts = (q0, q1, q2, q3)
+    loads = fetch(parts, [blocks.at[pl.ds(i * PER, PER)] for i in range(SIDE)], sems)
     tile_loads = fetch([tiles.at[c] for c in cuts], [held.at[c] for c in cuts], tile_sems)
     total[...] = jnp.zeros_like(total)
     wait(loads)
@@ -331,9 +354,41 @@
     at_back = jnp.where(live, at, n_blocks)
     info = jnp.stack([block_count[0], own_col.astype(jnp.int32)])
 
+    def piece(value, d):
+        return lax.dynamic_slice_in_dim(value, (own_col ^ d) * quarter, quarter, 1)
+
+    def exchange(pieces):
+        return [pieces[0]] + [swap_col(pieces[d], d) for d in (1, 2, 3)]
+
+    shape = (PER, width, size)
+    longer = (PER + 2, width, size)
+    lengths = [size + 2 * (i == 2) for i, (_, size) in enumerate(SPANS)]
+
+    def spread(value):
+        return [value] + [shift(value, d, 0) for d in (1, 2, 3)]
+
+    def route(values):
+        return [values[0]] + [shift(values[d], -d, 0) for d in (1, 2, 3)]
+
+    def join(arrived, *more):
+        count = 1 if more else 2
+        return call(
+            functools.partial(join_kernel, count),
+            "join%d" % count,
+            [struct(RB + 2, width, size)] * count,
+            [HBM] * (SIDE + len(more)),
+            [HBM] * count,
+            [
+                pltpu.VMEM((SIDE,) + arrived[0].shape, F32),
+                pltpu.VMEM((count, RB + 2, width, size), F32),
+                DMA((SIDE + 1,)),
+                DMA((count,)),
+            ],
+        )(*arrived, *more)
+
     scaled = features_t * root
     blocked = scaled.reshape(width, RB, size).transpose(1, 0, 2)
-    stack = [blocked] + [swap_z(blocked, d) for d in range(1, SIDE)]
+    deep = [blocked] + [swap_z(blocked, d) for d in range(1, SIDE)]
     adjacency = call(
         convert_kernel,
         "convert",
@@ -343,27 +398,27 @@
         [pltpu.VMEM(tiles.shape, jnp.int32), pltpu.VMEM(tiles.shape, BF16), DMA((8,)), DMA((8,))],
         nbytes=12 << 20,
     )(tiles)
-    stack, adjacency, pick = lax.optimization_barrier((stack, adjacency, pick))
-    stack = jnp.concatenate(stack)
-    arrived = [stack] + [shift(stack, d, 0) for d in (1, 2, 3)]
-    shape = (PER, width, size)
+    cot = [piece(cotangent_t, d) for d in range(4)]
+    own_part = spread(blocked)
+    next_part = spread(deep[1])
+    own_part, next_part, far_deep, adjacency, pick, cot = lax.optimization_barrier(
+        (own_part, next_part, deep[2:], adjacency, pick, cot)
+    )
+    far_part = spread(jnp.concatenate(far_deep))
     packed = call(
         pack_kernel,
         "pack",
         [struct(*shape)] * SIDE,
-        [SMEM] + [HBM] * SIDE,
+        [SMEM] + [HBM] * (3 * SIDE),
         [HBM] * SIDE,
-        [pltpu.VMEM((SIDE,) + shape, F32)] * 2 + [DMA((SIDE,))] * 2,
+        [
+            pltpu.VMEM((SIDE,) + shape, F32),
+            pltpu.VMEM((SIDE,) + shape, F32),
+            DMA((3 * SIDE,)),
+            DMA((SIDE,)),
+        ],
         nbytes=8 << 20,
-    )(pick, *arrived)
-
-    def piece(value, d):
-        return lax.dynamic_slice_in_dim(value, (own_col ^ d) * quarter, quarter, 1)
-
-    def exchange(pieces):
-        return [pieces[0]] + [swap_col(pieces[d], d) for d in (1, 2, 3)]
-
-    cot = [piece(cotangent_t, d) for d in range(4)]
+    )(pick, *own_part, *next_part, *far_part)
     cot, packed = lax.optimization_barrier((cot, packed))
     got = [packed[0]] + [shift(packed[d], 0, d) for d in (1, 2, 3)]
     cot = exchange(cot)
@@ -394,11 +449,10 @@
     )(info, *agg, *cot, weight)
     back = exchange(dense[:4])
 
-    shape = (PER + 2, width, size)
     direct, *sent = call(
         backward_kernel,
         "backward",
-        [struct(width, nodes)] + [struct(*shape)] * SIDE,
+        [struct(width, nodes)] + [struct(*longer)] * SIDE,
         [SMEM] * 3 + [VMEM] * 6 + [HBM],
         [VMEM] + [HBM] * SIDE,
         [
@@ -420,27 +474,30 @@
     summed = call(
         unpack_kernel,
         "unpack",
-        [struct(*shape)] * SIDE,
+        [struct(length, width, size) for length in lengths for _ in range(SIDE)],
         [SMEM] + [HBM] * SIDE,
-        [HBM] * SIDE,
-        [pltpu.VMEM((SIDE,) + shape, F32)] * 2 + [DMA((SIDE,))] * 2,
+        [HBM] * (3 * SIDE),
+        [
+            pltpu.VMEM((SIDE,) + longer, F32),
+            pltpu.VMEM((SIDE,) + longer, F32),
+            DMA((SIDE,)),
+            DMA((3 * SIDE,)),
+        ],
         nbytes=8 << 20,
     )(pick, *home)
-    arrived = [summed[0]] + [shift(summed[d], -d, 0) for d in (1, 2, 3)]
-    ends = call(
-        join_kernel,
-        "join",
-        [struct(RB + 2, width, size)] * SIDE,
-        [HBM] * SIDE,
-        [HBM] * SIDE,
-        [pltpu.VMEM((SIDE,) + shape, F32), pltpu.VMEM((SIDE, RB + 2, width, size), F32)]
-        + [DMA((SIDE,))] * 2,
-        nbytes=8 << 20,
-    )(*arrived)
-    total = ends[0] + swap_z(ends[1], 1) + swap_z(ends[2], 2) + swap_z(ends[3], 3)
-    summed_back = total[:RB].transpose(1, 0, 2).reshape(width, nodes)
+    own_part, next_part, far_part = summed[:SIDE], summed[SIDE : 2 * SIDE], summed[2 * SIDE :]
+    far_part, next_part = lax.optimization_barrier((route(far_part), next_part))
+    far_ends = join(far_part)
+    next_part, own_part = lax.optimization_barrier((route(next_part), own_part))
+    next_end = join(next_part, far_ends[0])[0]
+    own_part = route(own_part)
+    ends = [swap_z(next_end, 1), swap_z(far_ends[0], 2), swap_z(far_ends[1], 3)]
+    total = (ends[0][:RB] + ends[1][:RB]) + ends[2][:RB]
+    total += (own_part[0] + own_part[1]) + (own_part[2] + own_part[3])
+    tail = (far_ends[0][RB:] + ends[0][RB:]) + (ends[1][RB:] + ends[2][RB:])
+    summed_back = total.transpose(1, 0, 2).reshape(width, nodes)
     h_grad = (root * summed_back + direct).T
-    grad = total[RB:].transpose(1, 0, 2).reshape(width, 4 * width)
+    grad = tail.transpose(1, 0, 2).reshape(width, 4 * width)
 
     output = jnp.zeros((width, nodes), F32)
     for d in range(4):

time: 228 us -> 212 us (0.930); the launches traced: 224 us -> 211 us
  waiting for transfers between devices: 131 us -> 97 us
  starting transfers between devices: 59.4 us -> 83.1 us
  Pallas kernels: 18.9 us -> 16.2 us
    ppermute x12 -> x24, starting transfers between devices: 18.7 us -> 37.9 us  [shift(): return lax.ppermute(value, ('row', 'col'), pairs)]
    ppermute x12 -> x24, waiting for transfers between devices: 71.6 us -> 53.4 us  [shift(): return lax.ppermute(value, ('row', 'col'), pairs)]
    ppermute x6, waiting for transfers between devices: 31.3 us -> 13.3 us  [swap_z(): lax.ppermute(value, 'row', [(r, r ^ k * SIDE * SIDE) for r in range(SIDE...]
    ppermute x6, starting transfers between devices: 15.5 us -> 20.4 us  [swap_z(): lax.ppermute(value, 'row', [(r, r ^ k * SIDE * SIDE) for r in range(SIDE...]
    pallas_call x4 -> x5, Pallas kernels: 11.3 us -> 9.49 us  [the longest x1 3.75 us: on_device(): call(backward_kernel, 'backward', [struct(width, nodes)] + [struct(*longe...]
  transfers between devices with their start and end apart: 30 -> 42, of which waited for: 20 -> 21; matrix products, arithmetic and copies ran while one was open for 1% -> 2% of each run, Pallas kernels for 1% -> 1%
where the time goes in v2:
time: 212 us; the launch traced here: 211 us
  waiting for transfers between devices  97 us (46%)
  starting transfers between devices  83.1 us (39%)
  Pallas kernels  16.2 us (8%)
  local copies, waits for them, and re-layouts  9.32 us (4%)
  other arithmetic  3.5 us (2%)
    ppermute x24, waiting for transfers between devices, shift(): return lax.ppermute(value, ('row', 'col'), pairs)  53.4 us
    ppermute x24, starting transfers between devices, shift(): return lax.ppermute(value, ('row', 'col'), pairs)  37.9 us
    ppermute x12, waiting for transfers between devices, swap_col(): return lax.ppermute(value, 'col', [(c, c ^ k) for c in range(4)])  30.2 us
    ppermute x12, starting transfers between devices, swap_col(): return lax.ppermute(value, 'col', [(c, c ^ k) for c in range(4)])  24.8 us
    ppermute x6, starting transfers between devices, swap_z(): lax.ppermute(value, 'row', [(r, r ^ k * SIDE * SIDE) for r in range(SIDE...  20.4 us
    ppermute x6, waiting for transfers between devices, swap_z(): lax.ppermute(value, 'row', [(r, r ^ k * SIDE * SIDE) for r in range(SIDE...  13.3 us
    unnamed x22, local copies, waits for them, and re-layouts  7.48 us
  transfers between devices with their start and end apart: 42, of which 21 were waited for; matrix products, arithmetic and copies ran while one was open for 2% of the time, Pallas kernels for 1%

profile of v2, /device:TPU:8, one launch (start us, length us, event | category | flops | bytes accessed | tf_op | source)
XLA Modules:
  0.0 210.8 jit_solution(14272081413133465856)
XLA Ops:
  10.1 3.3 %collective-permute-start.7 = (f32[8,64,128]{2,1,0:T(8,128)S(1)}, f32[8,64,128]{2,1,0:T(8,128)S(1)}, u32[]{:S(2)}, u32[]{:S(2)}) collective-permute-start(f32[8,64,128]{2,1,0:T(8,128)S(1)} %bitcast.49), channel_id=1, source_target_pairs={{0,128},{4,132},{8,136},{12,140},{16,144},{20,148},{24,152},{28,15... | collective-permute-start | bytes 786440 | tf_op jit(solution)/shard_map/ppermute | solution.py:37
  13.5 2.8 %collective-permute-start.8 = (f32[8,64,128]{2,1,0:T(8,128)S(1)}, f32[8,64,128]{2,1,0:T(8,128)S(1)}, u32[]{:S(2)}, u32[]{:S(2)}) collective-permute-start(f32[8,64,128]{2,1,0:T(8,128)S(1)} %bitcast.50), channel_id=1, source_target_pairs={{0,192},{4,196},{8,200},{12,204},{16,208},{20,212},{24,216},{28,22... | collective-permute-start | bytes 786440 | tf_op jit(solution)/shard_map/ppermute | solution.py:37
  17.8 2.8 %collective-permute-start.5 = (f32[8,64,128]{2,1,0:T(8,128)S(1)}, f32[8,64,128]{2,1,0:T(8,128)S(1)}, u32[]{:S(2)}, u32[]{:S(2)}) collective-permute-start(f32[8,64,128]{2,1,0:T(8,128)S(1)} %collective-permute-done.3.refs_4_), channel_id=1, source_target_pairs={{0,32},{1,9},{2,34},{3,11},{4,36},{5,13},{6,38},{7,15},{8,40},{9,1... | collective-permute-start | bytes 786440 | tf_op jit(solution)/shard_map/ppermute | solution.py:33
  25.8 3.4 %copy-done.2 = s32[128,128,128]{2,1,0:T(8,128)S(1)} copy-done((s32[128,128,128]{2,1,0:T(8,128)S(1)}, s32[128,128,128]{2,1,0:T(8,128)}, u32[]{:S(2)}) %copy-start.2) | copy-done | bytes 8388632
  33.7 2.8 %collective-permute-start.11 = (f32[16,64,128]{2,1,0:T(8,128)S(1)}, f32[16,64,128]{2,1,0:T(8,128)S(1)}, u32[]{:S(2)}, u32[]{:S(2)}) collective-permute-start(f32[16,64,128]{2,1,0:T(8,128)S(1)} %constant_dynamic-update-slice_fusion.refs_8_), channel_id=1, source_target_pairs={{0,48},{1,13},{2,50},{3,15},{4,52},{5,1},{6,54},{7,3},{8,56},{9,5}... | collective-permute-start | bytes 1572872 | tf_op jit(solution)/shard_map/ppermute | solution.py:33
  36.5 7.5 %collective-permute-done.10.refs_10_ = f32[16,64,128]{2,1,0:T(8,128)S(1)} collective-permute-done((f32[16,64,128]{2,1,0:T(8,128)S(1)}, f32[16,64,128]{2,1,0:T(8,128)S(1)}, u32[]{:S(2)}, u32[]{:S(2)}) %collective-permute-start.10) | collective-permute-done | bytes 524320 | tf_op jit(solution)/shard_map/ppermute | solution.py:33
  44.0 2.9 %collective-permute-done.11.refs_11_ = f32[16,64,128]{2,1,0:T(8,128)S(1)} collective-permute-done((f32[16,64,128]{2,1,0:T(8,128)S(1)}, f32[16,64,128]{2,1,0:T(8,128)S(1)}, u32[]{:S(2)}, u32[]{:S(2)}) %collective-permute-start.11) | collective-permute-done | bytes 524320 | tf_op jit(solution)/shard_map/ppermute | solution.py:33
  57.4 6.0 %collective-permute-start.16 = (f32[64,256]{1,0:T(8,128)S(1)}, f32[64,256]{1,0:T(8,128)S(1)}, u32[]{:S(2)}, u32[]{:S(2)}) collective-permute-start(f32[64,256]{1,0:T(8,128)S(1)} %get-tuple-element.128), channel_id=1, source_target_pairs={{0,2},{1,3},{2,0},{3,1},{4,6},{5,7},{6,4},{7,5},{8,10},{9,11},{10,... | collective-permute-start | bytes 196616 | tf_op jit(solution)/shard_map/ppermute | solution.py:41
  66.1 5.4 %collective-permute-done.17.c3 = f32[64,256]{1,0:T(8,128)S(1)} collective-permute-done((f32[64,256]{1,0:T(8,128)S(1)}, f32[64,256]{1,0:T(8,128)S(1)}, u32[]{:S(2)}, u32[]{:S(2)}) %collective-permute-start.17) | collective-permute-done | bytes 65568 | tf_op jit(solution)/shard_map/ppermute | solution.py:41
  71.4 5.3 %collective-permute-done.12.q1 = f32[32,64,128]{2,1,0:T(8,128)S(1)} collective-permute-done((f32[32,64,128]{2,1,0:T(8,128)S(1)}, f32[32,64,128]{2,1,0:T(8,128)S(1)}, u32[]{:S(2)}, u32[]{:S(2)}) %collective-permute-start.12) | collective-permute-done | bytes 1048608 | tf_op jit(solution)/shard_map/ppermute | solution.py:33
  76.7 3.3 %collective-permute-done.14.q3 = f32[32,64,128]{2,1,0:T(8,128)S(1)} collective-permute-done((f32[32,64,128]{2,1,0:T(8,128)S(1)}, f32[32,64,128]{2,1,0:T(8,128)S(1)}, u32[]{:S(2)}, u32[]{:S(2)}) %collective-permute-start.14) | collective-permute-done | bytes 1048608 | tf_op jit(solution)/shard_map/ppermute | solution.py:33
  80.0 3.7 %forward.1 = (f32[64,256]{1,0:T(8,128)S(1)}, f32[64,256]{1,0:T(8,128)S(1)}, f32[64,256]{1,0:T(8,128)S(1)}, f32[64,256]{1,0:T(8,128)S(1)}) custom-call(s32[128]{0:T(128)S(1)} %compare_select_fusion.12.rows, s32[128]{0:T(128)S(1)} %get-tuple-element.202.at, s32[2]{0:T(128)S(1)} %pad_add_fusion.info, f32[64,1024]{1,0:T(8,128)S(1)} %get-tuple-element.204.scaled, ...), custom_call_target="tpu_custom_call" | custom-call | bytes 16777216 | tf_op jit(solution)/shard_map/forward/pallas_call | solution.py:426
  83.8 6.0 %collective-permute-start.19 = (f32[64,256]{1,0:T(8,128)S(1)}, f32[64,256]{1,0:T(8,128)S(1)}, u32[]{:S(2)}, u32[]{:S(2)}) collective-permute-start(f32[64,256]{1,0:T(8,128)S(1)} %get-tuple-element.136), channel_id=1, source_target_pairs={{0,2},{1,3},{2,0},{3,1},{4,6},{5,7},{6,4},{7,5},{8,10},{9,11},{10,... | collective-permute-start | bytes 196616 | tf_op jit(solution)/shard_map/ppermute | solution.py:41
  89.9 3.0 %collective-permute-done.19.a2 = f32[64,256]{1,0:T(8,128)S(1)} collective-permute-done((f32[64,256]{1,0:T(8,128)S(1)}, f32[64,256]{1,0:T(8,128)S(1)}, u32[]{:S(2)}, u32[]{:S(2)}) %collective-permute-start.19) | collective-permute-done | bytes 65568 | tf_op jit(solution)/shard_map/ppermute | solution.py:41
  92.9 5.8 %collective-permute-done.20.a3 = f32[64,256]{1,0:T(8,128)S(1)} collective-permute-done((f32[64,256]{1,0:T(8,128)S(1)}, f32[64,256]{1,0:T(8,128)S(1)}, u32[]{:S(2)}, u32[]{:S(2)}) %collective-permute-start.20) | collective-permute-done | bytes 65568 | tf_op jit(solution)/shard_map/ppermute | solution.py:41
  101.7 4.1 %collective-permute-start.23 = (f32[128,256]{1,0:T(8,128)S(1)}, f32[128,256]{1,0:T(8,128)S(1)}, u32[]{:S(2)}, u32[]{:S(2)}) collective-permute-start(f32[128,256]{1,0:T(8,128)S(1)} %get-tuple-element.145), channel_id=1, source_target_pairs={{0,3},{1,2},{2,1},{3,0},{4,7},{5,6},{6,5},{7,4},{8,11},{9,10},{10,... | collective-permute-start | bytes 393224 | tf_op jit(solution)/shard_map/ppermute | solution.py:41
  105.8 4.8 %collective-permute-done.22.i2 = f32[128,256]{1,0:T(8,128)S(1)} collective-permute-done((f32[128,256]{1,0:T(8,128)S(1)}, f32[128,256]{1,0:T(8,128)S(1)}, u32[]{:S(2)}, u32[]{:S(2)}) %collective-permute-start.22) | collective-permute-done | bytes 131104 | tf_op jit(solution)/shard_map/ppermute | solution.py:41
  110.6 3.6 %collective-permute-done.23.i3 = f32[128,256]{1,0:T(8,128)S(1)} collective-permute-done((f32[128,256]{1,0:T(8,128)S(1)}, f32[128,256]{1,0:T(8,128)S(1)}, u32[]{:S(2)}, u32[]{:S(2)}) %collective-permute-start.23) | collective-permute-done | bytes 131104 | tf_op jit(solution)/shard_map/ppermute | solution.py:41
  114.2 3.7 %backward.1 = (f32[64,1024]{1,0:T(8,128)S(1)}, f32[34,64,128]{2,1,0:T(8,128)S(1)}, f32[34,64,128]{2,1,0:T(8,128)S(1)}, f32[34,64,128]{2,1,0:T(8,128)S(1)}, f32[34,64,128]{2,1,0:T(8,128)S(1)}) custom-call(s32[128]{0:T(128)S(1)} %copy-done.4, s32[128]{0:T(128)S(1)} %get-tuple-element.201.at, s32[2]{0:T(128)S(1)} %pad_add_fusion.info, f32[1,1024]{1,0:T(1,128)S(1)} %bitcast.53, ...), custom_call_target="tpu_custom_call" | custom-call | bytes 16777216 | tf_op jit(solution)/shard_map/backward/pallas_call | solution.py:452
  117.9 3.5 %collective-permute-start.24 = (f32[34,64,128]{2,1,0:T(8,128)S(1)}, f32[34,64,128]{2,1,0:T(8,128)S(1)}, u32[]{:S(2)}, u32[]{:S(2)}) collective-permute-start(f32[34,64,128]{2,1,0:T(8,128)S(1)} %get-tuple-element.155), channel_id=1, source_target_pairs={{0,12},{1,49},{2,14},{3,51},{4,0},{5,53},{6,2},{7,55},{8,4},{9,57}... | collective-permute-start | bytes 3342344 | tf_op jit(solution)/shard_map/ppermute | solution.py:33
  122.9 3.8 %collective-permute-start.28 = (f32[64,256]{1,0:T(8,128)S(1)}, f32[64,256]{1,0:T(8,128)S(1)}, u32[]{:S(2)}, u32[]{:S(2)}) collective-permute-start(f32[64,256]{1,0:T(8,128)S(1)} %get-tuple-element.160), channel_id=1, source_target_pairs={{0,2},{1,3},{2,0},{3,1},{4,6},{5,7},{6,4},{7,5},{8,10},{9,11},{10,... | collective-permute-start | bytes 196616 | tf_op jit(solution)/shard_map/ppermute | solution.py:41
  131.3 3.4 %collective-permute-done.29 = f32[64,256]{1,0:T(8,128)S(1)} collective-permute-done((f32[64,256]{1,0:T(8,128)S(1)}, f32[64,256]{1,0:T(8,128)S(1)}, u32[]{:S(2)}, u32[]{:S(2)}) %collective-permute-start.29) | collective-permute-done | bytes 65568 | tf_op jit(solution)/shard_map/ppermute | solution.py:41
  134.7 11.6 %collective-permute-done.25.refs_2_ = f32[34,64,128]{2,1,0:T(8,128)S(1)} collective-permute-done((f32[34,64,128]{2,1,0:T(8,128)S(1)}, f32[34,64,128]{2,1,0:T(8,128)S(1)}, u32[]{:S(2)}, u32[]{:S(2)}) %collective-permute-start.25) | collective-permute-done | bytes 1114144 | tf_op jit(solution)/shard_map/ppermute | solution.py:33
  147.5 2.9 %unpack.1 = (f32[8,64,128]{2,1,0:T(8,128)S(1)}, f32[8,64,128]{2,1,0:T(8,128)S(1)}, f32[8,64,128]{2,1,0:T(8,128)S(1)}, f32[8,64,128]{2,1,0:T(8,128)S(1)}, f32[8,6...) custom-call(s32[128]{0:T(128)S(1)} %reshape.122.pick, ...), custom_call_target="tpu_custom_call" | custom-call | bytes 8388608 | tf_op jit(solution)/shard_map/unpack/pallas_call | solution.py:474
  152.6 3.3 %collective-permute-start.31 = (f32[18,64,128]{2,1,0:T(8,128)S(1)}, f32[18,64,128]{2,1,0:T(8,128)S(1)}, u32[]{:S(2)}, u32[]{:S(2)}) collective-permute-start(f32[18,64,128]{2,1,0:T(8,128)S(1)} %get-tuple-element.172), channel_id=1, source_target_pairs={{0,32},{1,9},{2,34},{3,11},{4,36},{5,13},{6,38},{7,15},{8,40},{9,1... | collective-permute-start | bytes 1769480 | tf_op jit(solution)/shard_map/ppermute | solution.py:33
  156.0 5.7 %collective-permute-done.30.refs_1_ = f32[18,64,128]{2,1,0:T(8,128)S(1)} collective-permute-done((f32[18,64,128]{2,1,0:T(8,128)S(1)}, f32[18,64,128]{2,1,0:T(8,128)S(1)}, u32[]{:S(2)}, u32[]{:S(2)}) %collective-permute-start.30) | collective-permute-done | bytes 589856 | tf_op jit(solution)/shard_map/ppermute | solution.py:33
  164.1 6.2 %collective-permute-done.32.refs_3_ = f32[18,64,128]{2,1,0:T(8,128)S(1)} collective-permute-done((f32[18,64,128]{2,1,0:T(8,128)S(1)}, f32[18,64,128]{2,1,0:T(8,128)S(1)}, u32[]{:S(2)}, u32[]{:S(2)}) %collective-permute-start.32) | collective-permute-done | bytes 589856 | tf_op jit(solution)/shard_map/ppermute | solution.py:33
  170.9 3.3 %collective-permute-start.34 = (f32[8,64,128]{2,1,0:T(8,128)S(1)}, f32[8,64,128]{2,1,0:T(8,128)S(1)}, u32[]{:S(2)}, u32[]{:S(2)}) collective-permute-start(f32[8,64,128]{2,1,0:T(8,128)S(1)} %get-tuple-element.180), channel_id=1, source_target_pairs={{0,32},{1,9},{2,34},{3,11},{4,36},{5,13},{6,38},{7,15},{8,40},{9,1... | collective-permute-start | bytes 786440 | tf_op jit(solution)/shard_map/ppermute | solution.py:33
  175.1 5.8 %collective-permute-start.37 = (f32[10,64,128]{2,1,0:T(8,128)S(1)}, f32[10,64,128]{2,1,0:T(8,128)S(1)}, u32[]{:S(2)}, u32[]{:S(2)}) collective-permute-start(f32[10,64,128]{2,1,0:T(8,128)S(1)} %get-tuple-element.194.refs_4_), channel_id=1, source_target_pairs={{0,128},{4,132},{8,136},{12,140},{16,144},{20,148},{24,152},{28,15... | collective-permute-start | bytes 983048 | tf_op jit(solution)/shard_map/ppermute | solution.py:37
  182.8 5.0 %collective-permute-start.36 = (f32[10,64,128]{2,1,0:T(8,128)S(1)}, f32[10,64,128]{2,1,0:T(8,128)S(1)}, u32[]{:S(2)}, u32[]{:S(2)}) collective-permute-start(f32[10,64,128]{2,1,0:T(8,128)S(1)} %join1.1), channel_id=1, source_target_pairs={{0,64},{4,68},{8,72},{12,76},{16,80},{20,84},{24,88},{28,92},{32,9... | collective-permute-start | bytes 983048 | tf_op jit(solution)/shard_map/ppermute | solution.py:37
  190.0 12.3 %collective-permute-done.37 = f32[10,64,128]{2,1,0:T(8,128)S(1)} collective-permute-done((f32[10,64,128]{2,1,0:T(8,128)S(1)}, f32[10,64,128]{2,1,0:T(8,128)S(1)}, u32[]{:S(2)}, u32[]{:S(2)}) %collective-permute-start.37) | collective-permute-done | bytes 327712 | tf_op jit(solution)/shard_map/ppermute | solution.py:37
  205.2 4.7 %collective-permute-done.41 = f32[8,64,128]{2,1,0:T(8,128)S(1)} collective-permute-done((f32[8,64,128]{2,1,0:T(8,128)S(1)}, f32[8,64,128]{2,1,0:T(8,128)S(1)}, u32[]{:S(2)}, u32[]{:S(2)}) %collective-permute-start.41) | collective-permute-done | bytes 262176 | tf_op jit(solution)/shard_map/ppermute | solution.py:33
  (105 shorter events, 57.6 us)
Async XLA Ops:
  2.4 11.1 %collective-permute-start.3 = (f32[8,64,128]{2,1,0:T(8,128)S(1)}, f32[8,64,128]{2,1,0:T(8,128)S(1)}, u32[]{:S(2)}, u32[]{:S(2)}) collective-permute-start(f32[8,64,128]{2,1,0:T(8,128)S(1)} %bitcast.45), channel_id=1, source_target_pairs={{0,64},{4,68},{8,72},{12,76},{16,80},{20,84},{24,88},{28,92},{32,9... | collective-permute-start | bytes 786440 | tf_op jit(solution)/shard_map/ppermute | solution.py:37
  4.4 11.9 %collective-permute-start = (f32[8,64,128]{2,1,0:T(8,128)S(1)}, f32[8,64,128]{2,1,0:T(8,128)S(1)}, u32[]{:S(2)}, u32[]{:S(2)}) collective-permute-start(f32[8,64,128]{2,1,0:T(8,128)S(1)} %bitcast.46), channel_id=1, source_target_pairs={{0,16},{1,5},{2,18},{3,7},{4,20},{5,9},{6,22},{7,11},{8,24},{9,13}... | collective-permute-start | bytes 786440 | tf_op jit(solution)/shard_map/ppermute | solution.py:33
  5.9 11.9 %collective-permute-start.1 = (f32[8,64,128]{2,1,0:T(8,128)S(1)}, f32[8,64,128]{2,1,0:T(8,128)S(1)}, u32[]{:S(2)}, u32[]{:S(2)}) collective-permute-start(f32[8,64,128]{2,1,0:T(8,128)S(1)} %bitcast.47), channel_id=1, source_target_pairs={{0,32},{1,9},{2,34},{3,11},{4,36},{5,13},{6,38},{7,15},{8,40},{9,1... | collective-permute-start | bytes 786440 | tf_op jit(solution)/shard_map/ppermute | solution.py:33
  8.6 11.9 %collective-permute-start.2 = (f32[8,64,128]{2,1,0:T(8,128)S(1)}, f32[8,64,128]{2,1,0:T(8,128)S(1)}, u32[]{:S(2)}, u32[]{:S(2)}) collective-permute-start(f32[8,64,128]{2,1,0:T(8,128)S(1)} %bitcast.48), channel_id=1, source_target_pairs={{0,48},{1,13},{2,50},{3,15},{4,52},{5,1},{6,54},{7,3},{8,56},{9,5}... | collective-permute-start | bytes 786440 | tf_op jit(solution)/shard_map/ppermute | solution.py:33
  10.1 22.9 %collective-permute-start.7 = (f32[8,64,128]{2,1,0:T(8,128)S(1)}, f32[8,64,128]{2,1,0:T(8,128)S(1)}, u32[]{:S(2)}, u32[]{:S(2)}) collective-permute-start(f32[8,64,128]{2,1,0:T(8,128)S(1)} %bitcast.49), channel_id=1, source_target_pairs={{0,128},{4,132},{8,136},{12,140},{16,144},{20,148},{24,152},{28,15... | collective-permute-start | bytes 786440 | tf_op jit(solution)/shard_map/ppermute | solution.py:37
  13.5 19.5 %collective-permute-start.8 = (f32[8,64,128]{2,1,0:T(8,128)S(1)}, f32[8,64,128]{2,1,0:T(8,128)S(1)}, u32[]{:S(2)}, u32[]{:S(2)}) collective-permute-start(f32[8,64,128]{2,1,0:T(8,128)S(1)} %bitcast.50), channel_id=1, source_target_pairs={{0,192},{4,196},{8,200},{12,204},{16,208},{20,212},{24,216},{28,22... | collective-permute-start | bytes 786440 | tf_op jit(solution)/shard_map/ppermute | solution.py:37
  16.3 16.7 %collective-permute-start.4 = (f32[8,64,128]{2,1,0:T(8,128)S(1)}, f32[8,64,128]{2,1,0:T(8,128)S(1)}, u32[]{:S(2)}, u32[]{:S(2)}) collective-permute-start(f32[8,64,128]{2,1,0:T(8,128)S(1)} %collective-permute-done.3.refs_4_), channel_id=1, source_target_pairs={{0,16},{1,5},{2,18},{3,7},{4,20},{5,9},{6,22},{7,11},{8,24},{9,13}... | collective-permute-start | bytes 786440 | tf_op jit(solution)/shard_map/ppermute | solution.py:33
  17.8 15.2 %collective-permute-start.5 = (f32[8,64,128]{2,1,0:T(8,128)S(1)}, f32[8,64,128]{2,1,0:T(8,128)S(1)}, u32[]{:S(2)}, u32[]{:S(2)}) collective-permute-start(f32[8,64,128]{2,1,0:T(8,128)S(1)} %collective-permute-done.3.refs_4_), channel_id=1, source_target_pairs={{0,32},{1,9},{2,34},{3,11},{4,36},{5,13},{6,38},{7,15},{8,40},{9,1... | collective-permute-start | bytes 786440 | tf_op jit(solution)/shard_map/ppermute | solution.py:33
  20.6 12.5 %collective-permute-start.6 = (f32[8,64,128]{2,1,0:T(8,128)S(1)}, f32[8,64,128]{2,1,0:T(8,128)S(1)}, u32[]{:S(2)}, u32[]{:S(2)}) collective-permute-start(f32[8,64,128]{2,1,0:T(8,128)S(1)} %collective-permute-done.3.refs_4_), channel_id=1, source_target_pairs={{0,48},{1,13},{2,50},{3,15},{4,52},{5,1},{6,54},{7,3},{8,56},{9,5}... | collective-permute-start | bytes 786440 | tf_op jit(solution)/shard_map/ppermute | solution.py:33
  33.1 10.9 %collective-permute-start.10 = (f32[16,64,128]{2,1,0:T(8,128)S(1)}, f32[16,64,128]{2,1,0:T(8,128)S(1)}, u32[]{:S(2)}, u32[]{:S(2)}) collective-permute-start(f32[16,64,128]{2,1,0:T(8,128)S(1)} %constant_dynamic-update-slice_fusion.refs_8_), channel_id=1, source_target_pairs={{0,32},{1,9},{2,34},{3,11},{4,36},{5,13},{6,38},{7,15},{8,40},{9,1... | collective-permute-start | bytes 1572872 | tf_op jit(solution)/shard_map/ppermute | solution.py:33
  33.7 13.2 %collective-permute-start.11 = (f32[16,64,128]{2,1,0:T(8,128)S(1)}, f32[16,64,128]{2,1,0:T(8,128)S(1)}, u32[]{:S(2)}, u32[]{:S(2)}) collective-permute-start(f32[16,64,128]{2,1,0:T(8,128)S(1)} %constant_dynamic-update-slice_fusion.refs_8_), channel_id=1, source_target_pairs={{0,48},{1,13},{2,50},{3,15},{4,52},{5,1},{6,54},{7,3},{8,56},{9,5}... | collective-permute-start | bytes 1572872 | tf_op jit(solution)/shard_map/ppermute | solution.py:33
  36.5 13.0 %collective-permute-start.9 = (f32[16,64,128]{2,1,0:T(8,128)S(1)}, f32[16,64,128]{2,1,0:T(8,128)S(1)}, u32[]{:S(2)}, u32[]{:S(2)}) collective-permute-start(f32[16,64,128]{2,1,0:T(8,128)S(1)} %constant_dynamic-update-slice_fusion.refs_8_), channel_id=1, source_target_pairs={{0,16},{1,5},{2,18},{3,7},{4,20},{5,9},{6,22},{7,11},{8,24},{9,13}... | collective-permute-start | bytes 1572872 | tf_op jit(solution)/shard_map/ppermute | solution.py:33
  51.1 25.6 %collective-permute-start.12 = (f32[32,64,128]{2,1,0:T(8,128)S(1)}, f32[32,64,128]{2,1,0:T(8,128)S(1)}, u32[]{:S(2)}, u32[]{:S(2)}) collective-permute-start(f32[32,64,128]{2,1,0:T(8,128)S(1)} %get-tuple-element.123), channel_id=1, source_target_pairs={{0,4},{1,17},{2,6},{3,19},{4,8},{5,21},{6,10},{7,23},{8,12},{9,25}... | collective-permute-start | bytes 3145736 | tf_op jit(solution)/shard_map/ppermute | solution.py:33
  53.1 23.6 %collective-permute-start.13 = (f32[32,64,128]{2,1,0:T(8,128)S(1)}, f32[32,64,128]{2,1,0:T(8,128)S(1)}, u32[]{:S(2)}, u32[]{:S(2)}) collective-permute-start(f32[32,64,128]{2,1,0:T(8,128)S(1)} %get-tuple-element.124), channel_id=1, source_target_pairs={{0,8},{1,33},{2,10},{3,35},{4,12},{5,37},{6,14},{7,39},{8,0},{9,41... | collective-permute-start | bytes 3145736 | tf_op jit(solution)/shard_map/ppermute | solution.py:33
  54.0 26.0 %collective-permute-start.14 = (f32[32,64,128]{2,1,0:T(8,128)S(1)}, f32[32,64,128]{2,1,0:T(8,128)S(1)}, u32[]{:S(2)}, u32[]{:S(2)}) collective-permute-start(f32[32,64,128]{2,1,0:T(8,128)S(1)} %get-tuple-element.125), channel_id=1, source_target_pairs={{0,12},{1,49},{2,14},{3,51},{4,0},{5,53},{6,2},{7,55},{8,4},{9,57}... | collective-permute-start | bytes 3145736 | tf_op jit(solution)/shard_map/ppermute | solution.py:33
  83.8 9.1 %collective-permute-start.19 = (f32[64,256]{1,0:T(8,128)S(1)}, f32[64,256]{1,0:T(8,128)S(1)}, u32[]{:S(2)}, u32[]{:S(2)}) collective-permute-start(f32[64,256]{1,0:T(8,128)S(1)} %get-tuple-element.136), channel_id=1, source_target_pairs={{0,2},{1,3},{2,0},{3,1},{4,6},{5,7},{6,4},{7,5},{8,10},{9,11},{10,... | collective-permute-start | bytes 196616 | tf_op jit(solution)/shard_map/ppermute | solution.py:41
  89.9 8.8 %collective-permute-start.20 = (f32[64,256]{1,0:T(8,128)S(1)}, f32[64,256]{1,0:T(8,128)S(1)}, u32[]{:S(2)}, u32[]{:S(2)}) collective-permute-start(f32[64,256]{1,0:T(8,128)S(1)} %get-tuple-element.137), channel_id=1, source_target_pairs={{0,3},{1,2},{2,1},{3,0},{4,7},{5,6},{6,5},{7,4},{8,11},{9,10},{10,... | collective-permute-start | bytes 196616 | tf_op jit(solution)/shard_map/ppermute | solution.py:41
  100.2 10.4 %collective-permute-start.22 = (f32[128,256]{1,0:T(8,128)S(1)}, f32[128,256]{1,0:T(8,128)S(1)}, u32[]{:S(2)}, u32[]{:S(2)}) collective-permute-start(f32[128,256]{1,0:T(8,128)S(1)} %get-tuple-element.144), channel_id=1, source_target_pairs={{0,2},{1,3},{2,0},{3,1},{4,6},{5,7},{6,4},{7,5},{8,10},{9,11},{10,... | collective-permute-start | bytes 393224 | tf_op jit(solution)/shard_map/ppermute | solution.py:41
  101.7 12.4 %collective-permute-start.23 = (f32[128,256]{1,0:T(8,128)S(1)}, f32[128,256]{1,0:T(8,128)S(1)}, u32[]{:S(2)}, u32[]{:S(2)}) collective-permute-start(f32[128,256]{1,0:T(8,128)S(1)} %get-tuple-element.145), channel_id=1, source_target_pairs={{0,3},{1,2},{2,1},{3,0},{4,7},{5,6},{6,5},{7,4},{8,11},{9,10},{10,... | collective-permute-start | bytes 393224 | tf_op jit(solution)/shard_map/ppermute | solution.py:41
  117.9 16.8 %collective-permute-start.24 = (f32[34,64,128]{2,1,0:T(8,128)S(1)}, f32[34,64,128]{2,1,0:T(8,128)S(1)}, u32[]{:S(2)}, u32[]{:S(2)}) collective-permute-start(f32[34,64,128]{2,1,0:T(8,128)S(1)} %get-tuple-element.155), channel_id=1, source_target_pairs={{0,12},{1,49},{2,14},{3,51},{4,0},{5,53},{6,2},{7,55},{8,4},{9,57}... | collective-permute-start | bytes 3342344 | tf_op jit(solution)/shard_map/ppermute | solution.py:33
  121.4 25.0 %collective-permute-start.25 = (f32[34,64,128]{2,1,0:T(8,128)S(1)}, f32[34,64,128]{2,1,0:T(8,128)S(1)}, u32[]{:S(2)}, u32[]{:S(2)}) collective-permute-start(f32[34,64,128]{2,1,0:T(8,128)S(1)} %get-tuple-element.156), channel_id=1, source_target_pairs={{0,8},{1,33},{2,10},{3,35},{4,12},{5,37},{6,14},{7,39},{8,0},{9,41... | collective-permute-start | bytes 3342344 | tf_op jit(solution)/shard_map/ppermute | solution.py:33
  121.4 26.2 %collective-permute-start.26 = (f32[34,64,128]{2,1,0:T(8,128)S(1)}, f32[34,64,128]{2,1,0:T(8,128)S(1)}, u32[]{:S(2)}, u32[]{:S(2)}) collective-permute-start(f32[34,64,128]{2,1,0:T(8,128)S(1)} %get-tuple-element.157), channel_id=1, source_target_pairs={{0,4},{1,17},{2,6},{3,19},{4,8},{5,21},{6,10},{7,23},{8,12},{9,25}... | collective-permute-start | bytes 3342344 | tf_op jit(solution)/shard_map/ppermute | solution.py:33
  150.4 11.3 %collective-permute-start.30 = (f32[18,64,128]{2,1,0:T(8,128)S(1)}, f32[18,64,128]{2,1,0:T(8,128)S(1)}, u32[]{:S(2)}, u32[]{:S(2)}) collective-permute-start(f32[18,64,128]{2,1,0:T(8,128)S(1)} %get-tuple-element.171), channel_id=1, source_target_pairs={{0,48},{1,13},{2,50},{3,15},{4,52},{5,1},{6,54},{7,3},{8,56},{9,5}... | collective-permute-start | bytes 1769480 | tf_op jit(solution)/shard_map/ppermute | solution.py:33
  152.6 11.5 %collective-permute-start.31 = (f32[18,64,128]{2,1,0:T(8,128)S(1)}, f32[18,64,128]{2,1,0:T(8,128)S(1)}, u32[]{:S(2)}, u32[]{:S(2)}) collective-permute-start(f32[18,64,128]{2,1,0:T(8,128)S(1)} %get-tuple-element.172), channel_id=1, source_target_pairs={{0,32},{1,9},{2,34},{3,11},{4,36},{5,13},{6,38},{7,15},{8,40},{9,1... | collective-permute-start | bytes 1769480 | tf_op jit(solution)/shard_map/ppermute | solution.py:33
  155.9 14.4 %collective-permute-start.32 = (f32[18,64,128]{2,1,0:T(8,128)S(1)}, f32[18,64,128]{2,1,0:T(8,128)S(1)}, u32[]{:S(2)}, u32[]{:S(2)}) collective-permute-start(f32[18,64,128]{2,1,0:T(8,128)S(1)} %get-tuple-element.173), channel_id=1, source_target_pairs={{0,16},{1,5},{2,18},{3,7},{4,20},{5,9},{6,22},{7,11},{8,24},{9,13}... | collective-permute-start | bytes 1769480 | tf_op jit(solution)/shard_map/ppermute | solution.py:33
  170.3 12.2 %collective-permute-start.33 = (f32[8,64,128]{2,1,0:T(8,128)S(1)}, f32[8,64,128]{2,1,0:T(8,128)S(1)}, u32[]{:S(2)}, u32[]{:S(2)}) collective-permute-start(f32[8,64,128]{2,1,0:T(8,128)S(1)} %get-tuple-element.179), channel_id=1, source_target_pairs={{0,48},{1,13},{2,50},{3,15},{4,52},{5,1},{6,54},{7,3},{8,56},{9,5}... | collective-permute-start | bytes 786440 | tf_op jit(solution)/shard_map/ppermute | solution.py:33
  170.9 11.6 %collective-permute-start.34 = (f32[8,64,128]{2,1,0:T(8,128)S(1)}, f32[8,64,128]{2,1,0:T(8,128)S(1)}, u32[]{:S(2)}, u32[]{:S(2)}) collective-permute-start(f32[8,64,128]{2,1,0:T(8,128)S(1)} %get-tuple-element.180), channel_id=1, source_target_pairs={{0,32},{1,9},{2,34},{3,11},{4,36},{5,13},{6,38},{7,15},{8,40},{9,1... | collective-permute-start | bytes 786440 | tf_op jit(solution)/shard_map/ppermute | solution.py:33
  175.1 27.2 %collective-permute-start.37 = (f32[10,64,128]{2,1,0:T(8,128)S(1)}, f32[10,64,128]{2,1,0:T(8,128)S(1)}, u32[]{:S(2)}, u32[]{:S(2)}) collective-permute-start(f32[10,64,128]{2,1,0:T(8,128)S(1)} %get-tuple-element.194.refs_4_), channel_id=1, source_target_pairs={{0,128},{4,132},{8,136},{12,140},{16,144},{20,148},{24,152},{28,15... | collective-permute-start | bytes 983048 | tf_op jit(solution)/shard_map/ppermute | solution.py:37
  180.9 22.7 %collective-permute-start.38 = (f32[10,64,128]{2,1,0:T(8,128)S(1)}, f32[10,64,128]{2,1,0:T(8,128)S(1)}, u32[]{:S(2)}, u32[]{:S(2)}) collective-permute-start(f32[10,64,128]{2,1,0:T(8,128)S(1)} %get-tuple-element.195), channel_id=1, source_target_pairs={{0,192},{4,196},{8,200},{12,204},{16,208},{20,212},{24,216},{28,22... | collective-permute-start | bytes 983048 | tf_op jit(solution)/shard_map/ppermute | solution.py:37
  182.8 21.7 %collective-permute-start.36 = (f32[10,64,128]{2,1,0:T(8,128)S(1)}, f32[10,64,128]{2,1,0:T(8,128)S(1)}, u32[]{:S(2)}, u32[]{:S(2)}) collective-permute-start(f32[10,64,128]{2,1,0:T(8,128)S(1)} %join1.1), channel_id=1, source_target_pairs={{0,64},{4,68},{8,72},{12,76},{16,80},{20,84},{24,88},{28,92},{32,9... | collective-permute-start | bytes 983048 | tf_op jit(solution)/shard_map/ppermute | solution.py:37
  187.9 17.3 %collective-permute-start.39 = (f32[8,64,128]{2,1,0:T(8,128)S(1)}, f32[8,64,128]{2,1,0:T(8,128)S(1)}, u32[]{:S(2)}, u32[]{:S(2)}) collective-permute-start(f32[8,64,128]{2,1,0:T(8,128)S(1)} %get-tuple-element.197), channel_id=1, source_target_pairs={{0,48},{1,13},{2,50},{3,15},{4,52},{5,1},{6,54},{7,3},{8,56},{9,5}... | collective-permute-start | bytes 786440 | tf_op jit(solution)/shard_map/ppermute | solution.py:33
  188.6 16.7 %collective-permute-start.40 = (f32[8,64,128]{2,1,0:T(8,128)S(1)}, f32[8,64,128]{2,1,0:T(8,128)S(1)}, u32[]{:S(2)}, u32[]{:S(2)}) collective-permute-start(f32[8,64,128]{2,1,0:T(8,128)S(1)} %get-tuple-element.198), channel_id=1, source_target_pairs={{0,32},{1,9},{2,34},{3,11},{4,36},{5,13},{6,38},{7,15},{8,40},{9,1... | collective-permute-start | bytes 786440 | tf_op jit(solution)/shard_map/ppermute | solution.py:33
  (20 other events, 246.8 us)

commit v3 on v2

--- a/solution.py
+++ b/solution.py
@@ -9,7 +9,7 @@
 
 SIDE = 4
 RB = 8
-GROUP = 8
+GROUP = 16
 CUTS = 4
 PER = SIDE * SIDE * 2
 F32 = jnp.float32
@@ -101,74 +101,43 @@
 def pack_kernel(pick, *refs):
     n = SIDE * len(SPANS)
     ins, outs = refs[:n], refs[n : n + SIDE]
-    held, built, in_sems, out_sems = refs[n + SIDE :]
-    spots = [held.at[near, pl.ds(*span)] for span in SPANS for near in range(SIDE)]
-    wait(fetch(ins, spots, in_sems))
-    copies = []
-    for far in (2, 3, 1, 0):
+    for far in range(SIDE):
         for near in range(SIDE):
             for k in range(SIDE):
+                source, base = ins[min(k, 2) * SIDE + near], RB * (k == 3)
                 for p in range(2):
                     at = (near * SIDE + k) * 2 + p
-                    built[far, at] = held[near, k * RB + pick[far * PER + at]]
-        copy = pltpu.make_async_copy(built.at[far], outs[far], out_sems.at[far])
-        copy.start()
-        copies.append(copy)
-    wait(copies)
+                    outs[far][at] = source[base + pick[far * PER + at]]
 
 
 def unpack_kernel(pick, *refs):
-    n = SIDE * len(SPANS)
-    ins, outs = refs[:SIDE], refs[SIDE : SIDE + n]
-    held, built, in_sems, out_sems = refs[SIDE + n :]
-    loads = fetch(ins, [held.at[i] for i in range(SIDE)], in_sems)
-    built[...] = jnp.zeros_like(built)
-    wait(loads)
-    tail = (held[0, PER:] + held[1, PER:]) + (held[2, PER:] + held[3, PER:])
-    copies = []
-    for part in (2, 1, 0):
-        start, size = SPANS[part]
-        for near in (1, 2, 3, 0):
-            for k in range(start // RB, (start + size) // RB):
-                for far in range(SIDE):
-                    for p in range(2):
-                        at = (near * SIDE + k) * 2 + p
-                        built[near, k * RB + pick[far * PER + at]] += held[far, at]
-            if part == 2:
-                built[near, PER:] = tail
-            message = part * SIDE + near
-            copy = pltpu.make_async_copy(
-                built.at[near, pl.ds(start, size + 2 * (part == 2))],
-                outs[message],
-                out_sems.at[message],
-            )
-            copy.start()
-            copies.append(copy)
-    wait(copies)
+    ins, outs = refs[:SIDE], refs[SIDE:]
+    for out in outs:
+        out[...] = jnp.zeros_like(out)
+    tail = (ins[0][PER:] + ins[1][PER:]) + (ins[2][PER:] + ins[3][PER:])
+    for near in range(SIDE):
+        outs[2 * SIDE + near][2 * RB :] = tail
+        for k in range(SIDE):
+            target, base = outs[min(k, 2) * SIDE + near], RB * (k == 3)
+            if k == 0 and near == 2:
+                target, base = outs[SIDE + near], RB
+            for far in range(SIDE):
+                for p in range(2):
+                    at = (near * SIDE + k) * 2 + p
+                    target[base + pick[far * PER + at]] += ins[far][at]
 
 
 def join_kernel(count, *refs):
     n = SIDE if count == 2 else SIDE + 1
-    ins, outs = refs[:n], refs[n : n + count]
-    held, built, in_sems, out_sems = refs[n + count :]
-    targets = [held.at[i] for i in range(SIDE)]
-    if count == 1:
-        ins = ins[:SIDE] + (ins[SIDE].at[pl.ds(RB, 2)],)
-        targets.append(built.at[0, pl.ds(RB, 2)])
-    wait(fetch(ins, targets, in_sems))
-    copies = []
-    for k in range(count):
+    ins, outs = refs[:n], refs[n:]
+    for k, out in enumerate(outs):
         spans = [(pl.ds(0, RB), pl.ds(k * RB, RB))]
         if count == 2:
             spans.append((pl.ds(RB, 2), pl.ds(2 * RB, 2)))
+        else:
+            out[RB:] = ins[SIDE][RB:]
         for target, source in spans:
-            built[k, target] = (held[0, source] + held[1, source]) + (
-                held[2, source] + held[3, source]
-            )
-        copy = pltpu.make_async_copy(built.at[k], outs[k], out_sems.at[k])
-        copy.start()
-        copies.append(copy)
-    wait(copies)
+            out[target] = (ins[0][source] + ins[1][source]) + (ins[2][source] + ins[3][source])
 
 
 def run_groups(group, count, span, tile_loads):
@@ -362,7 +331,11 @@
 
     shape = (PER, width, size)
     longer = (PER + 2, width, size)
-    lengths = [size + 2 * (i == 2) for i, (_, size) in enumerate(SPANS)]
+    lengths = [
+        size + 2 * (part == 2) + RB * (part == 1 and near == 2)
+        for part, (_, size) in enumerate(SPANS)
+        for near in range(SIDE)
+    ]
 
     def spread(value):
         return [value] + [shift(value, d, 0) for d in (1, 2, 3)]
@@ -376,14 +349,9 @@
             functools.partial(join_kernel, count),
             "join%d" % count,
             [struct(RB + 2, width, size)] * count,
-            [HBM] * (SIDE + len(more)),
-            [HBM] * count,
-            [
-                pltpu.VMEM((SIDE,) + arrived[0].shape, F32),
-                pltpu.VMEM((count, RB + 2, width, size), F32),
-                DMA((SIDE + 1,)),
-                DMA((count,)),
-            ],
+            [VMEM] * (SIDE + len(more)),
+            [VMEM] * count,
+            [],
         )(*arrived, *more)
 
     scaled = features_t * root
@@ -399,7 +367,8 @@
         nbytes=12 << 20,
     )(tiles)
     cot = [piece(cotangent_t, d) for d in range(4)]
-    own_part = spread(blocked)
+    later, pick = lax.optimization_barrier((blocked, pick))
+    own_part = spread(later)
     next_part = spread(deep[1])
     own_part, next_part, far_deep, adjacency, pick, cot = lax.optimization_barrier(
         (own_part, next_part, deep[2:], adjacency, pick, cot)
@@ -409,14 +378,9 @@
         pack_kernel,
         "pack",
         [struct(*shape)] * SIDE,
-        [SMEM] + [HBM] * (3 * SIDE),
-        [HBM] * SIDE,
-        [
-            pltpu.VMEM((SIDE,) + shape, F32),
-            pltpu.VMEM((SIDE,) + shape, F32),
-            DMA((3 * SIDE,)),
-            DMA((SIDE,)),
-        ],
+        [SMEM] + [VMEM] * (3 * SIDE),
+        [VMEM] * SIDE,
+        [],
         nbytes=8 << 20,
     )(pick, *own_part, *next_part, *far_part)
     cot, packed = lax.optimization_barrier((cot, packed))
@@ -474,15 +438,10 @@
     summed = call(
         unpack_kernel,
         "unpack",
-        [struct(length, width, size) for length in lengths for _ in range(SIDE)],
-        [SMEM] + [HBM] * SIDE,
-        [HBM] * (3 * SIDE),
-        [
-            pltpu.VMEM((SIDE,) + longer, F32),
-            pltpu.VMEM((SIDE,) + longer, F32),
-            DMA((SIDE,)),
-            DMA((3 * SIDE,)),
-        ],
+        [struct(length, width, size) for length in lengths],
+        [SMEM] + [VMEM] * SIDE,
+        [VMEM] * (3 * SIDE),
+        [],
         nbytes=8 << 20,
     )(pick, *home)
     own_part, next_part, far_part = summed[:SIDE], summed[SIDE : 2 * SIDE], summed[2 * SIDE :]
@@ -490,7 +449,9 @@
     far_ends = join(far_part)
     next_part, own_part = lax.optimization_barrier((route(next_part), own_part))
     next_end = join(next_part, far_ends[0])[0]
-    own_part = route(own_part)
+    own_part = [
+        own_part[0], shift(own_part[1], -1, 0), next_part[2][RB:], shift(own_part[3], -3, 0)
+    ]
     ends = [swap_z(next_end, 1), swap_z(far_ends[0], 2), swap_z(far_ends[1], 3)]
     total = (ends[0][:RB] + ends[1][:RB]) + ends[2][:RB]
     total += (own_part[0] + own_part[1]) + (own_part[2] + own_part[3])

time: 212 us -> 204 us (0.962)
  Pallas kernels: 16.2 us -> 12.3 us
  starting transfers between devices: 83.1 us -> 79.3 us
  waiting for transfers between devices: 97 us -> 99.3 us
    ppermute x24 -> x23, starting transfers between devices: 37.9 us -> 32.5 us  [shift(): return lax.ppermute(value, ('row', 'col'), pairs)]
    ppermute x6, waiting for transfers between devices: 13.3 us -> 18.5 us  [swap_z(): lax.ppermute(value, 'row', [(r, r ^ k * SIDE * SIDE) for r in range(SIDE...]
    ppermute x12, waiting for transfers between devices: 30.2 us -> 27.2 us  [swap_col(): return lax.ppermute(value, 'col', [(c, c ^ k) for c in range(4)])]
    unnamed x22 -> x24, local copies, waits for them, and re-layouts: 7.48 us -> 7 us
    ppermute x24 -> x23, waiting for transfers between devices: 53.4 us -> 53.6 us  [shift(): return lax.ppermute(value, ('row', 'col'), pairs)]
  transfers between devices with their start and end apart: 42 -> 41, of which waited for: 21 -> 22; matrix products, arithmetic and copies ran while one was open for 2% -> 0% of each run, Pallas kernels for 1% -> 1%
where the time goes in v3:
time: 204 us; the launch traced here: 203 us
  waiting for transfers between devices  99.3 us (49%)
  starting transfers between devices  79.3 us (39%)
  Pallas kernels  12.3 us (6%)
  local copies, waits for them, and re-layouts  8.23 us (4%)
    ppermute x23, waiting for transfers between devices, shift(): return lax.ppermute(value, ('row', 'col'), pairs)  53.6 us
    ppermute x23, starting transfers between devices, shift(): return lax.ppermute(value, ('row', 'col'), pairs)  32.5 us
    ppermute x12, waiting for transfers between devices, swap_col(): return lax.ppermute(value, 'col', [(c, c ^ k) for c in range(4)])  27.2 us
    ppermute x12, starting transfers between devices, swap_col(): return lax.ppermute(value, 'col', [(c, c ^ k) for c in range(4)])  25.7 us
    ppermute x6, starting transfers between devices, swap_z(): lax.ppermute(value, 'row', [(r, r ^ k * SIDE * SIDE) for r in range(SIDE...  21.2 us
    ppermute x6, waiting for transfers between devices, swap_z(): lax.ppermute(value, 'row', [(r, r ^ k * SIDE * SIDE) for r in range(SIDE...  18.5 us
    unnamed x24, local copies, waits for them, and re-layouts  7 us
  transfers between devices with their start and end apart: 41, of which 22 were waited for; matrix products, arithmetic and copies ran while one was open for 0% of the time, Pallas kernels for 1%

profile of v3, /device:TPU:8, one launch (start us, length us, event | category | flops | bytes accessed | tf_op | source)
XLA Modules:
  0.0 202.7 jit_solution(13323636950051336900)
XLA Ops:
  7.3 2.7 %collective-permute-start.1 = (f32[8,64,128]{2,1,0:T(8,128)S(1)}, f32[8,64,128]{2,1,0:T(8,128)S(1)}, u32[]{:S(2)}, u32[]{:S(2)}) collective-permute-start(f32[8,64,128]{2,1,0:T(8,128)S(1)} %bitcast.47), channel_id=1, source_target_pairs={{0,32},{1,9},{2,34},{3,11},{4,36},{5,13},{6,38},{7,15},{8,40},{9,1... | collective-permute-start | bytes 786440 | tf_op jit(solution)/shard_map/ppermute | solution.py:33
  11.4 3.3 %collective-permute-start.7 = (f32[8,64,128]{2,1,0:T(8,128)S(1)}, f32[8,64,128]{2,1,0:T(8,128)S(1)}, u32[]{:S(2)}, u32[]{:S(2)}) collective-permute-start(f32[8,64,128]{2,1,0:T(8,128)S(1)} %bitcast.49), channel_id=1, source_target_pairs={{0,128},{4,132},{8,136},{12,140},{16,144},{20,148},{24,152},{28,15... | collective-permute-start | bytes 786440 | tf_op jit(solution)/shard_map/ppermute | solution.py:37
  16.4 2.7 %collective-permute-start.5 = (f32[8,64,128]{2,1,0:T(8,128)S(1)}, f32[8,64,128]{2,1,0:T(8,128)S(1)}, u32[]{:S(2)}, u32[]{:S(2)}) collective-permute-start(f32[8,64,128]{2,1,0:T(8,128)S(1)} %collective-permute-done.3.refs_4_), channel_id=1, source_target_pairs={{0,32},{1,9},{2,34},{3,11},{4,36},{5,13},{6,38},{7,15},{8,40},{9,1... | collective-permute-start | bytes 786440 | tf_op jit(solution)/shard_map/ppermute | solution.py:33
  20.5 3.4 %copy-done.2 = s32[128,128,128]{2,1,0:T(8,128)S(1)} copy-done((s32[128,128,128]{2,1,0:T(8,128)S(1)}, s32[128,128,128]{2,1,0:T(8,128)}, u32[]{:S(2)}) %copy-start.2) | copy-done | bytes 8388632
  27.7 4.8 %collective-permute-done.7 = f32[8,64,128]{2,1,0:T(8,128)S(1)} collective-permute-done((f32[8,64,128]{2,1,0:T(8,128)S(1)}, f32[8,64,128]{2,1,0:T(8,128)S(1)}, u32[]{:S(2)}, u32[]{:S(2)}) %collective-permute-start.7) | collective-permute-done | bytes 262176 | tf_op jit(solution)/shard_map/ppermute | solution.py:37
  33.8 2.6 %collective-permute-start.11 = (f32[16,64,128]{2,1,0:T(8,128)S(1)}, f32[16,64,128]{2,1,0:T(8,128)S(1)}, u32[]{:S(2)}, u32[]{:S(2)}) collective-permute-start(f32[16,64,128]{2,1,0:T(8,128)S(1)} %constant_dynamic-update-slice_fusion.refs_8_), channel_id=1, source_target_pairs={{0,48},{1,13},{2,50},{3,15},{4,52},{5,1},{6,54},{7,3},{8,56},{9,5}... | collective-permute-start | bytes 1572872 | tf_op jit(solution)/shard_map/ppermute | solution.py:33
  36.4 7.1 %collective-permute-done.10.refs_10_ = f32[16,64,128]{2,1,0:T(8,128)S(1)} collective-permute-done((f32[16,64,128]{2,1,0:T(8,128)S(1)}, f32[16,64,128]{2,1,0:T(8,128)S(1)}, u32[]{:S(2)}, u32[]{:S(2)}) %collective-permute-start.10) | collective-permute-done | bytes 524320 | tf_op jit(solution)/shard_map/ppermute | solution.py:33
  43.5 3.4 %collective-permute-done.11.refs_11_ = f32[16,64,128]{2,1,0:T(8,128)S(1)} collective-permute-done((f32[16,64,128]{2,1,0:T(8,128)S(1)}, f32[16,64,128]{2,1,0:T(8,128)S(1)}, u32[]{:S(2)}, u32[]{:S(2)}) %collective-permute-start.11) | collective-permute-done | bytes 524320 | tf_op jit(solution)/shard_map/ppermute | solution.py:33
  46.9 2.1 %collective-permute-done.9.refs_9_ = f32[16,64,128]{2,1,0:T(8,128)S(1)} collective-permute-done((f32[16,64,128]{2,1,0:T(8,128)S(1)}, f32[16,64,128]{2,1,0:T(8,128)S(1)}, u32[]{:S(2)}, u32[]{:S(2)}) %collective-permute-start.9) | collective-permute-done | bytes 524320 | tf_op jit(solution)/shard_map/ppermute | solution.py:33
  54.6 5.7 %collective-permute-start.16 = (f32[64,256]{1,0:T(8,128)S(1)}, f32[64,256]{1,0:T(8,128)S(1)}, u32[]{:S(2)}, u32[]{:S(2)}) collective-permute-start(f32[64,256]{1,0:T(8,128)S(1)} %get-tuple-element.130), channel_id=1, source_target_pairs={{0,2},{1,3},{2,0},{3,1},{4,6},{5,7},{6,4},{7,5},{8,10},{9,11},{10,... | collective-permute-start | bytes 196616 | tf_op jit(solution)/shard_map/ppermute | solution.py:41
  63.0 5.4 %collective-permute-done.17.c3 = f32[64,256]{1,0:T(8,128)S(1)} collective-permute-done((f32[64,256]{1,0:T(8,128)S(1)}, f32[64,256]{1,0:T(8,128)S(1)}, u32[]{:S(2)}, u32[]{:S(2)}) %collective-permute-start.17) | collective-permute-done | bytes 65568 | tf_op jit(solution)/shard_map/ppermute | solution.py:41
  68.4 10.0 %collective-permute-done.14.q3 = f32[32,64,128]{2,1,0:T(8,128)S(1)} collective-permute-done((f32[32,64,128]{2,1,0:T(8,128)S(1)}, f32[32,64,128]{2,1,0:T(8,128)S(1)}, u32[]{:S(2)}, u32[]{:S(2)}) %collective-permute-start.14) | collective-permute-done | bytes 1048608 | tf_op jit(solution)/shard_map/ppermute | solution.py:33
  78.5 3.2 %forward.1 = (f32[64,256]{1,0:T(8,128)S(1)}, f32[64,256]{1,0:T(8,128)S(1)}, f32[64,256]{1,0:T(8,128)S(1)}, f32[64,256]{1,0:T(8,128)S(1)}) custom-call(s32[128]{0:T(128)S(1)} %compare_select_fusion.12.rows, s32[128]{0:T(128)S(1)} %get-tuple-element.202.at, s32[2]{0:T(128)S(1)} %pad_add_fusion.info, f32[64,1024]{1,0:T(8,128)S(1)} %get-tuple-element.204.scaled, ...), custom_call_target="tpu_custom_call" | custom-call | bytes 16777216 | tf_op jit(solution)/shard_map/forward/pallas_call | solution.py:390
  81.8 5.3 %collective-permute-start.19 = (f32[64,256]{1,0:T(8,128)S(1)}, f32[64,256]{1,0:T(8,128)S(1)}, u32[]{:S(2)}, u32[]{:S(2)}) collective-permute-start(f32[64,256]{1,0:T(8,128)S(1)} %get-tuple-element.138), channel_id=1, source_target_pairs={{0,2},{1,3},{2,0},{3,1},{4,6},{5,7},{6,4},{7,5},{8,10},{9,11},{10,... | collective-permute-start | bytes 196616 | tf_op jit(solution)/shard_map/ppermute | solution.py:41
  87.6 2.6 %collective-permute-done.19.a2 = f32[64,256]{1,0:T(8,128)S(1)} collective-permute-done((f32[64,256]{1,0:T(8,128)S(1)}, f32[64,256]{1,0:T(8,128)S(1)}, u32[]{:S(2)}, u32[]{:S(2)}) %collective-permute-start.19) | collective-permute-done | bytes 65568 | tf_op jit(solution)/shard_map/ppermute | solution.py:41
  90.2 4.8 %collective-permute-done.20.a3 = f32[64,256]{1,0:T(8,128)S(1)} collective-permute-done((f32[64,256]{1,0:T(8,128)S(1)}, f32[64,256]{1,0:T(8,128)S(1)}, u32[]{:S(2)}, u32[]{:S(2)}) %collective-permute-start.20) | collective-permute-done | bytes 65568 | tf_op jit(solution)/shard_map/ppermute | solution.py:41
  99.5 4.0 %collective-permute-start.23 = (f32[128,256]{1,0:T(8,128)S(1)}, f32[128,256]{1,0:T(8,128)S(1)}, u32[]{:S(2)}, u32[]{:S(2)}) collective-permute-start(f32[128,256]{1,0:T(8,128)S(1)} %get-tuple-element.147), channel_id=1, source_target_pairs={{0,3},{1,2},{2,1},{3,0},{4,7},{5,6},{6,5},{7,4},{8,11},{9,10},{10,... | collective-permute-start | bytes 393224 | tf_op jit(solution)/shard_map/ppermute | solution.py:41
  103.5 5.0 %collective-permute-done.22.i2 = f32[128,256]{1,0:T(8,128)S(1)} collective-permute-done((f32[128,256]{1,0:T(8,128)S(1)}, f32[128,256]{1,0:T(8,128)S(1)}, u32[]{:S(2)}, u32[]{:S(2)}) %collective-permute-start.22) | collective-permute-done | bytes 131104 | tf_op jit(solution)/shard_map/ppermute | solution.py:41
  108.5 3.1 %collective-permute-done.23.i3 = f32[128,256]{1,0:T(8,128)S(1)} collective-permute-done((f32[128,256]{1,0:T(8,128)S(1)}, f32[128,256]{1,0:T(8,128)S(1)}, u32[]{:S(2)}, u32[]{:S(2)}) %collective-permute-start.23) | collective-permute-done | bytes 131104 | tf_op jit(solution)/shard_map/ppermute | solution.py:41
  111.6 3.1 %backward.1 = (f32[64,1024]{1,0:T(8,128)S(1)}, f32[34,64,128]{2,1,0:T(8,128)S(1)}, f32[34,64,128]{2,1,0:T(8,128)S(1)}, f32[34,64,128]{2,1,0:T(8,128)S(1)}, f32[34,64,128]{2,1,0:T(8,128)S(1)}) custom-call(s32[128]{0:T(128)S(1)} %copy-done.4, s32[128]{0:T(128)S(1)} %get-tuple-element.201.at, s32[2]{0:T(128)S(1)} %pad_add_fusion.info, f32[1,1024]{1,0:T(1,128)S(1)} %bitcast.53, ...), custom_call_target="tpu_custom_call" | custom-call | bytes 16777216 | tf_op jit(solution)/shard_map/backward/pallas_call | solution.py:416
  115.9 3.5 %collective-permute-start.25 = (f32[34,64,128]{2,1,0:T(8,128)S(1)}, f32[34,64,128]{2,1,0:T(8,128)S(1)}, u32[]{:S(2)}, u32[]{:S(2)}) collective-permute-start(f32[34,64,128]{2,1,0:T(8,128)S(1)} %get-tuple-element.158), channel_id=1, source_target_pairs={{0,8},{1,33},{2,10},{3,35},{4,12},{5,37},{6,14},{7,39},{8,0},{9,41... | collective-permute-start | bytes 3342344 | tf_op jit(solution)/shard_map/ppermute | solution.py:33
  119.4 2.5 %collective-permute-start.26 = (f32[34,64,128]{2,1,0:T(8,128)S(1)}, f32[34,64,128]{2,1,0:T(8,128)S(1)}, u32[]{:S(2)}, u32[]{:S(2)}) collective-permute-start(f32[34,64,128]{2,1,0:T(8,128)S(1)} %get-tuple-element.159), channel_id=1, source_target_pairs={{0,4},{1,17},{2,6},{3,19},{4,8},{5,21},{6,10},{7,23},{8,12},{9,25}... | collective-permute-start | bytes 3342344 | tf_op jit(solution)/shard_map/ppermute | solution.py:33
  121.9 2.2 %collective-permute-start.28 = (f32[64,256]{1,0:T(8,128)S(1)}, f32[64,256]{1,0:T(8,128)S(1)}, u32[]{:S(2)}, u32[]{:S(2)}) collective-permute-start(f32[64,256]{1,0:T(8,128)S(1)} %get-tuple-element.162), channel_id=1, source_target_pairs={{0,2},{1,3},{2,0},{3,1},{4,6},{5,7},{6,4},{7,5},{8,10},{9,11},{10,... | collective-permute-start | bytes 196616 | tf_op jit(solution)/shard_map/ppermute | solution.py:41
  124.2 3.5 %collective-permute-start.29 = (f32[64,256]{1,0:T(8,128)S(1)}, f32[64,256]{1,0:T(8,128)S(1)}, u32[]{:S(2)}, u32[]{:S(2)}) collective-permute-start(f32[64,256]{1,0:T(8,128)S(1)} %get-tuple-element.163), channel_id=1, source_target_pairs={{0,3},{1,2},{2,1},{3,0},{4,7},{5,6},{6,5},{7,4},{8,11},{9,10},{10,... | collective-permute-start | bytes 196616 | tf_op jit(solution)/shard_map/ppermute | solution.py:41
  127.7 2.6 %collective-permute-done.28 = f32[64,256]{1,0:T(8,128)S(1)} collective-permute-done((f32[64,256]{1,0:T(8,128)S(1)}, f32[64,256]{1,0:T(8,128)S(1)}, u32[]{:S(2)}, u32[]{:S(2)}) %collective-permute-start.28) | collective-permute-done | bytes 65568 | tf_op jit(solution)/shard_map/ppermute | solution.py:41
  132.1 12.6 %collective-permute-done.25.refs_2_ = f32[34,64,128]{2,1,0:T(8,128)S(1)} collective-permute-done((f32[34,64,128]{2,1,0:T(8,128)S(1)}, f32[34,64,128]{2,1,0:T(8,128)S(1)}, u32[]{:S(2)}, u32[]{:S(2)}) %collective-permute-start.25) | collective-permute-done | bytes 1114144 | tf_op jit(solution)/shard_map/ppermute | solution.py:33
  149.9 7.9 %collective-permute-done.30.refs_1_ = f32[18,64,128]{2,1,0:T(8,128)S(1)} collective-permute-done((f32[18,64,128]{2,1,0:T(8,128)S(1)}, f32[18,64,128]{2,1,0:T(8,128)S(1)}, u32[]{:S(2)}, u32[]{:S(2)}) %collective-permute-start.30) | collective-permute-done | bytes 589856 | tf_op jit(solution)/shard_map/ppermute | solution.py:33
  159.4 6.2 %collective-permute-done.32.refs_3_ = f32[18,64,128]{2,1,0:T(8,128)S(1)} collective-permute-done((f32[18,64,128]{2,1,0:T(8,128)S(1)}, f32[18,64,128]{2,1,0:T(8,128)S(1)}, u32[]{:S(2)}, u32[]{:S(2)}) %collective-permute-start.32) | collective-permute-done | bytes 589856 | tf_op jit(solution)/shard_map/ppermute | solution.py:33
  169.2 6.7 %collective-permute-start.37 = (f32[10,64,128]{2,1,0:T(8,128)S(1)}, f32[10,64,128]{2,1,0:T(8,128)S(1)}, u32[]{:S(2)}, u32[]{:S(2)}) collective-permute-start(f32[10,64,128]{2,1,0:T(8,128)S(1)} %get-tuple-element.195.refs_4_), channel_id=1, source_target_pairs={{0,128},{4,132},{8,136},{12,140},{16,144},{20,148},{24,152},{28,15... | collective-permute-start | bytes 983048 | tf_op jit(solution)/shard_map/ppermute | solution.py:37
  179.2 6.3 %collective-permute-start.36 = (f32[10,64,128]{2,1,0:T(8,128)S(1)}, f32[10,64,128]{2,1,0:T(8,128)S(1)}, u32[]{:S(2)}, u32[]{:S(2)}) collective-permute-start(f32[10,64,128]{2,1,0:T(8,128)S(1)} %join1.1), channel_id=1, source_target_pairs={{0,64},{4,68},{8,72},{12,76},{16,80},{20,84},{24,88},{28,92},{32,9... | collective-permute-start | bytes 983048 | tf_op jit(solution)/shard_map/ppermute | solution.py:37
  187.6 9.5 %collective-permute-done.37 = f32[10,64,128]{2,1,0:T(8,128)S(1)} collective-permute-done((f32[10,64,128]{2,1,0:T(8,128)S(1)}, f32[10,64,128]{2,1,0:T(8,128)S(1)}, u32[]{:S(2)}, u32[]{:S(2)}) %collective-permute-start.37) | collective-permute-done | bytes 327712 | tf_op jit(solution)/shard_map/ppermute | solution.py:37
  197.1 4.2 %collective-permute-done.36 = f32[10,64,128]{2,1,0:T(8,128)S(1)} collective-permute-done((f32[10,64,128]{2,1,0:T(8,128)S(1)}, f32[10,64,128]{2,1,0:T(8,128)S(1)}, u32[]{:S(2)}, u32[]{:S(2)}) %collective-permute-start.36) | collective-permute-done | bytes 327712 | tf_op jit(solution)/shard_map/ppermute | solution.py:37
  (105 shorter events, 48.7 us)
Async XLA Ops:
  3.8 10.9 %collective-permute-start = (f32[8,64,128]{2,1,0:T(8,128)S(1)}, f32[8,64,128]{2,1,0:T(8,128)S(1)}, u32[]{:S(2)}, u32[]{:S(2)}) collective-permute-start(f32[8,64,128]{2,1,0:T(8,128)S(1)} %bitcast.45), channel_id=1, source_target_pairs={{0,16},{1,5},{2,18},{3,7},{4,20},{5,9},{6,22},{7,11},{8,24},{9,13}... | collective-permute-start | bytes 786440 | tf_op jit(solution)/shard_map/ppermute | solution.py:33
  5.4 10.7 %collective-permute-start.3 = (f32[8,64,128]{2,1,0:T(8,128)S(1)}, f32[8,64,128]{2,1,0:T(8,128)S(1)}, u32[]{:S(2)}, u32[]{:S(2)}) collective-permute-start(f32[8,64,128]{2,1,0:T(8,128)S(1)} %bitcast.46), channel_id=1, source_target_pairs={{0,64},{4,68},{8,72},{12,76},{16,80},{20,84},{24,88},{28,92},{32,9... | collective-permute-start | bytes 786440 | tf_op jit(solution)/shard_map/ppermute | solution.py:37
  7.3 9.1 %collective-permute-start.1 = (f32[8,64,128]{2,1,0:T(8,128)S(1)}, f32[8,64,128]{2,1,0:T(8,128)S(1)}, u32[]{:S(2)}, u32[]{:S(2)}) collective-permute-start(f32[8,64,128]{2,1,0:T(8,128)S(1)} %bitcast.47), channel_id=1, source_target_pairs={{0,32},{1,9},{2,34},{3,11},{4,36},{5,13},{6,38},{7,15},{8,40},{9,1... | collective-permute-start | bytes 786440 | tf_op jit(solution)/shard_map/ppermute | solution.py:33
  10.0 9.1 %collective-permute-start.2 = (f32[8,64,128]{2,1,0:T(8,128)S(1)}, f32[8,64,128]{2,1,0:T(8,128)S(1)}, u32[]{:S(2)}, u32[]{:S(2)}) collective-permute-start(f32[8,64,128]{2,1,0:T(8,128)S(1)} %bitcast.48), channel_id=1, source_target_pairs={{0,48},{1,13},{2,50},{3,15},{4,52},{5,1},{6,54},{7,3},{8,56},{9,5}... | collective-permute-start | bytes 786440 | tf_op jit(solution)/shard_map/ppermute | solution.py:33
  11.4 21.1 %collective-permute-start.7 = (f32[8,64,128]{2,1,0:T(8,128)S(1)}, f32[8,64,128]{2,1,0:T(8,128)S(1)}, u32[]{:S(2)}, u32[]{:S(2)}) collective-permute-start(f32[8,64,128]{2,1,0:T(8,128)S(1)} %bitcast.49), channel_id=1, source_target_pairs={{0,128},{4,132},{8,136},{12,140},{16,144},{20,148},{24,152},{28,15... | collective-permute-start | bytes 786440 | tf_op jit(solution)/shard_map/ppermute | solution.py:37
  14.7 17.8 %collective-permute-start.8 = (f32[8,64,128]{2,1,0:T(8,128)S(1)}, f32[8,64,128]{2,1,0:T(8,128)S(1)}, u32[]{:S(2)}, u32[]{:S(2)}) collective-permute-start(f32[8,64,128]{2,1,0:T(8,128)S(1)} %bitcast.50), channel_id=1, source_target_pairs={{0,192},{4,196},{8,200},{12,204},{16,208},{20,212},{24,216},{28,22... | collective-permute-start | bytes 786440 | tf_op jit(solution)/shard_map/ppermute | solution.py:37
  16.1 16.4 %collective-permute-start.4 = (f32[8,64,128]{2,1,0:T(8,128)S(1)}, f32[8,64,128]{2,1,0:T(8,128)S(1)}, u32[]{:S(2)}, u32[]{:S(2)}) collective-permute-start(f32[8,64,128]{2,1,0:T(8,128)S(1)} %collective-permute-done.3.refs_4_), channel_id=1, source_target_pairs={{0,16},{1,5},{2,18},{3,7},{4,20},{5,9},{6,22},{7,11},{8,24},{9,13}... | collective-permute-start | bytes 786440 | tf_op jit(solution)/shard_map/ppermute | solution.py:33
  16.4 16.1 %collective-permute-start.5 = (f32[8,64,128]{2,1,0:T(8,128)S(1)}, f32[8,64,128]{2,1,0:T(8,128)S(1)}, u32[]{:S(2)}, u32[]{:S(2)}) collective-permute-start(f32[8,64,128]{2,1,0:T(8,128)S(1)} %collective-permute-done.3.refs_4_), channel_id=1, source_target_pairs={{0,32},{1,9},{2,34},{3,11},{4,36},{5,13},{6,38},{7,15},{8,40},{9,1... | collective-permute-start | bytes 786440 | tf_op jit(solution)/shard_map/ppermute | solution.py:33
  19.1 13.4 %collective-permute-start.6 = (f32[8,64,128]{2,1,0:T(8,128)S(1)}, f32[8,64,128]{2,1,0:T(8,128)S(1)}, u32[]{:S(2)}, u32[]{:S(2)}) collective-permute-start(f32[8,64,128]{2,1,0:T(8,128)S(1)} %collective-permute-done.3.refs_4_), channel_id=1, source_target_pairs={{0,48},{1,13},{2,50},{3,15},{4,52},{5,1},{6,54},{7,3},{8,56},{9,5}... | collective-permute-start | bytes 786440 | tf_op jit(solution)/shard_map/ppermute | solution.py:33
  32.6 10.9 %collective-permute-start.10 = (f32[16,64,128]{2,1,0:T(8,128)S(1)}, f32[16,64,128]{2,1,0:T(8,128)S(1)}, u32[]{:S(2)}, u32[]{:S(2)}) collective-permute-start(f32[16,64,128]{2,1,0:T(8,128)S(1)} %constant_dynamic-update-slice_fusion.refs_8_), channel_id=1, source_target_pairs={{0,32},{1,9},{2,34},{3,11},{4,36},{5,13},{6,38},{7,15},{8,40},{9,1... | collective-permute-start | bytes 1572872 | tf_op jit(solution)/shard_map/ppermute | solution.py:33
  33.8 13.1 %collective-permute-start.11 = (f32[16,64,128]{2,1,0:T(8,128)S(1)}, f32[16,64,128]{2,1,0:T(8,128)S(1)}, u32[]{:S(2)}, u32[]{:S(2)}) collective-permute-start(f32[16,64,128]{2,1,0:T(8,128)S(1)} %constant_dynamic-update-slice_fusion.refs_8_), channel_id=1, source_target_pairs={{0,48},{1,13},{2,50},{3,15},{4,52},{5,1},{6,54},{7,3},{8,56},{9,5}... | collective-permute-start | bytes 1572872 | tf_op jit(solution)/shard_map/ppermute | solution.py:33
  36.4 12.6 %collective-permute-start.9 = (f32[16,64,128]{2,1,0:T(8,128)S(1)}, f32[16,64,128]{2,1,0:T(8,128)S(1)}, u32[]{:S(2)}, u32[]{:S(2)}) collective-permute-start(f32[16,64,128]{2,1,0:T(8,128)S(1)} %constant_dynamic-update-slice_fusion.refs_8_), channel_id=1, source_target_pairs={{0,16},{1,5},{2,18},{3,7},{4,20},{5,9},{6,22},{7,11},{8,24},{9,13}... | collective-permute-start | bytes 1572872 | tf_op jit(solution)/shard_map/ppermute | solution.py:33
  49.8 18.6 %collective-permute-start.12 = (f32[32,64,128]{2,1,0:T(8,128)S(1)}, f32[32,64,128]{2,1,0:T(8,128)S(1)}, u32[]{:S(2)}, u32[]{:S(2)}) collective-permute-start(f32[32,64,128]{2,1,0:T(8,128)S(1)} %get-tuple-element.125), channel_id=1, source_target_pairs={{0,4},{1,17},{2,6},{3,19},{4,8},{5,21},{6,10},{7,23},{8,12},{9,25}... | collective-permute-start | bytes 3145736 | tf_op jit(solution)/shard_map/ppermute | solution.py:33
  51.0 17.5 %collective-permute-start.13 = (f32[32,64,128]{2,1,0:T(8,128)S(1)}, f32[32,64,128]{2,1,0:T(8,128)S(1)}, u32[]{:S(2)}, u32[]{:S(2)}) collective-permute-start(f32[32,64,128]{2,1,0:T(8,128)S(1)} %get-tuple-element.126), channel_id=1, source_target_pairs={{0,8},{1,33},{2,10},{3,35},{4,12},{5,37},{6,14},{7,39},{8,0},{9,41... | collective-permute-start | bytes 3145736 | tf_op jit(solution)/shard_map/ppermute | solution.py:33
  52.4 26.0 %collective-permute-start.14 = (f32[32,64,128]{2,1,0:T(8,128)S(1)}, f32[32,64,128]{2,1,0:T(8,128)S(1)}, u32[]{:S(2)}, u32[]{:S(2)}) collective-permute-start(f32[32,64,128]{2,1,0:T(8,128)S(1)} %get-tuple-element.127), channel_id=1, source_target_pairs={{0,12},{1,49},{2,14},{3,51},{4,0},{5,53},{6,2},{7,55},{8,4},{9,57}... | collective-permute-start | bytes 3145736 | tf_op jit(solution)/shard_map/ppermute | solution.py:33
  81.8 8.4 %collective-permute-start.19 = (f32[64,256]{1,0:T(8,128)S(1)}, f32[64,256]{1,0:T(8,128)S(1)}, u32[]{:S(2)}, u32[]{:S(2)}) collective-permute-start(f32[64,256]{1,0:T(8,128)S(1)} %get-tuple-element.138), channel_id=1, source_target_pairs={{0,2},{1,3},{2,0},{3,1},{4,6},{5,7},{6,4},{7,5},{8,10},{9,11},{10,... | collective-permute-start | bytes 196616 | tf_op jit(solution)/shard_map/ppermute | solution.py:41
  98.1 10.4 %collective-permute-start.22 = (f32[128,256]{1,0:T(8,128)S(1)}, f32[128,256]{1,0:T(8,128)S(1)}, u32[]{:S(2)}, u32[]{:S(2)}) collective-permute-start(f32[128,256]{1,0:T(8,128)S(1)} %get-tuple-element.146), channel_id=1, source_target_pairs={{0,2},{1,3},{2,0},{3,1},{4,6},{5,7},{6,4},{7,5},{8,10},{9,11},{10,... | collective-permute-start | bytes 393224 | tf_op jit(solution)/shard_map/ppermute | solution.py:41
  99.5 12.2 %collective-permute-start.23 = (f32[128,256]{1,0:T(8,128)S(1)}, f32[128,256]{1,0:T(8,128)S(1)}, u32[]{:S(2)}, u32[]{:S(2)}) collective-permute-start(f32[128,256]{1,0:T(8,128)S(1)} %get-tuple-element.147), channel_id=1, source_target_pairs={{0,3},{1,2},{2,1},{3,0},{4,7},{5,6},{6,5},{7,4},{8,11},{9,10},{10,... | collective-permute-start | bytes 393224 | tf_op jit(solution)/shard_map/ppermute | solution.py:41
  114.8 17.3 %collective-permute-start.24 = (f32[34,64,128]{2,1,0:T(8,128)S(1)}, f32[34,64,128]{2,1,0:T(8,128)S(1)}, u32[]{:S(2)}, u32[]{:S(2)}) collective-permute-start(f32[34,64,128]{2,1,0:T(8,128)S(1)} %get-tuple-element.157), channel_id=1, source_target_pairs={{0,12},{1,49},{2,14},{3,51},{4,0},{5,53},{6,2},{7,55},{8,4},{9,57}... | collective-permute-start | bytes 3342344 | tf_op jit(solution)/shard_map/ppermute | solution.py:33
  115.9 28.8 %collective-permute-start.25 = (f32[34,64,128]{2,1,0:T(8,128)S(1)}, f32[34,64,128]{2,1,0:T(8,128)S(1)}, u32[]{:S(2)}, u32[]{:S(2)}) collective-permute-start(f32[34,64,128]{2,1,0:T(8,128)S(1)} %get-tuple-element.158), channel_id=1, source_target_pairs={{0,8},{1,33},{2,10},{3,35},{4,12},{5,37},{6,14},{7,39},{8,0},{9,41... | collective-permute-start | bytes 3342344 | tf_op jit(solution)/shard_map/ppermute | solution.py:33
  119.4 26.5 %collective-permute-start.26 = (f32[34,64,128]{2,1,0:T(8,128)S(1)}, f32[34,64,128]{2,1,0:T(8,128)S(1)}, u32[]{:S(2)}, u32[]{:S(2)}) collective-permute-start(f32[34,64,128]{2,1,0:T(8,128)S(1)} %get-tuple-element.159), channel_id=1, source_target_pairs={{0,4},{1,17},{2,6},{3,19},{4,8},{5,21},{6,10},{7,23},{8,12},{9,25}... | collective-permute-start | bytes 3342344 | tf_op jit(solution)/shard_map/ppermute | solution.py:33
  147.9 9.9 %collective-permute-start.30 = (f32[18,64,128]{2,1,0:T(8,128)S(1)}, f32[18,64,128]{2,1,0:T(8,128)S(1)}, u32[]{:S(2)}, u32[]{:S(2)}) collective-permute-start(f32[18,64,128]{2,1,0:T(8,128)S(1)} %get-tuple-element.173), channel_id=1, source_target_pairs={{0,48},{1,13},{2,50},{3,15},{4,52},{5,1},{6,54},{7,3},{8,56},{9,5}... | collective-permute-start | bytes 1769480 | tf_op jit(solution)/shard_map/ppermute | solution.py:33
  147.9 11.5 %collective-permute-start.31 = (f32[18,64,128]{2,1,0:T(8,128)S(1)}, f32[18,64,128]{2,1,0:T(8,128)S(1)}, u32[]{:S(2)}, u32[]{:S(2)}) collective-permute-start(f32[18,64,128]{2,1,0:T(8,128)S(1)} %get-tuple-element.174), channel_id=1, source_target_pairs={{0,32},{1,9},{2,34},{3,11},{4,36},{5,13},{6,38},{7,15},{8,40},{9,1... | collective-permute-start | bytes 1769480 | tf_op jit(solution)/shard_map/ppermute | solution.py:33
  149.3 16.3 %collective-permute-start.32 = (f32[18,64,128]{2,1,0:T(8,128)S(1)}, f32[18,64,128]{2,1,0:T(8,128)S(1)}, u32[]{:S(2)}, u32[]{:S(2)}) collective-permute-start(f32[18,64,128]{2,1,0:T(8,128)S(1)} %get-tuple-element.175), channel_id=1, source_target_pairs={{0,16},{1,5},{2,18},{3,7},{4,20},{5,9},{6,22},{7,11},{8,24},{9,13}... | collective-permute-start | bytes 1769480 | tf_op jit(solution)/shard_map/ppermute | solution.py:33
  165.6 13.5 %collective-permute-start.34 = (f32[16,64,128]{2,1,0:T(8,128)S(1)}, f32[16,64,128]{2,1,0:T(8,128)S(1)}, u32[]{:S(2)}, u32[]{:S(2)}) collective-permute-start(f32[16,64,128]{2,1,0:T(8,128)S(1)} %get-tuple-element.182), channel_id=1, source_target_pairs={{0,32},{1,9},{2,34},{3,11},{4,36},{5,13},{6,38},{7,15},{8,40},{9,1... | collective-permute-start | bytes 1572872 | tf_op jit(solution)/shard_map/ppermute | solution.py:33
  167.0 10.6 %collective-permute-start.33 = (f32[8,64,128]{2,1,0:T(8,128)S(1)}, f32[8,64,128]{2,1,0:T(8,128)S(1)}, u32[]{:S(2)}, u32[]{:S(2)}) collective-permute-start(f32[8,64,128]{2,1,0:T(8,128)S(1)} %get-tuple-element.181), channel_id=1, source_target_pairs={{0,48},{1,13},{2,50},{3,15},{4,52},{5,1},{6,54},{7,3},{8,56},{9,5}... | collective-permute-start | bytes 786440 | tf_op jit(solution)/shard_map/ppermute | solution.py:33
  168.2 10.9 %collective-permute-start.35 = (f32[8,64,128]{2,1,0:T(8,128)S(1)}, f32[8,64,128]{2,1,0:T(8,128)S(1)}, u32[]{:S(2)}, u32[]{:S(2)}) collective-permute-start(f32[8,64,128]{2,1,0:T(8,128)S(1)} %get-tuple-element.183), channel_id=1, source_target_pairs={{0,16},{1,5},{2,18},{3,7},{4,20},{5,9},{6,22},{7,11},{8,24},{9,13}... | collective-permute-start | bytes 786440 | tf_op jit(solution)/shard_map/ppermute | solution.py:33
  169.2 27.9 %collective-permute-start.37 = (f32[10,64,128]{2,1,0:T(8,128)S(1)}, f32[10,64,128]{2,1,0:T(8,128)S(1)}, u32[]{:S(2)}, u32[]{:S(2)}) collective-permute-start(f32[10,64,128]{2,1,0:T(8,128)S(1)} %get-tuple-element.195.refs_4_), channel_id=1, source_target_pairs={{0,128},{4,132},{8,136},{12,140},{16,144},{20,148},{24,152},{28,15... | collective-permute-start | bytes 983048 | tf_op jit(solution)/shard_map/ppermute | solution.py:37
  175.9 21.1 %collective-permute-start.38 = (f32[10,64,128]{2,1,0:T(8,128)S(1)}, f32[10,64,128]{2,1,0:T(8,128)S(1)}, u32[]{:S(2)}, u32[]{:S(2)}) collective-permute-start(f32[10,64,128]{2,1,0:T(8,128)S(1)} %get-tuple-element.196), channel_id=1, source_target_pairs={{0,192},{4,196},{8,200},{12,204},{16,208},{20,212},{24,216},{28,22... | collective-permute-start | bytes 983048 | tf_op jit(solution)/shard_map/ppermute | solution.py:37
  179.2 22.1 %collective-permute-start.36 = (f32[10,64,128]{2,1,0:T(8,128)S(1)}, f32[10,64,128]{2,1,0:T(8,128)S(1)}, u32[]{:S(2)}, u32[]{:S(2)}) collective-permute-start(f32[10,64,128]{2,1,0:T(8,128)S(1)} %join1.1), channel_id=1, source_target_pairs={{0,64},{4,68},{8,72},{12,76},{16,80},{20,84},{24,88},{28,92},{32,9... | collective-permute-start | bytes 983048 | tf_op jit(solution)/shard_map/ppermute | solution.py:37
  185.5 16.4 %collective-permute-start.39 = (f32[8,64,128]{2,1,0:T(8,128)S(1)}, f32[8,64,128]{2,1,0:T(8,128)S(1)}, u32[]{:S(2)}, u32[]{:S(2)}) collective-permute-start(f32[8,64,128]{2,1,0:T(8,128)S(1)} %get-tuple-element.198), channel_id=1, source_target_pairs={{0,48},{1,13},{2,50},{3,15},{4,52},{5,1},{6,54},{7,3},{8,56},{9,5}... | collective-permute-start | bytes 786440 | tf_op jit(solution)/shard_map/ppermute | solution.py:33
  186.2 15.7 %collective-permute-start.40 = (f32[8,64,128]{2,1,0:T(8,128)S(1)}, f32[8,64,128]{2,1,0:T(8,128)S(1)}, u32[]{:S(2)}, u32[]{:S(2)}) collective-permute-start(f32[8,64,128]{2,1,0:T(8,128)S(1)} %get-tuple-element.199), channel_id=1, source_target_pairs={{0,16},{1,5},{2,18},{3,7},{4,20},{5,9},{6,22},{7,11},{8,24},{9,13}... | collective-permute-start | bytes 786440 | tf_op jit(solution)/shard_map/ppermute | solution.py:33
  (20 other events, 219.5 us)

commit v4 on v3

--- a/solution.py
+++ b/solution.py
@@ -9,7 +9,7 @@
 
 SIDE = 4
 RB = 8
-GROUP = 16
+GROUP = 32
 CUTS = 4
 PER = SIDE * SIDE * 2
 F32 = jnp.float32
@@ -110,15 +110,27 @@
                     outs[far][at] = source[base + pick[far * PER + at]]
 
 
-def unpack_kernel(pick, *refs):
+def unpack_far_kernel(pick, *refs):
     ins, outs = refs[:SIDE], refs[SIDE:]
     for out in outs:
         out[...] = jnp.zeros_like(out)
     tail = (ins[0][PER:] + ins[1][PER:]) + (ins[2][PER:] + ins[3][PER:])
     for near in range(SIDE):
-        outs[2 * SIDE + near][2 * RB :] = tail
-        for k in range(SIDE):
-            target, base = outs[min(k, 2) * SIDE + near], RB * (k == 3)
+        outs[near][2 * RB :] = tail
+        for k in (2, 3):
+            for far in range(SIDE):
+                for p in range(2):
+                    at = (near * SIDE + k) * 2 + p
+                    outs[near][RB * (k == 3) + pick[far * PER + at]] += ins[far][at]
+
+
+def unpack_kernel(pick, *refs):
+    ins, outs = refs[:SIDE], refs[SIDE:]
+    for out in outs:
+        out[...] = jnp.zeros_like(out)
+    for near in range(SIDE):
+        for k in range(2):
+            target, base = outs[k * SIDE + near], 0
             if k == 0 and near == 2:
                 target, base = outs[SIDE + near], RB
             for far in range(SIDE):
@@ -435,16 +447,23 @@
     home = [sent[0]] + [shift(sent[d], 0, -d) for d in (1, 2, 3)]
     out = exchange(out)
     home, out = lax.optimization_barrier((home, out))
+    far_part = call(
+        unpack_far_kernel,
+        "unpack_far",
+        [struct(length, width, size) for length in lengths[2 * SIDE :]],
+        [SMEM] + [VMEM] * SIDE,
+        [VMEM] * SIDE,
+        [],
+    )(pick, *home)
     summed = call(
         unpack_kernel,
         "unpack",
-        [struct(length, width, size) for length in lengths],
+        [struct(length, width, size) for length in lengths[: 2 * SIDE]],
         [SMEM] + [VMEM] * SIDE,
-        [VMEM] * (3 * SIDE),
+        [VMEM] * (2 * SIDE),
         [],
-        nbytes=8 << 20,
     )(pick, *home)
-    own_part, next_part, far_part = summed[:SIDE], summed[SIDE : 2 * SIDE], summed[2 * SIDE :]
+    own_part, next_part = summed[:SIDE], summed[SIDE:]
     far_part, next_part = lax.optimization_barrier((route(far_part), next_part))
     far_ends = join(far_part)
     next_part, own_part = lax.optimization_barrier((route(next_part), own_part))

time: 204 us -> 202 us (level)
  waiting for transfers between devices: 99.3 us -> 94.9 us
    ppermute x23, starting transfers between devices: 32.5 us -> 36.1 us  [shift(): return lax.ppermute(value, ('row', 'col'), pairs)]
    ppermute x23, waiting for transfers between devices: 53.6 us -> 50.2 us  [shift(): return lax.ppermute(value, ('row', 'col'), pairs)]
  transfers between devices with their start and end apart: 41 -> 41, of which waited for: 22 -> 21; matrix products, arithmetic and copies ran while one was open for 0% -> 0% of each run, Pallas kernels for 1% -> 2%
where the time goes in v4:
time: 202 us; the launch traced here: 201 us
  waiting for transfers between devices  94.9 us (47%)
  starting transfers between devices  81 us (40%)
  Pallas kernels  13.6 us (7%)
  local copies, waits for them, and re-layouts  8.23 us (4%)
    ppermute x23, waiting for transfers between devices, shift(): return lax.ppermute(value, ('row', 'col'), pairs)  50.2 us
    ppermute x23, starting transfers between devices, shift(): return lax.ppermute(value, ('row', 'col'), pairs)  36.1 us
    ppermute x12, waiting for transfers between devices, swap_col(): return lax.ppermute(value, 'col', [(c, c ^ k) for c in range(4)])  26.3 us
    ppermute x12, starting transfers between devices, swap_col(): return lax.ppermute(value, 'col', [(c, c ^ k) for c in range(4)])  24.4 us
    ppermute x6, starting transfers between devices, swap_z(): lax.ppermute(value, 'row', [(r, r ^ k * SIDE * SIDE) for r in range(SIDE...  20.5 us
    ppermute x6, waiting for transfers between devices, swap_z(): lax.ppermute(value, 'row', [(r, r ^ k * SIDE * SIDE) for r in range(SIDE...  18.5 us
    unnamed x24, local copies, waits for them, and re-layouts  7 us
  transfers between devices with their start and end apart: 41, of which 21 were waited for; matrix products, arithmetic and copies ran while one was open for 0% of the time, Pallas kernels for 2%

profile of v4, /device:TPU:8, one launch (start us, length us, event | category | flops | bytes accessed | tf_op | source)
XLA Modules:
  0.0 201.2 jit_solution(15309941787384456801)
XLA Ops:
  7.3 2.7 %collective-permute-start.1 = (f32[8,64,128]{2,1,0:T(8,128)S(1)}, f32[8,64,128]{2,1,0:T(8,128)S(1)}, u32[]{:S(2)}, u32[]{:S(2)}) collective-permute-start(f32[8,64,128]{2,1,0:T(8,128)S(1)} %bitcast.47), channel_id=1, source_target_pairs={{0,32},{1,9},{2,34},{3,11},{4,36},{5,13},{6,38},{7,15},{8,40},{9,1... | collective-permute-start | bytes 786440 | tf_op jit(solution)/shard_map/ppermute | solution.py:33
  11.4 3.3 %collective-permute-start.7 = (f32[8,64,128]{2,1,0:T(8,128)S(1)}, f32[8,64,128]{2,1,0:T(8,128)S(1)}, u32[]{:S(2)}, u32[]{:S(2)}) collective-permute-start(f32[8,64,128]{2,1,0:T(8,128)S(1)} %bitcast.49), channel_id=1, source_target_pairs={{0,128},{4,132},{8,136},{12,140},{16,144},{20,148},{24,152},{28,15... | collective-permute-start | bytes 786440 | tf_op jit(solution)/shard_map/ppermute | solution.py:37
  16.4 2.7 %collective-permute-start.5 = (f32[8,64,128]{2,1,0:T(8,128)S(1)}, f32[8,64,128]{2,1,0:T(8,128)S(1)}, u32[]{:S(2)}, u32[]{:S(2)}) collective-permute-start(f32[8,64,128]{2,1,0:T(8,128)S(1)} %collective-permute-done.3.refs_4_), channel_id=1, source_target_pairs={{0,32},{1,9},{2,34},{3,11},{4,36},{5,13},{6,38},{7,15},{8,40},{9,1... | collective-permute-start | bytes 786440 | tf_op jit(solution)/shard_map/ppermute | solution.py:33
  20.5 3.4 %copy-done.2 = s32[128,128,128]{2,1,0:T(8,128)S(1)} copy-done((s32[128,128,128]{2,1,0:T(8,128)S(1)}, s32[128,128,128]{2,1,0:T(8,128)}, u32[]{:S(2)}) %copy-start.2) | copy-done | bytes 8388632
  27.7 4.8 %collective-permute-done.7 = f32[8,64,128]{2,1,0:T(8,128)S(1)} collective-permute-done((f32[8,64,128]{2,1,0:T(8,128)S(1)}, f32[8,64,128]{2,1,0:T(8,128)S(1)}, u32[]{:S(2)}, u32[]{:S(2)}) %collective-permute-start.7) | collective-permute-done | bytes 262176 | tf_op jit(solution)/shard_map/ppermute | solution.py:37
  33.8 2.6 %collective-permute-start.11 = (f32[16,64,128]{2,1,0:T(8,128)S(1)}, f32[16,64,128]{2,1,0:T(8,128)S(1)}, u32[]{:S(2)}, u32[]{:S(2)}) collective-permute-start(f32[16,64,128]{2,1,0:T(8,128)S(1)} %constant_dynamic-update-slice_fusion.refs_8_), channel_id=1, source_target_pairs={{0,48},{1,13},{2,50},{3,15},{4,52},{5,1},{6,54},{7,3},{8,56},{9,5}... | collective-permute-start | bytes 1572872 | tf_op jit(solution)/shard_map/ppermute | solution.py:33
  36.4 7.1 %collective-permute-done.10.refs_10_ = f32[16,64,128]{2,1,0:T(8,128)S(1)} collective-permute-done((f32[16,64,128]{2,1,0:T(8,128)S(1)}, f32[16,64,128]{2,1,0:T(8,128)S(1)}, u32[]{:S(2)}, u32[]{:S(2)}) %collective-permute-start.10) | collective-permute-done | bytes 524320 | tf_op jit(solution)/shard_map/ppermute | solution.py:33
  43.5 3.4 %collective-permute-done.11.refs_11_ = f32[16,64,128]{2,1,0:T(8,128)S(1)} collective-permute-done((f32[16,64,128]{2,1,0:T(8,128)S(1)}, f32[16,64,128]{2,1,0:T(8,128)S(1)}, u32[]{:S(2)}, u32[]{:S(2)}) %collective-permute-start.11) | collective-permute-done | bytes 524320 | tf_op jit(solution)/shard_map/ppermute | solution.py:33
  54.6 5.7 %collective-permute-start.16 = (f32[64,256]{1,0:T(8,128)S(1)}, f32[64,256]{1,0:T(8,128)S(1)}, u32[]{:S(2)}, u32[]{:S(2)}) collective-permute-start(f32[64,256]{1,0:T(8,128)S(1)} %get-tuple-element.130), channel_id=1, source_target_pairs={{0,2},{1,3},{2,0},{3,1},{4,6},{5,7},{6,4},{7,5},{8,10},{9,11},{10,... | collective-permute-start | bytes 196616 | tf_op jit(solution)/shard_map/ppermute | solution.py:41
  63.0 5.4 %collective-permute-done.17.c3 = f32[64,256]{1,0:T(8,128)S(1)} collective-permute-done((f32[64,256]{1,0:T(8,128)S(1)}, f32[64,256]{1,0:T(8,128)S(1)}, u32[]{:S(2)}, u32[]{:S(2)}) %collective-permute-start.17) | collective-permute-done | bytes 65568 | tf_op jit(solution)/shard_map/ppermute | solution.py:41
  68.4 10.0 %collective-permute-done.14.q3 = f32[32,64,128]{2,1,0:T(8,128)S(1)} collective-permute-done((f32[32,64,128]{2,1,0:T(8,128)S(1)}, f32[32,64,128]{2,1,0:T(8,128)S(1)}, u32[]{:S(2)}, u32[]{:S(2)}) %collective-permute-start.14) | collective-permute-done | bytes 1048608 | tf_op jit(solution)/shard_map/ppermute | solution.py:33
  78.5 3.8 %forward.1 = (f32[64,256]{1,0:T(8,128)S(1)}, f32[64,256]{1,0:T(8,128)S(1)}, f32[64,256]{1,0:T(8,128)S(1)}, f32[64,256]{1,0:T(8,128)S(1)}) custom-call(s32[128]{0:T(128)S(1)} %compare_select_fusion.12.rows, s32[128]{0:T(128)S(1)} %get-tuple-element.202.at, s32[2]{0:T(128)S(1)} %pad_add_fusion.info, f32[64,1024]{1,0:T(8,128)S(1)} %get-tuple-element.204.scaled, ...), custom_call_target="tpu_custom_call" | custom-call | bytes 16777216 | tf_op jit(solution)/shard_map/forward/pallas_call | solution.py:402
  82.4 5.3 %collective-permute-start.19 = (f32[64,256]{1,0:T(8,128)S(1)}, f32[64,256]{1,0:T(8,128)S(1)}, u32[]{:S(2)}, u32[]{:S(2)}) collective-permute-start(f32[64,256]{1,0:T(8,128)S(1)} %get-tuple-element.138), channel_id=1, source_target_pairs={{0,2},{1,3},{2,0},{3,1},{4,6},{5,7},{6,4},{7,5},{8,10},{9,11},{10,... | collective-permute-start | bytes 196616 | tf_op jit(solution)/shard_map/ppermute | solution.py:41
  88.1 2.6 %collective-permute-done.19.a2 = f32[64,256]{1,0:T(8,128)S(1)} collective-permute-done((f32[64,256]{1,0:T(8,128)S(1)}, f32[64,256]{1,0:T(8,128)S(1)}, u32[]{:S(2)}, u32[]{:S(2)}) %collective-permute-start.19) | collective-permute-done | bytes 65568 | tf_op jit(solution)/shard_map/ppermute | solution.py:41
  90.8 4.8 %collective-permute-done.20.a3 = f32[64,256]{1,0:T(8,128)S(1)} collective-permute-done((f32[64,256]{1,0:T(8,128)S(1)}, f32[64,256]{1,0:T(8,128)S(1)}, u32[]{:S(2)}, u32[]{:S(2)}) %collective-permute-start.20) | collective-permute-done | bytes 65568 | tf_op jit(solution)/shard_map/ppermute | solution.py:41
  97.1 2.9 %collective-permute-start.22 = (f32[128,256]{1,0:T(8,128)S(1)}, f32[128,256]{1,0:T(8,128)S(1)}, u32[]{:S(2)}, u32[]{:S(2)}) collective-permute-start(f32[128,256]{1,0:T(8,128)S(1)} %get-tuple-element.146), channel_id=1, source_target_pairs={{0,2},{1,3},{2,0},{3,1},{4,6},{5,7},{6,4},{7,5},{8,10},{9,11},{10,... | collective-permute-start | bytes 393224 | tf_op jit(solution)/shard_map/ppermute | solution.py:41
  100.1 2.7 %collective-permute-start.23 = (f32[128,256]{1,0:T(8,128)S(1)}, f32[128,256]{1,0:T(8,128)S(1)}, u32[]{:S(2)}, u32[]{:S(2)}) collective-permute-start(f32[128,256]{1,0:T(8,128)S(1)} %get-tuple-element.147), channel_id=1, source_target_pairs={{0,3},{1,2},{2,1},{3,0},{4,7},{5,6},{6,5},{7,4},{8,11},{9,10},{10,... | collective-permute-start | bytes 393224 | tf_op jit(solution)/shard_map/ppermute | solution.py:41
  102.7 4.1 %collective-permute-done.22.i2 = f32[128,256]{1,0:T(8,128)S(1)} collective-permute-done((f32[128,256]{1,0:T(8,128)S(1)}, f32[128,256]{1,0:T(8,128)S(1)}, u32[]{:S(2)}, u32[]{:S(2)}) %collective-permute-start.22) | collective-permute-done | bytes 131104 | tf_op jit(solution)/shard_map/ppermute | solution.py:41
  106.9 3.1 %collective-permute-done.23.i3 = f32[128,256]{1,0:T(8,128)S(1)} collective-permute-done((f32[128,256]{1,0:T(8,128)S(1)}, f32[128,256]{1,0:T(8,128)S(1)}, u32[]{:S(2)}, u32[]{:S(2)}) %collective-permute-start.23) | collective-permute-done | bytes 131104 | tf_op jit(solution)/shard_map/ppermute | solution.py:41
  110.0 3.3 %backward.1 = (f32[64,1024]{1,0:T(8,128)S(1)}, f32[34,64,128]{2,1,0:T(8,128)S(1)}, f32[34,64,128]{2,1,0:T(8,128)S(1)}, f32[34,64,128]{2,1,0:T(8,128)S(1)}, f32[34,64,128]{2,1,0:T(8,128)S(1)}) custom-call(s32[128]{0:T(128)S(1)} %copy-done.4, s32[128]{0:T(128)S(1)} %get-tuple-element.201.at, s32[2]{0:T(128)S(1)} %pad_add_fusion.info, f32[1,1024]{1,0:T(1,128)S(1)} %bitcast.53, ...), custom_call_target="tpu_custom_call" | custom-call | bytes 16777216 | tf_op jit(solution)/shard_map/backward/pallas_call | solution.py:428
  113.3 4.2 %collective-permute-start.24 = (f32[34,64,128]{2,1,0:T(8,128)S(1)}, f32[34,64,128]{2,1,0:T(8,128)S(1)}, u32[]{:S(2)}, u32[]{:S(2)}) collective-permute-start(f32[34,64,128]{2,1,0:T(8,128)S(1)} %get-tuple-element.157), channel_id=1, source_target_pairs={{0,12},{1,49},{2,14},{3,51},{4,0},{5,53},{6,2},{7,55},{8,4},{9,57}... | collective-permute-start | bytes 3342344 | tf_op jit(solution)/shard_map/ppermute | solution.py:33
  119.0 2.5 %collective-permute-start.26 = (f32[34,64,128]{2,1,0:T(8,128)S(1)}, f32[34,64,128]{2,1,0:T(8,128)S(1)}, u32[]{:S(2)}, u32[]{:S(2)}) collective-permute-start(f32[34,64,128]{2,1,0:T(8,128)S(1)} %get-tuple-element.159), channel_id=1, source_target_pairs={{0,4},{1,17},{2,6},{3,19},{4,8},{5,21},{6,10},{7,23},{8,12},{9,25}... | collective-permute-start | bytes 3342344 | tf_op jit(solution)/shard_map/ppermute | solution.py:33
  123.8 3.5 %collective-permute-start.29 = (f32[64,256]{1,0:T(8,128)S(1)}, f32[64,256]{1,0:T(8,128)S(1)}, u32[]{:S(2)}, u32[]{:S(2)}) collective-permute-start(f32[64,256]{1,0:T(8,128)S(1)} %get-tuple-element.163), channel_id=1, source_target_pairs={{0,3},{1,2},{2,1},{3,0},{4,7},{5,6},{6,5},{7,4},{8,11},{9,10},{10,... | collective-permute-start | bytes 196616 | tf_op jit(solution)/shard_map/ppermute | solution.py:41
  127.3 2.6 %collective-permute-done.28 = f32[64,256]{1,0:T(8,128)S(1)} collective-permute-done((f32[64,256]{1,0:T(8,128)S(1)}, f32[64,256]{1,0:T(8,128)S(1)}, u32[]{:S(2)}, u32[]{:S(2)}) %collective-permute-start.28) | collective-permute-done | bytes 65568 | tf_op jit(solution)/shard_map/ppermute | solution.py:41
  131.8 12.6 %collective-permute-done.25.refs_2_ = f32[34,64,128]{2,1,0:T(8,128)S(1)} collective-permute-done((f32[34,64,128]{2,1,0:T(8,128)S(1)}, f32[34,64,128]{2,1,0:T(8,128)S(1)}, u32[]{:S(2)}, u32[]{:S(2)}) %collective-permute-start.25) | collective-permute-done | bytes 1114144 | tf_op jit(solution)/shard_map/ppermute | solution.py:33
  146.7 2.3 %collective-permute-start.31 = (f32[18,64,128]{2,1,0:T(8,128)S(1)}, f32[18,64,128]{2,1,0:T(8,128)S(1)}, u32[]{:S(2)}, u32[]{:S(2)}) collective-permute-start(f32[18,64,128]{2,1,0:T(8,128)S(1)} %get-tuple-element.174), channel_id=1, source_target_pairs={{0,32},{1,9},{2,34},{3,11},{4,36},{5,13},{6,38},{7,15},{8,40},{9,1... | collective-permute-start | bytes 1769480 | tf_op jit(solution)/shard_map/ppermute | solution.py:33
  151.9 4.5 %collective-permute-done.30.refs_1_ = f32[18,64,128]{2,1,0:T(8,128)S(1)} collective-permute-done((f32[18,64,128]{2,1,0:T(8,128)S(1)}, f32[18,64,128]{2,1,0:T(8,128)S(1)}, u32[]{:S(2)}, u32[]{:S(2)}) %collective-permute-start.30) | collective-permute-done | bytes 589856 | tf_op jit(solution)/shard_map/ppermute | solution.py:33
  158.2 6.2 %collective-permute-done.32.refs_3_ = f32[18,64,128]{2,1,0:T(8,128)S(1)} collective-permute-done((f32[18,64,128]{2,1,0:T(8,128)S(1)}, f32[18,64,128]{2,1,0:T(8,128)S(1)}, u32[]{:S(2)}, u32[]{:S(2)}) %collective-permute-start.32) | collective-permute-done | bytes 589856 | tf_op jit(solution)/shard_map/ppermute | solution.py:33
  168.8 6.2 %collective-permute-start.37 = (f32[10,64,128]{2,1,0:T(8,128)S(1)}, f32[10,64,128]{2,1,0:T(8,128)S(1)}, u32[]{:S(2)}, u32[]{:S(2)}) collective-permute-start(f32[10,64,128]{2,1,0:T(8,128)S(1)} %get-tuple-element.195.refs_4_), channel_id=1, source_target_pairs={{0,128},{4,132},{8,136},{12,140},{16,144},{20,148},{24,152},{28,15... | collective-permute-start | bytes 983048 | tf_op jit(solution)/shard_map/ppermute | solution.py:37
  178.0 6.0 %collective-permute-start.36 = (f32[10,64,128]{2,1,0:T(8,128)S(1)}, f32[10,64,128]{2,1,0:T(8,128)S(1)}, u32[]{:S(2)}, u32[]{:S(2)}) collective-permute-start(f32[10,64,128]{2,1,0:T(8,128)S(1)} %join1.1), channel_id=1, source_target_pairs={{0,64},{4,68},{8,72},{12,76},{16,80},{20,84},{24,88},{28,92},{32,9... | collective-permute-start | bytes 983048 | tf_op jit(solution)/shard_map/ppermute | solution.py:37
  186.1 9.2 %collective-permute-done.37 = f32[10,64,128]{2,1,0:T(8,128)S(1)} collective-permute-done((f32[10,64,128]{2,1,0:T(8,128)S(1)}, f32[10,64,128]{2,1,0:T(8,128)S(1)}, u32[]{:S(2)}, u32[]{:S(2)}) %collective-permute-start.37) | collective-permute-done | bytes 327712 | tf_op jit(solution)/shard_map/ppermute | solution.py:37
  195.3 4.5 %collective-permute-done.36 = f32[10,64,128]{2,1,0:T(8,128)S(1)} collective-permute-done((f32[10,64,128]{2,1,0:T(8,128)S(1)}, f32[10,64,128]{2,1,0:T(8,128)S(1)}, u32[]{:S(2)}, u32[]{:S(2)}) %collective-permute-start.36) | collective-permute-done | bytes 327712 | tf_op jit(solution)/shard_map/ppermute | solution.py:37
  (106 shorter events, 51.3 us)
Async XLA Ops:
  3.8 10.9 %collective-permute-start = (f32[8,64,128]{2,1,0:T(8,128)S(1)}, f32[8,64,128]{2,1,0:T(8,128)S(1)}, u32[]{:S(2)}, u32[]{:S(2)}) collective-permute-start(f32[8,64,128]{2,1,0:T(8,128)S(1)} %bitcast.45), channel_id=1, source_target_pairs={{0,16},{1,5},{2,18},{3,7},{4,20},{5,9},{6,22},{7,11},{8,24},{9,13}... | collective-permute-start | bytes 786440 | tf_op jit(solution)/shard_map/ppermute | solution.py:33
  5.4 10.7 %collective-permute-start.3 = (f32[8,64,128]{2,1,0:T(8,128)S(1)}, f32[8,64,128]{2,1,0:T(8,128)S(1)}, u32[]{:S(2)}, u32[]{:S(2)}) collective-permute-start(f32[8,64,128]{2,1,0:T(8,128)S(1)} %bitcast.46), channel_id=1, source_target_pairs={{0,64},{4,68},{8,72},{12,76},{16,80},{20,84},{24,88},{28,92},{32,9... | collective-permute-start | bytes 786440 | tf_op jit(solution)/shard_map/ppermute | solution.py:37
  7.3 9.1 %collective-permute-start.1 = (f32[8,64,128]{2,1,0:T(8,128)S(1)}, f32[8,64,128]{2,1,0:T(8,128)S(1)}, u32[]{:S(2)}, u32[]{:S(2)}) collective-permute-start(f32[8,64,128]{2,1,0:T(8,128)S(1)} %bitcast.47), channel_id=1, source_target_pairs={{0,32},{1,9},{2,34},{3,11},{4,36},{5,13},{6,38},{7,15},{8,40},{9,1... | collective-permute-start | bytes 786440 | tf_op jit(solution)/shard_map/ppermute | solution.py:33
  10.0 9.1 %collective-permute-start.2 = (f32[8,64,128]{2,1,0:T(8,128)S(1)}, f32[8,64,128]{2,1,0:T(8,128)S(1)}, u32[]{:S(2)}, u32[]{:S(2)}) collective-permute-start(f32[8,64,128]{2,1,0:T(8,128)S(1)} %bitcast.48), channel_id=1, source_target_pairs={{0,48},{1,13},{2,50},{3,15},{4,52},{5,1},{6,54},{7,3},{8,56},{9,5}... | collective-permute-start | bytes 786440 | tf_op jit(solution)/shard_map/ppermute | solution.py:33
  11.4 21.1 %collective-permute-start.7 = (f32[8,64,128]{2,1,0:T(8,128)S(1)}, f32[8,64,128]{2,1,0:T(8,128)S(1)}, u32[]{:S(2)}, u32[]{:S(2)}) collective-permute-start(f32[8,64,128]{2,1,0:T(8,128)S(1)} %bitcast.49), channel_id=1, source_target_pairs={{0,128},{4,132},{8,136},{12,140},{16,144},{20,148},{24,152},{28,15... | collective-permute-start | bytes 786440 | tf_op jit(solution)/shard_map/ppermute | solution.py:37
  14.7 17.8 %collective-permute-start.8 = (f32[8,64,128]{2,1,0:T(8,128)S(1)}, f32[8,64,128]{2,1,0:T(8,128)S(1)}, u32[]{:S(2)}, u32[]{:S(2)}) collective-permute-start(f32[8,64,128]{2,1,0:T(8,128)S(1)} %bitcast.50), channel_id=1, source_target_pairs={{0,192},{4,196},{8,200},{12,204},{16,208},{20,212},{24,216},{28,22... | collective-permute-start | bytes 786440 | tf_op jit(solution)/shard_map/ppermute | solution.py:37
  16.1 16.4 %collective-permute-start.4 = (f32[8,64,128]{2,1,0:T(8,128)S(1)}, f32[8,64,128]{2,1,0:T(8,128)S(1)}, u32[]{:S(2)}, u32[]{:S(2)}) collective-permute-start(f32[8,64,128]{2,1,0:T(8,128)S(1)} %collective-permute-done.3.refs_4_), channel_id=1, source_target_pairs={{0,16},{1,5},{2,18},{3,7},{4,20},{5,9},{6,22},{7,11},{8,24},{9,13}... | collective-permute-start | bytes 786440 | tf_op jit(solution)/shard_map/ppermute | solution.py:33
  16.4 16.1 %collective-permute-start.5 = (f32[8,64,128]{2,1,0:T(8,128)S(1)}, f32[8,64,128]{2,1,0:T(8,128)S(1)}, u32[]{:S(2)}, u32[]{:S(2)}) collective-permute-start(f32[8,64,128]{2,1,0:T(8,128)S(1)} %collective-permute-done.3.refs_4_), channel_id=1, source_target_pairs={{0,32},{1,9},{2,34},{3,11},{4,36},{5,13},{6,38},{7,15},{8,40},{9,1... | collective-permute-start | bytes 786440 | tf_op jit(solution)/shard_map/ppermute | solution.py:33
  19.1 13.4 %collective-permute-start.6 = (f32[8,64,128]{2,1,0:T(8,128)S(1)}, f32[8,64,128]{2,1,0:T(8,128)S(1)}, u32[]{:S(2)}, u32[]{:S(2)}) collective-permute-start(f32[8,64,128]{2,1,0:T(8,128)S(1)} %collective-permute-done.3.refs_4_), channel_id=1, source_target_pairs={{0,48},{1,13},{2,50},{3,15},{4,52},{5,1},{6,54},{7,3},{8,56},{9,5}... | collective-permute-start | bytes 786440 | tf_op jit(solution)/shard_map/ppermute | solution.py:33
  32.6 10.9 %collective-permute-start.10 = (f32[16,64,128]{2,1,0:T(8,128)S(1)}, f32[16,64,128]{2,1,0:T(8,128)S(1)}, u32[]{:S(2)}, u32[]{:S(2)}) collective-permute-start(f32[16,64,128]{2,1,0:T(8,128)S(1)} %constant_dynamic-update-slice_fusion.refs_8_), channel_id=1, source_target_pairs={{0,32},{1,9},{2,34},{3,11},{4,36},{5,13},{6,38},{7,15},{8,40},{9,1... | collective-permute-start | bytes 1572872 | tf_op jit(solution)/shard_map/ppermute | solution.py:33
  33.8 13.1 %collective-permute-start.11 = (f32[16,64,128]{2,1,0:T(8,128)S(1)}, f32[16,64,128]{2,1,0:T(8,128)S(1)}, u32[]{:S(2)}, u32[]{:S(2)}) collective-permute-start(f32[16,64,128]{2,1,0:T(8,128)S(1)} %constant_dynamic-update-slice_fusion.refs_8_), channel_id=1, source_target_pairs={{0,48},{1,13},{2,50},{3,15},{4,52},{5,1},{6,54},{7,3},{8,56},{9,5}... | collective-permute-start | bytes 1572872 | tf_op jit(solution)/shard_map/ppermute | solution.py:33
  36.4 12.6 %collective-permute-start.9 = (f32[16,64,128]{2,1,0:T(8,128)S(1)}, f32[16,64,128]{2,1,0:T(8,128)S(1)}, u32[]{:S(2)}, u32[]{:S(2)}) collective-permute-start(f32[16,64,128]{2,1,0:T(8,128)S(1)} %constant_dynamic-update-slice_fusion.refs_8_), channel_id=1, source_target_pairs={{0,16},{1,5},{2,18},{3,7},{4,20},{5,9},{6,22},{7,11},{8,24},{9,13}... | collective-permute-start | bytes 1572872 | tf_op jit(solution)/shard_map/ppermute | solution.py:33
  49.8 18.6 %collective-permute-start.12 = (f32[32,64,128]{2,1,0:T(8,128)S(1)}, f32[32,64,128]{2,1,0:T(8,128)S(1)}, u32[]{:S(2)}, u32[]{:S(2)}) collective-permute-start(f32[32,64,128]{2,1,0:T(8,128)S(1)} %get-tuple-element.125), channel_id=1, source_target_pairs={{0,4},{1,17},{2,6},{3,19},{4,8},{5,21},{6,10},{7,23},{8,12},{9,25}... | collective-permute-start | bytes 3145736 | tf_op jit(solution)/shard_map/ppermute | solution.py:33
  51.0 17.5 %collective-permute-start.13 = (f32[32,64,128]{2,1,0:T(8,128)S(1)}, f32[32,64,128]{2,1,0:T(8,128)S(1)}, u32[]{:S(2)}, u32[]{:S(2)}) collective-permute-start(f32[32,64,128]{2,1,0:T(8,128)S(1)} %get-tuple-element.126), channel_id=1, source_target_pairs={{0,8},{1,33},{2,10},{3,35},{4,12},{5,37},{6,14},{7,39},{8,0},{9,41... | collective-permute-start | bytes 3145736 | tf_op jit(solution)/shard_map/ppermute | solution.py:33
  52.4 26.0 %collective-permute-start.14 = (f32[32,64,128]{2,1,0:T(8,128)S(1)}, f32[32,64,128]{2,1,0:T(8,128)S(1)}, u32[]{:S(2)}, u32[]{:S(2)}) collective-permute-start(f32[32,64,128]{2,1,0:T(8,128)S(1)} %get-tuple-element.127), channel_id=1, source_target_pairs={{0,12},{1,49},{2,14},{3,51},{4,0},{5,53},{6,2},{7,55},{8,4},{9,57}... | collective-permute-start | bytes 3145736 | tf_op jit(solution)/shard_map/ppermute | solution.py:33
  82.4 8.4 %collective-permute-start.19 = (f32[64,256]{1,0:T(8,128)S(1)}, f32[64,256]{1,0:T(8,128)S(1)}, u32[]{:S(2)}, u32[]{:S(2)}) collective-permute-start(f32[64,256]{1,0:T(8,128)S(1)} %get-tuple-element.138), channel_id=1, source_target_pairs={{0,2},{1,3},{2,0},{3,1},{4,6},{5,7},{6,4},{7,5},{8,10},{9,11},{10,... | collective-permute-start | bytes 196616 | tf_op jit(solution)/shard_map/ppermute | solution.py:41
  97.1 9.8 %collective-permute-start.22 = (f32[128,256]{1,0:T(8,128)S(1)}, f32[128,256]{1,0:T(8,128)S(1)}, u32[]{:S(2)}, u32[]{:S(2)}) collective-permute-start(f32[128,256]{1,0:T(8,128)S(1)} %get-tuple-element.146), channel_id=1, source_target_pairs={{0,2},{1,3},{2,0},{3,1},{4,6},{5,7},{6,4},{7,5},{8,10},{9,11},{10,... | collective-permute-start | bytes 393224 | tf_op jit(solution)/shard_map/ppermute | solution.py:41
  100.1 10.0 %collective-permute-start.23 = (f32[128,256]{1,0:T(8,128)S(1)}, f32[128,256]{1,0:T(8,128)S(1)}, u32[]{:S(2)}, u32[]{:S(2)}) collective-permute-start(f32[128,256]{1,0:T(8,128)S(1)} %get-tuple-element.147), channel_id=1, source_target_pairs={{0,3},{1,2},{2,1},{3,0},{4,7},{5,6},{6,5},{7,4},{8,11},{9,10},{10,... | collective-permute-start | bytes 393224 | tf_op jit(solution)/shard_map/ppermute | solution.py:41
  113.3 18.5 %collective-permute-start.24 = (f32[34,64,128]{2,1,0:T(8,128)S(1)}, f32[34,64,128]{2,1,0:T(8,128)S(1)}, u32[]{:S(2)}, u32[]{:S(2)}) collective-permute-start(f32[34,64,128]{2,1,0:T(8,128)S(1)} %get-tuple-element.157), channel_id=1, source_target_pairs={{0,12},{1,49},{2,14},{3,51},{4,0},{5,53},{6,2},{7,55},{8,4},{9,57}... | collective-permute-start | bytes 3342344 | tf_op jit(solution)/shard_map/ppermute | solution.py:33
  117.5 26.9 %collective-permute-start.25 = (f32[34,64,128]{2,1,0:T(8,128)S(1)}, f32[34,64,128]{2,1,0:T(8,128)S(1)}, u32[]{:S(2)}, u32[]{:S(2)}) collective-permute-start(f32[34,64,128]{2,1,0:T(8,128)S(1)} %get-tuple-element.158), channel_id=1, source_target_pairs={{0,8},{1,33},{2,10},{3,35},{4,12},{5,37},{6,14},{7,39},{8,0},{9,41... | collective-permute-start | bytes 3342344 | tf_op jit(solution)/shard_map/ppermute | solution.py:33
  119.0 26.5 %collective-permute-start.26 = (f32[34,64,128]{2,1,0:T(8,128)S(1)}, f32[34,64,128]{2,1,0:T(8,128)S(1)}, u32[]{:S(2)}, u32[]{:S(2)}) collective-permute-start(f32[34,64,128]{2,1,0:T(8,128)S(1)} %get-tuple-element.159), channel_id=1, source_target_pairs={{0,4},{1,17},{2,6},{3,19},{4,8},{5,21},{6,10},{7,23},{8,12},{9,25}... | collective-permute-start | bytes 3342344 | tf_op jit(solution)/shard_map/ppermute | solution.py:33
  146.5 10.0 %collective-permute-start.30 = (f32[18,64,128]{2,1,0:T(8,128)S(1)}, f32[18,64,128]{2,1,0:T(8,128)S(1)}, u32[]{:S(2)}, u32[]{:S(2)}) collective-permute-start(f32[18,64,128]{2,1,0:T(8,128)S(1)} %get-tuple-element.173), channel_id=1, source_target_pairs={{0,48},{1,13},{2,50},{3,15},{4,52},{5,1},{6,54},{7,3},{8,56},{9,5}... | collective-permute-start | bytes 1769480 | tf_op jit(solution)/shard_map/ppermute | solution.py:33
  146.7 11.5 %collective-permute-start.31 = (f32[18,64,128]{2,1,0:T(8,128)S(1)}, f32[18,64,128]{2,1,0:T(8,128)S(1)}, u32[]{:S(2)}, u32[]{:S(2)}) collective-permute-start(f32[18,64,128]{2,1,0:T(8,128)S(1)} %get-tuple-element.174), channel_id=1, source_target_pairs={{0,32},{1,9},{2,34},{3,11},{4,36},{5,13},{6,38},{7,15},{8,40},{9,1... | collective-permute-start | bytes 1769480 | tf_op jit(solution)/shard_map/ppermute | solution.py:33
  149.0 15.4 %collective-permute-start.32 = (f32[18,64,128]{2,1,0:T(8,128)S(1)}, f32[18,64,128]{2,1,0:T(8,128)S(1)}, u32[]{:S(2)}, u32[]{:S(2)}) collective-permute-start(f32[18,64,128]{2,1,0:T(8,128)S(1)} %get-tuple-element.175), channel_id=1, source_target_pairs={{0,16},{1,5},{2,18},{3,7},{4,20},{5,9},{6,22},{7,11},{8,24},{9,13}... | collective-permute-start | bytes 1769480 | tf_op jit(solution)/shard_map/ppermute | solution.py:33
  164.4 13.5 %collective-permute-start.34 = (f32[16,64,128]{2,1,0:T(8,128)S(1)}, f32[16,64,128]{2,1,0:T(8,128)S(1)}, u32[]{:S(2)}, u32[]{:S(2)}) collective-permute-start(f32[16,64,128]{2,1,0:T(8,128)S(1)} %get-tuple-element.182), channel_id=1, source_target_pairs={{0,32},{1,9},{2,34},{3,11},{4,36},{5,13},{6,38},{7,15},{8,40},{9,1... | collective-permute-start | bytes 1572872 | tf_op jit(solution)/shard_map/ppermute | solution.py:33
  166.6 10.2 %collective-permute-start.33 = (f32[8,64,128]{2,1,0:T(8,128)S(1)}, f32[8,64,128]{2,1,0:T(8,128)S(1)}, u32[]{:S(2)}, u32[]{:S(2)}) collective-permute-start(f32[8,64,128]{2,1,0:T(8,128)S(1)} %get-tuple-element.181), channel_id=1, source_target_pairs={{0,48},{1,13},{2,50},{3,15},{4,52},{5,1},{6,54},{7,3},{8,56},{9,5}... | collective-permute-start | bytes 786440 | tf_op jit(solution)/shard_map/ppermute | solution.py:33
  167.9 10.0 %collective-permute-start.35 = (f32[8,64,128]{2,1,0:T(8,128)S(1)}, f32[8,64,128]{2,1,0:T(8,128)S(1)}, u32[]{:S(2)}, u32[]{:S(2)}) collective-permute-start(f32[8,64,128]{2,1,0:T(8,128)S(1)} %get-tuple-element.183), channel_id=1, source_target_pairs={{0,16},{1,5},{2,18},{3,7},{4,20},{5,9},{6,22},{7,11},{8,24},{9,13}... | collective-permute-start | bytes 786440 | tf_op jit(solution)/shard_map/ppermute | solution.py:33
  168.8 26.5 %collective-permute-start.37 = (f32[10,64,128]{2,1,0:T(8,128)S(1)}, f32[10,64,128]{2,1,0:T(8,128)S(1)}, u32[]{:S(2)}, u32[]{:S(2)}) collective-permute-start(f32[10,64,128]{2,1,0:T(8,128)S(1)} %get-tuple-element.195.refs_4_), channel_id=1, source_target_pairs={{0,128},{4,132},{8,136},{12,140},{16,144},{20,148},{24,152},{28,15... | collective-permute-start | bytes 983048 | tf_op jit(solution)/shard_map/ppermute | solution.py:37
  175.0 20.3 %collective-permute-start.38 = (f32[10,64,128]{2,1,0:T(8,128)S(1)}, f32[10,64,128]{2,1,0:T(8,128)S(1)}, u32[]{:S(2)}, u32[]{:S(2)}) collective-permute-start(f32[10,64,128]{2,1,0:T(8,128)S(1)} %get-tuple-element.196), channel_id=1, source_target_pairs={{0,192},{4,196},{8,200},{12,204},{16,208},{20,212},{24,216},{28,22... | collective-permute-start | bytes 983048 | tf_op jit(solution)/shard_map/ppermute | solution.py:37
  178.0 21.8 %collective-permute-start.36 = (f32[10,64,128]{2,1,0:T(8,128)S(1)}, f32[10,64,128]{2,1,0:T(8,128)S(1)}, u32[]{:S(2)}, u32[]{:S(2)}) collective-permute-start(f32[10,64,128]{2,1,0:T(8,128)S(1)} %join1.1), channel_id=1, source_target_pairs={{0,64},{4,68},{8,72},{12,76},{16,80},{20,84},{24,88},{28,92},{32,9... | collective-permute-start | bytes 983048 | tf_op jit(solution)/shard_map/ppermute | solution.py:37
  184.0 16.4 %collective-permute-start.39 = (f32[8,64,128]{2,1,0:T(8,128)S(1)}, f32[8,64,128]{2,1,0:T(8,128)S(1)}, u32[]{:S(2)}, u32[]{:S(2)}) collective-permute-start(f32[8,64,128]{2,1,0:T(8,128)S(1)} %get-tuple-element.198), channel_id=1, source_target_pairs={{0,48},{1,13},{2,50},{3,15},{4,52},{5,1},{6,54},{7,3},{8,56},{9,5}... | collective-permute-start | bytes 786440 | tf_op jit(solution)/shard_map/ppermute | solution.py:33
  184.9 15.6 %collective-permute-start.40 = (f32[8,64,128]{2,1,0:T(8,128)S(1)}, f32[8,64,128]{2,1,0:T(8,128)S(1)}, u32[]{:S(2)}, u32[]{:S(2)}) collective-permute-start(f32[8,64,128]{2,1,0:T(8,128)S(1)} %get-tuple-element.199), channel_id=1, source_target_pairs={{0,16},{1,5},{2,18},{3,7},{4,20},{5,9},{6,22},{7,11},{8,24},{9,13}... | collective-permute-start | bytes 786440 | tf_op jit(solution)/shard_map/ppermute | solution.py:33
  (20 other events, 218.7 us)

commit v5 on v4

--- a/solution.py
+++ b/solution.py
@@ -9,8 +9,8 @@
 
 SIDE = 4
 RB = 8
-GROUP = 32
-CUTS = 4
+GROUP = 64
+CUTS = 2
 PER = SIDE * SIDE * 2
 F32 = jnp.float32
 BF16 = jnp.bfloat16

time: 202 us -> 202 us (level)
  starting transfers between devices: 81 us -> 76.6 us
  waiting for transfers between devices: 94.9 us -> 98.5 us
    ppermute x23, waiting for transfers between devices: 50.2 us -> 54.1 us  [shift(): return lax.ppermute(value, ('row', 'col'), pairs)]
    ppermute x23, starting transfers between devices: 36.1 us -> 32.3 us  [shift(): return lax.ppermute(value, ('row', 'col'), pairs)]
where the time goes in v5:
time: 202 us; the launch traced here: 201 us
  waiting for transfers between devices  98.5 us (49%)
  starting transfers between devices  76.6 us (38%)
  Pallas kernels  14.2 us (7%)
  local copies, waits for them, and re-layouts  8.23 us (4%)
    ppermute x23, waiting for transfers between devices, shift(): return lax.ppermute(value, ('row', 'col'), pairs)  54.1 us
    ppermute x23, starting transfers between devices, shift(): return lax.ppermute(value, ('row', 'col'), pairs)  32.3 us
    ppermute x12, waiting for transfers between devices, swap_col(): return lax.ppermute(value, 'col', [(c, c ^ k) for c in range(4)])  26.3 us
    ppermute x12, starting transfers between devices, swap_col(): return lax.ppermute(value, 'col', [(c, c ^ k) for c in range(4)])  24.4 us
    ppermute x6, starting transfers between devices, swap_z(): lax.ppermute(value, 'row', [(r, r ^ k * SIDE * SIDE) for r in range(SIDE...  19.9 us
    ppermute x6, waiting for transfers between devices, swap_z(): lax.ppermute(value, 'row', [(r, r ^ k * SIDE * SIDE) for r in range(SIDE...  18.1 us
    unnamed x24, local copies, waits for them, and re-layouts  7 us
    pallas_call x1, Pallas kernels, on_device(): call(forward_kernel, 'forward', [struct(width, quarter)] * 4, [SMEM] * 3...  4.34 us
  transfers between devices with their start and end apart: 41, of which 21 were waited for; matrix products, arithmetic and copies ran while one was open for 0% of the time, Pallas kernels for 2%

profile of v5, /device:TPU:8, one launch (start us, length us, event | category | flops | bytes accessed | tf_op | source)
XLA Modules:
  0.0 201.1 jit_solution(1674202845174489353)
XLA Ops:
  7.3 2.7 %collective-permute-start.1 = (f32[8,64,128]{2,1,0:T(8,128)S(1)}, f32[8,64,128]{2,1,0:T(8,128)S(1)}, u32[]{:S(2)}, u32[]{:S(2)}) collective-permute-start(f32[8,64,128]{2,1,0:T(8,128)S(1)} %bitcast.47), channel_id=1, source_target_pairs={{0,32},{1,9},{2,34},{3,11},{4,36},{5,13},{6,38},{7,15},{8,40},{9,1... | collective-permute-start | bytes 786440 | tf_op jit(solution)/shard_map/ppermute | solution.py:33
  11.4 3.3 %collective-permute-start.7 = (f32[8,64,128]{2,1,0:T(8,128)S(1)}, f32[8,64,128]{2,1,0:T(8,128)S(1)}, u32[]{:S(2)}, u32[]{:S(2)}) collective-permute-start(f32[8,64,128]{2,1,0:T(8,128)S(1)} %bitcast.49), channel_id=1, source_target_pairs={{0,128},{4,132},{8,136},{12,140},{16,144},{20,148},{24,152},{28,15... | collective-permute-start | bytes 786440 | tf_op jit(solution)/shard_map/ppermute | solution.py:37
  16.4 2.7 %collective-permute-start.5 = (f32[8,64,128]{2,1,0:T(8,128)S(1)}, f32[8,64,128]{2,1,0:T(8,128)S(1)}, u32[]{:S(2)}, u32[]{:S(2)}) collective-permute-start(f32[8,64,128]{2,1,0:T(8,128)S(1)} %collective-permute-done.3.refs_4_), channel_id=1, source_target_pairs={{0,32},{1,9},{2,34},{3,11},{4,36},{5,13},{6,38},{7,15},{8,40},{9,1... | collective-permute-start | bytes 786440 | tf_op jit(solution)/shard_map/ppermute | solution.py:33
  20.5 3.4 %copy-done.2 = s32[128,128,128]{2,1,0:T(8,128)S(1)} copy-done((s32[128,128,128]{2,1,0:T(8,128)S(1)}, s32[128,128,128]{2,1,0:T(8,128)}, u32[]{:S(2)}) %copy-start.2) | copy-done | bytes 8388632
  27.7 4.8 %collective-permute-done.7 = f32[8,64,128]{2,1,0:T(8,128)S(1)} collective-permute-done((f32[8,64,128]{2,1,0:T(8,128)S(1)}, f32[8,64,128]{2,1,0:T(8,128)S(1)}, u32[]{:S(2)}, u32[]{:S(2)}) %collective-permute-start.7) | collective-permute-done | bytes 262176 | tf_op jit(solution)/shard_map/ppermute | solution.py:37
  33.8 2.6 %collective-permute-start.11 = (f32[16,64,128]{2,1,0:T(8,128)S(1)}, f32[16,64,128]{2,1,0:T(8,128)S(1)}, u32[]{:S(2)}, u32[]{:S(2)}) collective-permute-start(f32[16,64,128]{2,1,0:T(8,128)S(1)} %constant_dynamic-update-slice_fusion.refs_8_), channel_id=1, source_target_pairs={{0,48},{1,13},{2,50},{3,15},{4,52},{5,1},{6,54},{7,3},{8,56},{9,5}... | collective-permute-start | bytes 1572872 | tf_op jit(solution)/shard_map/ppermute | solution.py:33
  36.4 7.1 %collective-permute-done.10.refs_10_ = f32[16,64,128]{2,1,0:T(8,128)S(1)} collective-permute-done((f32[16,64,128]{2,1,0:T(8,128)S(1)}, f32[16,64,128]{2,1,0:T(8,128)S(1)}, u32[]{:S(2)}, u32[]{:S(2)}) %collective-permute-start.10) | collective-permute-done | bytes 524320 | tf_op jit(solution)/shard_map/ppermute | solution.py:33
  43.5 3.4 %collective-permute-done.11.refs_11_ = f32[16,64,128]{2,1,0:T(8,128)S(1)} collective-permute-done((f32[16,64,128]{2,1,0:T(8,128)S(1)}, f32[16,64,128]{2,1,0:T(8,128)S(1)}, u32[]{:S(2)}, u32[]{:S(2)}) %collective-permute-start.11) | collective-permute-done | bytes 524320 | tf_op jit(solution)/shard_map/ppermute | solution.py:33
  54.6 5.7 %collective-permute-start.16 = (f32[64,256]{1,0:T(8,128)S(1)}, f32[64,256]{1,0:T(8,128)S(1)}, u32[]{:S(2)}, u32[]{:S(2)}) collective-permute-start(f32[64,256]{1,0:T(8,128)S(1)} %get-tuple-element.130), channel_id=1, source_target_pairs={{0,2},{1,3},{2,0},{3,1},{4,6},{5,7},{6,4},{7,5},{8,10},{9,11},{10,... | collective-permute-start | bytes 196616 | tf_op jit(solution)/shard_map/ppermute | solution.py:41
  63.0 5.4 %collective-permute-done.17.c3 = f32[64,256]{1,0:T(8,128)S(1)} collective-permute-done((f32[64,256]{1,0:T(8,128)S(1)}, f32[64,256]{1,0:T(8,128)S(1)}, u32[]{:S(2)}, u32[]{:S(2)}) %collective-permute-start.17) | collective-permute-done | bytes 65568 | tf_op jit(solution)/shard_map/ppermute | solution.py:41
  68.4 10.0 %collective-permute-done.14.q3 = f32[32,64,128]{2,1,0:T(8,128)S(1)} collective-permute-done((f32[32,64,128]{2,1,0:T(8,128)S(1)}, f32[32,64,128]{2,1,0:T(8,128)S(1)}, u32[]{:S(2)}, u32[]{:S(2)}) %collective-permute-start.14) | collective-permute-done | bytes 1048608 | tf_op jit(solution)/shard_map/ppermute | solution.py:33
  78.5 4.3 %forward.1 = (f32[64,256]{1,0:T(8,128)S(1)}, f32[64,256]{1,0:T(8,128)S(1)}, f32[64,256]{1,0:T(8,128)S(1)}, f32[64,256]{1,0:T(8,128)S(1)}) custom-call(s32[128]{0:T(128)S(1)} %compare_select_fusion.12.rows, s32[128]{0:T(128)S(1)} %get-tuple-element.202.at, s32[2]{0:T(128)S(1)} %pad_add_fusion.info, f32[64,1024]{1,0:T(8,128)S(1)} %get-tuple-element.204.scaled, ...), custom_call_target="tpu_custom_call" | custom-call | bytes 16777216 | tf_op jit(solution)/shard_map/forward/pallas_call | solution.py:402
  82.9 5.3 %collective-permute-start.19 = (f32[64,256]{1,0:T(8,128)S(1)}, f32[64,256]{1,0:T(8,128)S(1)}, u32[]{:S(2)}, u32[]{:S(2)}) collective-permute-start(f32[64,256]{1,0:T(8,128)S(1)} %get-tuple-element.138), channel_id=1, source_target_pairs={{0,2},{1,3},{2,0},{3,1},{4,6},{5,7},{6,4},{7,5},{8,10},{9,11},{10,... | collective-permute-start | bytes 196616 | tf_op jit(solution)/shard_map/ppermute | solution.py:41
  88.7 2.6 %collective-permute-done.19.a2 = f32[64,256]{1,0:T(8,128)S(1)} collective-permute-done((f32[64,256]{1,0:T(8,128)S(1)}, f32[64,256]{1,0:T(8,128)S(1)}, u32[]{:S(2)}, u32[]{:S(2)}) %collective-permute-start.19) | collective-permute-done | bytes 65568 | tf_op jit(solution)/shard_map/ppermute | solution.py:41
  91.3 4.8 %collective-permute-done.20.a3 = f32[64,256]{1,0:T(8,128)S(1)} collective-permute-done((f32[64,256]{1,0:T(8,128)S(1)}, f32[64,256]{1,0:T(8,128)S(1)}, u32[]{:S(2)}, u32[]{:S(2)}) %collective-permute-start.20) | collective-permute-done | bytes 65568 | tf_op jit(solution)/shard_map/ppermute | solution.py:41
  97.7 2.9 %collective-permute-start.22 = (f32[128,256]{1,0:T(8,128)S(1)}, f32[128,256]{1,0:T(8,128)S(1)}, u32[]{:S(2)}, u32[]{:S(2)}) collective-permute-start(f32[128,256]{1,0:T(8,128)S(1)} %get-tuple-element.146), channel_id=1, source_target_pairs={{0,2},{1,3},{2,0},{3,1},{4,6},{5,7},{6,4},{7,5},{8,10},{9,11},{10,... | collective-permute-start | bytes 393224 | tf_op jit(solution)/shard_map/ppermute | solution.py:41
  100.6 2.7 %collective-permute-start.23 = (f32[128,256]{1,0:T(8,128)S(1)}, f32[128,256]{1,0:T(8,128)S(1)}, u32[]{:S(2)}, u32[]{:S(2)}) collective-permute-start(f32[128,256]{1,0:T(8,128)S(1)} %get-tuple-element.147), channel_id=1, source_target_pairs={{0,3},{1,2},{2,1},{3,0},{4,7},{5,6},{6,5},{7,4},{8,11},{9,10},{10,... | collective-permute-start | bytes 393224 | tf_op jit(solution)/shard_map/ppermute | solution.py:41
  103.3 4.1 %collective-permute-done.22.i2 = f32[128,256]{1,0:T(8,128)S(1)} collective-permute-done((f32[128,256]{1,0:T(8,128)S(1)}, f32[128,256]{1,0:T(8,128)S(1)}, u32[]{:S(2)}, u32[]{:S(2)}) %collective-permute-start.22) | collective-permute-done | bytes 131104 | tf_op jit(solution)/shard_map/ppermute | solution.py:41
  107.4 3.1 %collective-permute-done.23.i3 = f32[128,256]{1,0:T(8,128)S(1)} collective-permute-done((f32[128,256]{1,0:T(8,128)S(1)}, f32[128,256]{1,0:T(8,128)S(1)}, u32[]{:S(2)}, u32[]{:S(2)}) %collective-permute-start.23) | collective-permute-done | bytes 131104 | tf_op jit(solution)/shard_map/ppermute | solution.py:41
  110.6 3.4 %backward.1 = (f32[64,1024]{1,0:T(8,128)S(1)}, f32[34,64,128]{2,1,0:T(8,128)S(1)}, f32[34,64,128]{2,1,0:T(8,128)S(1)}, f32[34,64,128]{2,1,0:T(8,128)S(1)}, f32[34,64,128]{2,1,0:T(8,128)S(1)}) custom-call(s32[128]{0:T(128)S(1)} %copy-done.4, s32[128]{0:T(128)S(1)} %get-tuple-element.201.at, s32[2]{0:T(128)S(1)} %pad_add_fusion.info, f32[1,1024]{1,0:T(1,128)S(1)} %bitcast.53, ...), custom_call_target="tpu_custom_call" | custom-call | bytes 16777216 | tf_op jit(solution)/shard_map/backward/pallas_call | solution.py:428
  115.7 2.7 %collective-permute-start.25 = (f32[34,64,128]{2,1,0:T(8,128)S(1)}, f32[34,64,128]{2,1,0:T(8,128)S(1)}, u32[]{:S(2)}, u32[]{:S(2)}) collective-permute-start(f32[34,64,128]{2,1,0:T(8,128)S(1)} %get-tuple-element.158), channel_id=1, source_target_pairs={{0,8},{1,33},{2,10},{3,35},{4,12},{5,37},{6,14},{7,39},{8,0},{9,41... | collective-permute-start | bytes 3342344 | tf_op jit(solution)/shard_map/ppermute | solution.py:33
  118.4 2.5 %collective-permute-start.26 = (f32[34,64,128]{2,1,0:T(8,128)S(1)}, f32[34,64,128]{2,1,0:T(8,128)S(1)}, u32[]{:S(2)}, u32[]{:S(2)}) collective-permute-start(f32[34,64,128]{2,1,0:T(8,128)S(1)} %get-tuple-element.159), channel_id=1, source_target_pairs={{0,4},{1,17},{2,6},{3,19},{4,8},{5,21},{6,10},{7,23},{8,12},{9,25}... | collective-permute-start | bytes 3342344 | tf_op jit(solution)/shard_map/ppermute | solution.py:33
  120.9 2.2 %collective-permute-start.28 = (f32[64,256]{1,0:T(8,128)S(1)}, f32[64,256]{1,0:T(8,128)S(1)}, u32[]{:S(2)}, u32[]{:S(2)}) collective-permute-start(f32[64,256]{1,0:T(8,128)S(1)} %get-tuple-element.162), channel_id=1, source_target_pairs={{0,2},{1,3},{2,0},{3,1},{4,6},{5,7},{6,4},{7,5},{8,10},{9,11},{10,... | collective-permute-start | bytes 196616 | tf_op jit(solution)/shard_map/ppermute | solution.py:41
  123.2 3.5 %collective-permute-start.29 = (f32[64,256]{1,0:T(8,128)S(1)}, f32[64,256]{1,0:T(8,128)S(1)}, u32[]{:S(2)}, u32[]{:S(2)}) collective-permute-start(f32[64,256]{1,0:T(8,128)S(1)} %get-tuple-element.163), channel_id=1, source_target_pairs={{0,3},{1,2},{2,1},{3,0},{4,7},{5,6},{6,5},{7,4},{8,11},{9,10},{10,... | collective-permute-start | bytes 196616 | tf_op jit(solution)/shard_map/ppermute | solution.py:41
  126.7 2.6 %collective-permute-done.28 = f32[64,256]{1,0:T(8,128)S(1)} collective-permute-done((f32[64,256]{1,0:T(8,128)S(1)}, f32[64,256]{1,0:T(8,128)S(1)}, u32[]{:S(2)}, u32[]{:S(2)}) %collective-permute-start.28) | collective-permute-done | bytes 65568 | tf_op jit(solution)/shard_map/ppermute | solution.py:41
  131.1 12.6 %collective-permute-done.25.refs_2_ = f32[34,64,128]{2,1,0:T(8,128)S(1)} collective-permute-done((f32[34,64,128]{2,1,0:T(8,128)S(1)}, f32[34,64,128]{2,1,0:T(8,128)S(1)}, u32[]{:S(2)}, u32[]{:S(2)}) %collective-permute-start.25) | collective-permute-done | bytes 1114144 | tf_op jit(solution)/shard_map/ppermute | solution.py:33
  150.6 11.2 %collective-permute-done.30.refs_1_ = f32[18,64,128]{2,1,0:T(8,128)S(1)} collective-permute-done((f32[18,64,128]{2,1,0:T(8,128)S(1)}, f32[18,64,128]{2,1,0:T(8,128)S(1)}, u32[]{:S(2)}, u32[]{:S(2)}) %collective-permute-start.30) | collective-permute-done | bytes 589856 | tf_op jit(solution)/shard_map/ppermute | solution.py:33
  161.8 3.9 %collective-permute-done.32.refs_3_ = f32[18,64,128]{2,1,0:T(8,128)S(1)} collective-permute-done((f32[18,64,128]{2,1,0:T(8,128)S(1)}, f32[18,64,128]{2,1,0:T(8,128)S(1)}, u32[]{:S(2)}, u32[]{:S(2)}) %collective-permute-start.32) | collective-permute-done | bytes 589856 | tf_op jit(solution)/shard_map/ppermute | solution.py:33
  168.2 6.4 %collective-permute-start.37 = (f32[10,64,128]{2,1,0:T(8,128)S(1)}, f32[10,64,128]{2,1,0:T(8,128)S(1)}, u32[]{:S(2)}, u32[]{:S(2)}) collective-permute-start(f32[10,64,128]{2,1,0:T(8,128)S(1)} %get-tuple-element.195.refs_4_), channel_id=1, source_target_pairs={{0,128},{4,132},{8,136},{12,140},{16,144},{20,148},{24,152},{28,15... | collective-permute-start | bytes 983048 | tf_op jit(solution)/shard_map/ppermute | solution.py:37
  179.2 5.0 %collective-permute-start.36 = (f32[10,64,128]{2,1,0:T(8,128)S(1)}, f32[10,64,128]{2,1,0:T(8,128)S(1)}, u32[]{:S(2)}, u32[]{:S(2)}) collective-permute-start(f32[10,64,128]{2,1,0:T(8,128)S(1)} %join1.1), channel_id=1, source_target_pairs={{0,64},{4,68},{8,72},{12,76},{16,80},{20,84},{24,88},{28,92},{32,9... | collective-permute-start | bytes 983048 | tf_op jit(solution)/shard_map/ppermute | solution.py:37
  186.4 9.5 %collective-permute-done.37 = f32[10,64,128]{2,1,0:T(8,128)S(1)} collective-permute-done((f32[10,64,128]{2,1,0:T(8,128)S(1)}, f32[10,64,128]{2,1,0:T(8,128)S(1)}, u32[]{:S(2)}, u32[]{:S(2)}) %collective-permute-start.37) | collective-permute-done | bytes 327712 | tf_op jit(solution)/shard_map/ppermute | solution.py:37
  195.9 3.8 %collective-permute-done.36 = f32[10,64,128]{2,1,0:T(8,128)S(1)} collective-permute-done((f32[10,64,128]{2,1,0:T(8,128)S(1)}, f32[10,64,128]{2,1,0:T(8,128)S(1)}, u32[]{:S(2)}, u32[]{:S(2)}) %collective-permute-start.36) | collective-permute-done | bytes 327712 | tf_op jit(solution)/shard_map/ppermute | solution.py:37
  (106 shorter events, 48.9 us)
Async XLA Ops:
  3.8 10.9 %collective-permute-start = (f32[8,64,128]{2,1,0:T(8,128)S(1)}, f32[8,64,128]{2,1,0:T(8,128)S(1)}, u32[]{:S(2)}, u32[]{:S(2)}) collective-permute-start(f32[8,64,128]{2,1,0:T(8,128)S(1)} %bitcast.45), channel_id=1, source_target_pairs={{0,16},{1,5},{2,18},{3,7},{4,20},{5,9},{6,22},{7,11},{8,24},{9,13}... | collective-permute-start | bytes 786440 | tf_op jit(solution)/shard_map/ppermute | solution.py:33
  5.4 10.7 %collective-permute-start.3 = (f32[8,64,128]{2,1,0:T(8,128)S(1)}, f32[8,64,128]{2,1,0:T(8,128)S(1)}, u32[]{:S(2)}, u32[]{:S(2)}) collective-permute-start(f32[8,64,128]{2,1,0:T(8,128)S(1)} %bitcast.46), channel_id=1, source_target_pairs={{0,64},{4,68},{8,72},{12,76},{16,80},{20,84},{24,88},{28,92},{32,9... | collective-permute-start | bytes 786440 | tf_op jit(solution)/shard_map/ppermute | solution.py:37
  7.3 9.1 %collective-permute-start.1 = (f32[8,64,128]{2,1,0:T(8,128)S(1)}, f32[8,64,128]{2,1,0:T(8,128)S(1)}, u32[]{:S(2)}, u32[]{:S(2)}) collective-permute-start(f32[8,64,128]{2,1,0:T(8,128)S(1)} %bitcast.47), channel_id=1, source_target_pairs={{0,32},{1,9},{2,34},{3,11},{4,36},{5,13},{6,38},{7,15},{8,40},{9,1... | collective-permute-start | bytes 786440 | tf_op jit(solution)/shard_map/ppermute | solution.py:33
  10.0 9.1 %collective-permute-start.2 = (f32[8,64,128]{2,1,0:T(8,128)S(1)}, f32[8,64,128]{2,1,0:T(8,128)S(1)}, u32[]{:S(2)}, u32[]{:S(2)}) collective-permute-start(f32[8,64,128]{2,1,0:T(8,128)S(1)} %bitcast.48), channel_id=1, source_target_pairs={{0,48},{1,13},{2,50},{3,15},{4,52},{5,1},{6,54},{7,3},{8,56},{9,5}... | collective-permute-start | bytes 786440 | tf_op jit(solution)/shard_map/ppermute | solution.py:33
  11.4 21.1 %collective-permute-start.7 = (f32[8,64,128]{2,1,0:T(8,128)S(1)}, f32[8,64,128]{2,1,0:T(8,128)S(1)}, u32[]{:S(2)}, u32[]{:S(2)}) collective-permute-start(f32[8,64,128]{2,1,0:T(8,128)S(1)} %bitcast.49), channel_id=1, source_target_pairs={{0,128},{4,132},{8,136},{12,140},{16,144},{20,148},{24,152},{28,15... | collective-permute-start | bytes 786440 | tf_op jit(solution)/shard_map/ppermute | solution.py:37
  14.7 17.8 %collective-permute-start.8 = (f32[8,64,128]{2,1,0:T(8,128)S(1)}, f32[8,64,128]{2,1,0:T(8,128)S(1)}, u32[]{:S(2)}, u32[]{:S(2)}) collective-permute-start(f32[8,64,128]{2,1,0:T(8,128)S(1)} %bitcast.50), channel_id=1, source_target_pairs={{0,192},{4,196},{8,200},{12,204},{16,208},{20,212},{24,216},{28,22... | collective-permute-start | bytes 786440 | tf_op jit(solution)/shard_map/ppermute | solution.py:37
  16.1 16.4 %collective-permute-start.4 = (f32[8,64,128]{2,1,0:T(8,128)S(1)}, f32[8,64,128]{2,1,0:T(8,128)S(1)}, u32[]{:S(2)}, u32[]{:S(2)}) collective-permute-start(f32[8,64,128]{2,1,0:T(8,128)S(1)} %collective-permute-done.3.refs_4_), channel_id=1, source_target_pairs={{0,16},{1,5},{2,18},{3,7},{4,20},{5,9},{6,22},{7,11},{8,24},{9,13}... | collective-permute-start | bytes 786440 | tf_op jit(solution)/shard_map/ppermute | solution.py:33
  16.4 16.1 %collective-permute-start.5 = (f32[8,64,128]{2,1,0:T(8,128)S(1)}, f32[8,64,128]{2,1,0:T(8,128)S(1)}, u32[]{:S(2)}, u32[]{:S(2)}) collective-permute-start(f32[8,64,128]{2,1,0:T(8,128)S(1)} %collective-permute-done.3.refs_4_), channel_id=1, source_target_pairs={{0,32},{1,9},{2,34},{3,11},{4,36},{5,13},{6,38},{7,15},{8,40},{9,1... | collective-permute-start | bytes 786440 | tf_op jit(solution)/shard_map/ppermute | solution.py:33
  19.1 13.4 %collective-permute-start.6 = (f32[8,64,128]{2,1,0:T(8,128)S(1)}, f32[8,64,128]{2,1,0:T(8,128)S(1)}, u32[]{:S(2)}, u32[]{:S(2)}) collective-permute-start(f32[8,64,128]{2,1,0:T(8,128)S(1)} %collective-permute-done.3.refs_4_), channel_id=1, source_target_pairs={{0,48},{1,13},{2,50},{3,15},{4,52},{5,1},{6,54},{7,3},{8,56},{9,5}... | collective-permute-start | bytes 786440 | tf_op jit(solution)/shard_map/ppermute | solution.py:33
  32.6 10.9 %collective-permute-start.10 = (f32[16,64,128]{2,1,0:T(8,128)S(1)}, f32[16,64,128]{2,1,0:T(8,128)S(1)}, u32[]{:S(2)}, u32[]{:S(2)}) collective-permute-start(f32[16,64,128]{2,1,0:T(8,128)S(1)} %constant_dynamic-update-slice_fusion.refs_8_), channel_id=1, source_target_pairs={{0,32},{1,9},{2,34},{3,11},{4,36},{5,13},{6,38},{7,15},{8,40},{9,1... | collective-permute-start | bytes 1572872 | tf_op jit(solution)/shard_map/ppermute | solution.py:33
  33.8 13.1 %collective-permute-start.11 = (f32[16,64,128]{2,1,0:T(8,128)S(1)}, f32[16,64,128]{2,1,0:T(8,128)S(1)}, u32[]{:S(2)}, u32[]{:S(2)}) collective-permute-start(f32[16,64,128]{2,1,0:T(8,128)S(1)} %constant_dynamic-update-slice_fusion.refs_8_), channel_id=1, source_target_pairs={{0,48},{1,13},{2,50},{3,15},{4,52},{5,1},{6,54},{7,3},{8,56},{9,5}... | collective-permute-start | bytes 1572872 | tf_op jit(solution)/shard_map/ppermute | solution.py:33
  36.4 12.6 %collective-permute-start.9 = (f32[16,64,128]{2,1,0:T(8,128)S(1)}, f32[16,64,128]{2,1,0:T(8,128)S(1)}, u32[]{:S(2)}, u32[]{:S(2)}) collective-permute-start(f32[16,64,128]{2,1,0:T(8,128)S(1)} %constant_dynamic-update-slice_fusion.refs_8_), channel_id=1, source_target_pairs={{0,16},{1,5},{2,18},{3,7},{4,20},{5,9},{6,22},{7,11},{8,24},{9,13}... | collective-permute-start | bytes 1572872 | tf_op jit(solution)/shard_map/ppermute | solution.py:33
  49.8 18.6 %collective-permute-start.12 = (f32[32,64,128]{2,1,0:T(8,128)S(1)}, f32[32,64,128]{2,1,0:T(8,128)S(1)}, u32[]{:S(2)}, u32[]{:S(2)}) collective-permute-start(f32[32,64,128]{2,1,0:T(8,128)S(1)} %get-tuple-element.125), channel_id=1, source_target_pairs={{0,4},{1,17},{2,6},{3,19},{4,8},{5,21},{6,10},{7,23},{8,12},{9,25}... | collective-permute-start | bytes 3145736 | tf_op jit(solution)/shard_map/ppermute | solution.py:33
  51.0 17.5 %collective-permute-start.13 = (f32[32,64,128]{2,1,0:T(8,128)S(1)}, f32[32,64,128]{2,1,0:T(8,128)S(1)}, u32[]{:S(2)}, u32[]{:S(2)}) collective-permute-start(f32[32,64,128]{2,1,0:T(8,128)S(1)} %get-tuple-element.126), channel_id=1, source_target_pairs={{0,8},{1,33},{2,10},{3,35},{4,12},{5,37},{6,14},{7,39},{8,0},{9,41... | collective-permute-start | bytes 3145736 | tf_op jit(solution)/shard_map/ppermute | solution.py:33
  52.4 26.0 %collective-permute-start.14 = (f32[32,64,128]{2,1,0:T(8,128)S(1)}, f32[32,64,128]{2,1,0:T(8,128)S(1)}, u32[]{:S(2)}, u32[]{:S(2)}) collective-permute-start(f32[32,64,128]{2,1,0:T(8,128)S(1)} %get-tuple-element.127), channel_id=1, source_target_pairs={{0,12},{1,49},{2,14},{3,51},{4,0},{5,53},{6,2},{7,55},{8,4},{9,57}... | collective-permute-start | bytes 3145736 | tf_op jit(solution)/shard_map/ppermute | solution.py:33
  82.9 8.4 %collective-permute-start.19 = (f32[64,256]{1,0:T(8,128)S(1)}, f32[64,256]{1,0:T(8,128)S(1)}, u32[]{:S(2)}, u32[]{:S(2)}) collective-permute-start(f32[64,256]{1,0:T(8,128)S(1)} %get-tuple-element.138), channel_id=1, source_target_pairs={{0,2},{1,3},{2,0},{3,1},{4,6},{5,7},{6,4},{7,5},{8,10},{9,11},{10,... | collective-permute-start | bytes 196616 | tf_op jit(solution)/shard_map/ppermute | solution.py:41
  97.7 9.8 %collective-permute-start.22 = (f32[128,256]{1,0:T(8,128)S(1)}, f32[128,256]{1,0:T(8,128)S(1)}, u32[]{:S(2)}, u32[]{:S(2)}) collective-permute-start(f32[128,256]{1,0:T(8,128)S(1)} %get-tuple-element.146), channel_id=1, source_target_pairs={{0,2},{1,3},{2,0},{3,1},{4,6},{5,7},{6,4},{7,5},{8,10},{9,11},{10,... | collective-permute-start | bytes 393224 | tf_op jit(solution)/shard_map/ppermute | solution.py:41
  100.6 10.0 %collective-permute-start.23 = (f32[128,256]{1,0:T(8,128)S(1)}, f32[128,256]{1,0:T(8,128)S(1)}, u32[]{:S(2)}, u32[]{:S(2)}) collective-permute-start(f32[128,256]{1,0:T(8,128)S(1)} %get-tuple-element.147), channel_id=1, source_target_pairs={{0,3},{1,2},{2,1},{3,0},{4,7},{5,6},{6,5},{7,4},{8,11},{9,10},{10,... | collective-permute-start | bytes 393224 | tf_op jit(solution)/shard_map/ppermute | solution.py:41
  113.9 17.2 %collective-permute-start.24 = (f32[34,64,128]{2,1,0:T(8,128)S(1)}, f32[34,64,128]{2,1,0:T(8,128)S(1)}, u32[]{:S(2)}, u32[]{:S(2)}) collective-permute-start(f32[34,64,128]{2,1,0:T(8,128)S(1)} %get-tuple-element.157), channel_id=1, source_target_pairs={{0,12},{1,49},{2,14},{3,51},{4,0},{5,53},{6,2},{7,55},{8,4},{9,57}... | collective-permute-start | bytes 3342344 | tf_op jit(solution)/shard_map/ppermute | solution.py:33
  115.7 28.0 %collective-permute-start.25 = (f32[34,64,128]{2,1,0:T(8,128)S(1)}, f32[34,64,128]{2,1,0:T(8,128)S(1)}, u32[]{:S(2)}, u32[]{:S(2)}) collective-permute-start(f32[34,64,128]{2,1,0:T(8,128)S(1)} %get-tuple-element.158), channel_id=1, source_target_pairs={{0,8},{1,33},{2,10},{3,35},{4,12},{5,37},{6,14},{7,39},{8,0},{9,41... | collective-permute-start | bytes 3342344 | tf_op jit(solution)/shard_map/ppermute | solution.py:33
  118.4 26.5 %collective-permute-start.26 = (f32[34,64,128]{2,1,0:T(8,128)S(1)}, f32[34,64,128]{2,1,0:T(8,128)S(1)}, u32[]{:S(2)}, u32[]{:S(2)}) collective-permute-start(f32[34,64,128]{2,1,0:T(8,128)S(1)} %get-tuple-element.159), channel_id=1, source_target_pairs={{0,4},{1,17},{2,6},{3,19},{4,8},{5,21},{6,10},{7,23},{8,12},{9,25}... | collective-permute-start | bytes 3342344 | tf_op jit(solution)/shard_map/ppermute | solution.py:33
  145.8 16.0 %collective-permute-start.30 = (f32[18,64,128]{2,1,0:T(8,128)S(1)}, f32[18,64,128]{2,1,0:T(8,128)S(1)}, u32[]{:S(2)}, u32[]{:S(2)}) collective-permute-start(f32[18,64,128]{2,1,0:T(8,128)S(1)} %get-tuple-element.173), channel_id=1, source_target_pairs={{0,48},{1,13},{2,50},{3,15},{4,52},{5,1},{6,54},{7,3},{8,56},{9,5}... | collective-permute-start | bytes 1769480 | tf_op jit(solution)/shard_map/ppermute | solution.py:33
  148.0 13.8 %collective-permute-start.31 = (f32[18,64,128]{2,1,0:T(8,128)S(1)}, f32[18,64,128]{2,1,0:T(8,128)S(1)}, u32[]{:S(2)}, u32[]{:S(2)}) collective-permute-start(f32[18,64,128]{2,1,0:T(8,128)S(1)} %get-tuple-element.174), channel_id=1, source_target_pairs={{0,32},{1,9},{2,34},{3,11},{4,36},{5,13},{6,38},{7,15},{8,40},{9,1... | collective-permute-start | bytes 1769480 | tf_op jit(solution)/shard_map/ppermute | solution.py:33
  148.3 17.4 %collective-permute-start.32 = (f32[18,64,128]{2,1,0:T(8,128)S(1)}, f32[18,64,128]{2,1,0:T(8,128)S(1)}, u32[]{:S(2)}, u32[]{:S(2)}) collective-permute-start(f32[18,64,128]{2,1,0:T(8,128)S(1)} %get-tuple-element.175), channel_id=1, source_target_pairs={{0,16},{1,5},{2,18},{3,7},{4,20},{5,9},{6,22},{7,11},{8,24},{9,13}... | collective-permute-start | bytes 1769480 | tf_op jit(solution)/shard_map/ppermute | solution.py:33
  165.7 13.5 %collective-permute-start.34 = (f32[16,64,128]{2,1,0:T(8,128)S(1)}, f32[16,64,128]{2,1,0:T(8,128)S(1)}, u32[]{:S(2)}, u32[]{:S(2)}) collective-permute-start(f32[16,64,128]{2,1,0:T(8,128)S(1)} %get-tuple-element.182), channel_id=1, source_target_pairs={{0,32},{1,9},{2,34},{3,11},{4,36},{5,13},{6,38},{7,15},{8,40},{9,1... | collective-permute-start | bytes 1572872 | tf_op jit(solution)/shard_map/ppermute | solution.py:33
  166.0 11.3 %collective-permute-start.33 = (f32[8,64,128]{2,1,0:T(8,128)S(1)}, f32[8,64,128]{2,1,0:T(8,128)S(1)}, u32[]{:S(2)}, u32[]{:S(2)}) collective-permute-start(f32[8,64,128]{2,1,0:T(8,128)S(1)} %get-tuple-element.181), channel_id=1, source_target_pairs={{0,48},{1,13},{2,50},{3,15},{4,52},{5,1},{6,54},{7,3},{8,56},{9,5}... | collective-permute-start | bytes 786440 | tf_op jit(solution)/shard_map/ppermute | solution.py:33
  167.2 12.0 %collective-permute-start.35 = (f32[8,64,128]{2,1,0:T(8,128)S(1)}, f32[8,64,128]{2,1,0:T(8,128)S(1)}, u32[]{:S(2)}, u32[]{:S(2)}) collective-permute-start(f32[8,64,128]{2,1,0:T(8,128)S(1)} %get-tuple-element.183), channel_id=1, source_target_pairs={{0,16},{1,5},{2,18},{3,7},{4,20},{5,9},{6,22},{7,11},{8,24},{9,13}... | collective-permute-start | bytes 786440 | tf_op jit(solution)/shard_map/ppermute | solution.py:33
  168.2 27.7 %collective-permute-start.37 = (f32[10,64,128]{2,1,0:T(8,128)S(1)}, f32[10,64,128]{2,1,0:T(8,128)S(1)}, u32[]{:S(2)}, u32[]{:S(2)}) collective-permute-start(f32[10,64,128]{2,1,0:T(8,128)S(1)} %get-tuple-element.195.refs_4_), channel_id=1, source_target_pairs={{0,128},{4,132},{8,136},{12,140},{16,144},{20,148},{24,152},{28,15... | collective-permute-start | bytes 983048 | tf_op jit(solution)/shard_map/ppermute | solution.py:37
  174.6 21.2 %collective-permute-start.38 = (f32[10,64,128]{2,1,0:T(8,128)S(1)}, f32[10,64,128]{2,1,0:T(8,128)S(1)}, u32[]{:S(2)}, u32[]{:S(2)}) collective-permute-start(f32[10,64,128]{2,1,0:T(8,128)S(1)} %get-tuple-element.196), channel_id=1, source_target_pairs={{0,192},{4,196},{8,200},{12,204},{16,208},{20,212},{24,216},{28,22... | collective-permute-start | bytes 983048 | tf_op jit(solution)/shard_map/ppermute | solution.py:37
  179.2 20.4 %collective-permute-start.36 = (f32[10,64,128]{2,1,0:T(8,128)S(1)}, f32[10,64,128]{2,1,0:T(8,128)S(1)}, u32[]{:S(2)}, u32[]{:S(2)}) collective-permute-start(f32[10,64,128]{2,1,0:T(8,128)S(1)} %join1.1), channel_id=1, source_target_pairs={{0,64},{4,68},{8,72},{12,76},{16,80},{20,84},{24,88},{28,92},{32,9... | collective-permute-start | bytes 983048 | tf_op jit(solution)/shard_map/ppermute | solution.py:37
  184.3 16.0 %collective-permute-start.39 = (f32[8,64,128]{2,1,0:T(8,128)S(1)}, f32[8,64,128]{2,1,0:T(8,128)S(1)}, u32[]{:S(2)}, u32[]{:S(2)}) collective-permute-start(f32[8,64,128]{2,1,0:T(8,128)S(1)} %get-tuple-element.198), channel_id=1, source_target_pairs={{0,48},{1,13},{2,50},{3,15},{4,52},{5,1},{6,54},{7,3},{8,56},{9,5}... | collective-permute-start | bytes 786440 | tf_op jit(solution)/shard_map/ppermute | solution.py:33
  184.9 15.4 %collective-permute-start.40 = (f32[8,64,128]{2,1,0:T(8,128)S(1)}, f32[8,64,128]{2,1,0:T(8,128)S(1)}, u32[]{:S(2)}, u32[]{:S(2)}) collective-permute-start(f32[8,64,128]{2,1,0:T(8,128)S(1)} %get-tuple-element.199), channel_id=1, source_target_pairs={{0,16},{1,5},{2,18},{3,7},{4,20},{5,9},{6,22},{7,11},{8,24},{9,13}... | collective-permute-start | bytes 786440 | tf_op jit(solution)/shard_map/ppermute | solution.py:33
  (20 other events, 218.9 us)
